TPU v7x, 256 devices: a whole 4x4x8 slice. The times are simulated.
256 devices in a mesh: wide: 64 (over y, z_hi, x), narrow: 4 (over z_lo, core).
Axes of the slice: x: 4, y: 4, z: 8 (z_hi: 4, z_lo: 2; z = z_hi * 2 + z_lo), core: 2. Of those that a mesh axis runs over, the one named last changes fastest.
Arguments:
- charges: float32 [2, 64, 65536], P(None, None, ('wide', 'narrow')), may hold values from -6 to 6
- projection: float32 [64, 64], replicated, may hold values from -0.75 to 0.75
- green_hat: float32 [2, 256, 512, 512], P(None, ('wide', 'narrow')), may hold values from -6 to 6
- near_table: float32 [27, 2, 64, 64], replicated, may hold values from -0.109375 to 0.109375
- block_site: int32 [65536], P(('wide', 'narrow')), may hold values from 0 to 511, as said below
- block_count: int32 [256], P(('wide', 'narrow')), may hold values from 128 to 256, as said below
- near_source: int32 [27, 65536], P(None, ('wide', 'narrow')), may hold values from 0 to 2303
Outputs:
- result: float32 [2, 64, 65536], P(None, None, ('wide', 'narrow'))
Inputs may be any that keep to these rules, and one draw needn't show every extreme that they name: `block_count`: slots at or beyond a device's count hold no block; at least one device has all 256 slots occupied. `block_site`: distinct among the slots of one device.
All inputs are finite; a program needn't handle non-finite values.
Results may differ from a plain program's by a relative error of at most 0.0003.
Values sent between devices are 32-bit elements; how exact they have to be, the bound alone decides.
No kernel may reach another device: no remote copies, remote signals or barrier semaphores. Data moves between devices by JAX's collectives and lax.ppermute only.
A program may use at most 128 MiB of HBM per device.

v0:
```python
import numpy as np

import jax
import jax.numpy as jnp
from jax import lax
from jax.experimental import pallas as pl
from jax.experimental.pallas import tpu as pltpu
from jax.sharding import PartitionSpec as P

W = 64
N = 4
F32 = jnp.float32
BF16 = jnp.bfloat16
VMEM = pltpu.VMEM
BOTH = ("wide", "narrow")


def halves(table):
    high = table.astype(jnp.bfloat16)
    low = (table - high.astype(np.float64)).astype(jnp.bfloat16)
    return high, low


def split(value):
    high = value.astype(BF16)
    return high, (value - high.astype(F32)).astype(BF16)


def dot(left, right):
    return lax.dot_general(left, right, (((1,), (0,)), ((), ())), preferred_element_type=F32)


def dot_t(left, right):
    return lax.dot_general(left, right, (((1,), (1,)), ((), ())), preferred_element_type=F32)


def dot3(lh, ll, rh, rl):
    return dot(lh, rh) + (dot(lh, rl) + dot(ll, rh))


def tables():
    z = np.arange(128)
    z_of = 4 * (z % 32) + z // 32
    kz = np.arange(256)
    ang = 2 * np.pi * ((kz[:, None] * z_of[None, :]) % 256) / 256
    forward_z = np.concatenate([np.cos(ang), np.sin(ang)], 1)
    inverse_z = np.concatenate([np.cos(ang).T, -np.sin(ang).T], 1) * 2.0**-26
    lane = np.arange(2048)
    group, inner = lane // 128, lane % 128
    ez, ex = group // 4, group % 4
    r, ey = inner // 64, inner // 16 % 4
    row = r * 64 + 16 * ex + 4 * ey + ez
    expand = (np.arange(128)[:, None] == row[None, :]).astype(np.float32)
    k = np.arange(512)
    col = np.arange(512)
    n, rr, q = col // 128, col // 64 % 2, col % 64
    y = 64 * n + 4 * (q % 16) + q // 16
    ang = 2 * np.pi * ((y[:, None] * k[None, :]) % 512) / 512
    c, s = np.cos(ang), np.sin(ang)
    real = rr[:, None] == 0
    along = np.concatenate([np.where(real, c, s), np.where(real, -s, c)], 1)
    xi = np.arange(256)
    x = 4 * (xi % 64) + xi // 64
    ang = 2 * np.pi * ((k[:, None] * x[None, :]) % 512) / 512
    c, s = np.cos(ang), np.sin(ang)
    across = np.block([[c, s], [-s, c]])
    return forward_z, inverse_z, expand, along, across


def swap(value):
    lanes = value.shape[1]
    rolled = jnp.concatenate(
        [pltpu.roll(value[:, i : i + 128], 64, 1) for i in range(0, lanes, 128)], axis=1
    )
    sign = jnp.where(lax.broadcasted_iota(jnp.int32, (1, lanes), 1) % 128 < 64, 1.0, -1.0)
    return rolled * sign


def site_masks(count, site):
    rows = lax.broadcasted_iota(jnp.int32, (32, 256), 0)
    line = jnp.where(rows == site % 32, 1.0, 0.0)
    lanes = lax.broadcasted_iota(jnp.int32, (128, 256), 0)
    slots = lax.broadcasted_iota(jnp.int32, (128, 256), 1)
    plane = jnp.where((lanes % 16 == site // 32) & (slots < count), 1.0, 0.0)
    return line, plane.T


def to_grid(count_ref, site_ref, charges_ref, proj_ref, expand_ref, fh_ref, fl_ref, masked_ref, out_ref):
    count = count_ref[0]
    line, plane = site_masks(count, site_ref[...])
    slots = lax.broadcasted_iota(jnp.int32, (128, 256), 1)
    masked = jnp.where(slots < count, charges_ref[...], 0.0)
    turned = masked.T
    masked_ref[...] = turned
    ph, plo = split(proj_ref[...])
    parts = []
    for r in range(2):
        mh, ml = split(turned[:, 64 * r : 64 * r + 64])
        parts.append(dot_t(mh, ph) + (dot_t(mh, plo) + dot_t(ml, ph)))
    stencil = jnp.concatenate(parts, axis=1)
    sh, sl = split(stencil)
    line = line.astype(BF16)
    rows = []
    for ez in range(4):
        cols = []
        for ex in range(4):
            lo = (ez * 4 + ex) * 128
            e = expand_ref[:, lo : lo + 128]
            high = (dot(sh, e) * plane).astype(BF16)
            low = (dot(sl, e) * plane).astype(BF16)
            cols.append(dot(line, high) + dot(line, low))
        rows.append(jnp.concatenate(cols, axis=1))
    grid = jnp.concatenate(rows, axis=0)
    gh, gl = split(jnp.concatenate([grid, swap(grid)], axis=0))
    for ex in range(4):
        c = slice(128 * ex, 128 * ex + 128)
        out_ref[pl.ds(ex, 256, stride=4), :] = dot3(fh_ref[...], fl_ref[...], gh[:, c], gl[:, c])


def convolve(in_ref, green_ref, yh_ref, yl_ref, xh_ref, xl_ref, ih_ref, il_ref, out_ref,
             dh, dl, sh, sl, ph, plo, uh, ul):
    for n in range(4):
        for ex in range(4):
            h, l = split(in_ref[pl.ds(n * 4 + ex, 64, stride=16), :])
            dh[64 * ex : 64 * ex + 64, 128 * n : 128 * n + 128] = h
            dl[64 * ex : 64 * ex + 64, 128 * n : 128 * n + 128] = l
    for j in range(4):
        c = slice(256 * j, 256 * j + 256)
        h, l = split(dot3(dh[...], dl[...], yh_ref[:, c], yl_ref[:, c]))
        r, o = j // 2, 256 * (j % 2)
        sh[256 * r : 256 * r + 256, o : o + 256] = h
        sl[256 * r : 256 * r + 256, o : o + 256] = l
    for j in range(2):
        c = slice(256 * j, 256 * j + 256)
        for i in range(2):
            a = slice(256 * i, 256 * i + 256)
            b = slice(512 + 256 * i, 768 + 256 * i)
            re = dot3(xh_ref[a, :], xl_ref[a, :], sh[:, c], sl[:, c])
            im = dot3(xh_ref[b, :], xl_ref[b, :], sh[:, c], sl[:, c])
            gr, gi = green_ref[0, a, c], green_ref[1, a, c]
            h, l = split(gr * re - gi * im)
            ph[a, c] = h
            plo[a, c] = l
            h, l = split(gr * im + gi * re)
            ph[b, c] = h
            plo[b, c] = l
        for r in range(2):
            a = slice(256 * r, 256 * r + 256)
            h, l = split(dot3(ih_ref[a, :], il_ref[a, :], ph[:, c], plo[:, c]))
            o = slice(512 * r + 256 * j, 512 * r + 256 * j + 256)
            uh[:, o] = h
            ul[:, o] = l
    for j in range(2):
        a = slice(256 * j, 256 * j + 256)
        v = dot_t(uh[...], yh_ref[a, :]) + (dot_t(uh[...], yl_ref[a, :]) + dot_t(ul[...], yh_ref[a, :]))
        for m in range(2):
            n = 2 * j + m
            for ex in range(4):
                out_ref[pl.ds(n * 4 + ex, 64, stride=16), :] = v[64 * ex : 64 * ex + 64, 128 * m : 128 * m + 128]


def from_grid(count_ref, site_ref, in_ref, proj_ref, expand_ref, fh_ref, fl_ref, near_ref, out_ref):
    count = count_ref[0]
    line, plane = site_masks(count, site_ref[...])
    field = jnp.concatenate([in_ref[pl.ds(ex, 256, stride=4), :] for ex in range(4)], axis=1)
    vh, vl = split(jnp.concatenate([field, swap(field)], axis=0))
    points = dot3(fh_ref[...], fl_ref[...], vh, vl)
    bh, bl = split(points)
    pick = line.T.astype(BF16)
    total = jnp.zeros((256, 128), F32)
    for ez in range(4):
        rows = slice(32 * ez, 32 * ez + 32)
        for ex in range(4):
            c = slice(128 * ex, 128 * ex + 128)
            high = (dot(pick, bh[rows, c]) * plane).astype(BF16)
            low = (dot(pick, bl[rows, c]) * plane).astype(BF16)
            lo = (ez * 4 + ex) * 128
            e = expand_ref[:, lo : lo + 128]
            total = total + (dot_t(high, e) + dot_t(low, e))
    th, tl = split(total)
    ph, plo = split(proj_ref[...])
    parts = []
    for r in range(2):
        c = slice(64 * r, 64 * r + 64)
        parts.append(dot3(th[:, c], tl[:, c], ph, plo))
    far = jnp.concatenate(parts, axis=1).T
    slots = lax.broadcasted_iota(jnp.int32, (128, 256), 1)
    out_ref[...] = far + jnp.where(slots < count, near_ref[...], 0.0)


CLASSES = 27


def near(index_ref, source_ref, table_ref, out_ref, picked):
    def one(k, carry):
        for b in range(256):
            i = index_ref[k * 256 + b]
            picked[k, pl.ds(b, 1), :] = source_ref[pl.ds(i, 1), :]
        return carry

    lax.fori_loop(0, CLASSES, one, 0)
    total = jnp.zeros((256, 128), F32)
    for k in range(CLASSES):
        gh, gl = split(picked[k])
        th, tl = split(table_ref[k])
        total = total + (dot(gh, th) + (dot(gh, tl) + dot(gl, th)))
    out_ref[...] = total.T


def call(kernel, outs, args, smem, scratch=(), flops=0, bytes_accessed=0, name=None):
    specs = [pl.BlockSpec(memory_space=pltpu.SMEM if i in smem else VMEM) for i in range(len(args))]
    single = not isinstance(outs, (tuple, list))
    return pl.pallas_call(
        kernel,
        out_shape=outs,
        in_specs=specs,
        out_specs=pl.BlockSpec(memory_space=VMEM) if single else tuple(pl.BlockSpec(memory_space=VMEM) for _ in outs),
        scratch_shapes=list(scratch),
        compiler_params=pltpu.CompilerParams(vmem_limit_bytes=40 << 20),
        cost_estimate=pl.CostEstimate(flops=flops, bytes_accessed=bytes_accessed, transcendentals=0),
        name=name,
    )(*args)


def neighbours(array, axis, size):
    up = [(i, i + 1) for i in range(size - 1)]
    down = [(i + 1, i) for i in range(size - 1)]
    return lax.ppermute(array, axis, up), lax.ppermute(array, axis, down)


def per_device(charges, projection, green_hat, near_table, block_site, block_count, near_source):
    forward_z, inverse_z, expand, along, across = tables()
    fzh, fzl = halves(forward_z)
    izh, izl = halves(inverse_z)
    yh, yl = halves(along)
    xh, xl = halves(across)
    ih, il = halves(np.ascontiguousarray(across.T))
    expand = expand.astype(jnp.bfloat16)
    site = block_site.reshape(1, 256)
    shape = lambda *s: jax.ShapeDtypeStruct(s, F32)

    masked, sent = call(
        to_grid, (shape(256, 128), shape(1024, 128)),
        (block_count, site, charges.reshape(128, 256), projection, expand, fzh, fzl), (0,),
        flops=2 * 10**9, bytes_accessed=2 << 20, name="to_grid",
    )
    before, after = neighbours(masked, "wide", W)
    own = jnp.concatenate([before, masked, after], axis=0)
    planes = lax.all_to_all(sent.reshape(256, 4, 128), BOTH, split_axis=0, concat_axis=0, tiled=True)
    left, right = neighbours(own, "narrow", N)
    back = call(
        convolve, shape(1024, 128),
        (planes.reshape(1024, 128), green_hat.reshape(2, 512, 512), yh, yl, xh, xl, ih, il), (),
        scratch=[VMEM((256, 512), BF16)] * 2 + [VMEM((512, 512), BF16)] * 2
        + [VMEM((1024, 512), BF16)] * 2 + [VMEM((256, 1024), BF16)] * 2,
        flops=5 * 10**9, bytes_accessed=9 << 20, name="convolve",
    )
    field = lax.all_to_all(back.reshape(256, 4, 128), BOTH, split_axis=0, concat_axis=0, tiled=True)
    source = jnp.stack([left.reshape(3, 256, 128), own.reshape(3, 256, 128), right.reshape(3, 256, 128)], axis=1)
    turned = near_table.transpose(0, 1, 3, 2)
    table = jnp.concatenate(
        [
            jnp.concatenate([turned[:, 0], turned[:, 1]], axis=2),
            jnp.concatenate([-turned[:, 1], turned[:, 0]], axis=2),
        ],
        axis=1,
    )
    beside = call(
        near, shape(128, 256),
        (near_source.reshape(CLASSES * 256), source.reshape(2304, 128), table), (0,),
        scratch=[VMEM((CLASSES, 256, 128), F32)],
        flops=10**10, bytes_accessed=40 << 20, name="near",
    )
    result = call(
        from_grid, shape(128, 256),
        (block_count, site, field.reshape(1024, 128), projection, expand, izh, izl, beside), (0,),
        flops=2 * 10**9, bytes_accessed=2 << 20, name="from_grid",
    )
    return result.reshape(2, 64, 256)


def solution(mesh):
    placed = (
        P(None, None, BOTH),
        P(),
        P(None, BOTH, None, None),
        P(),
        P(BOTH),
        P(BOTH),
        P(None, BOTH),
    )
    return jax.shard_map(
        per_device,
        mesh=mesh,
        in_specs=placed,
        out_specs=P(None, None, BOTH),
        check_vma=False,
    )
```

profile of v0, /device:TPU:1, one launch (start us, length us, event | category | flops | bytes accessed | tf_op | source)
XLA Modules:
  0.0 98.8 jit_solution(18349234355782599023)
XLA Ops:
  3.0 1.0 %copy-done.12 = bf16[128,2048]{1,0:T(8,128)(2,1)S(1)} copy-done((bf16[128,2048]{1,0:T(8,128)(2,1)S(1)}, bf16[128,2048]{1,0:T(8,128)(2,1)}, u32[]{:S(2)}) %copy-start.12) | copy-done | bytes 524312
  4.0 0.9 copy-done.16
  5.8 4.7 %to_grid.1 = (f32[256,128]{1,0:T(8,128)S(1)}, f32[1024,128]{1,0:T(8,128)}) custom-call(s32[1]{0:T(128)S(6)} %copy.25.count_ref, s32[1,256]{1,0:T(1,128)S(1)} %bitcast.30, f32[128,256]{1,0:T(8,128)S(1)} %bitcast.29, f32[64,64]{1,0:T(8,128)S(1)} %copy-done.2, bf16[128,2048]{1,0:T(8,128)(2,1)S(1)} %copy-done.12, bf16[256,256]{1,0:T(8,128)(2,1)S(1)} %copy-done.16, ...), custom_call_target="tpu_custom_call" | custom-call | flops 2000000000 | bytes 2097152 | tf_op jit(solution)/shard_map/to_grid/pallas_call | solution.py:213
  10.6 4.6 %collective-permute-start = (f32[256,128]{1,0:T(8,128)S(1)}, f32[256,128]{1,0:T(8,128)}, u32[]{:S(2)}, u32[]{:S(2)}) collective-permute-start(f32[256,128]{1,0:T(8,128)S(1)} %get-tuple-element.8), channel_id=1, source_target_pairs={{0,4},{4,8},{8,12},{12,16},{16,20},{20,24},{24,28},{28,32},{32,36}... | collective-permute-start | bytes 393224 | tf_op jit(solution)/shard_map/ppermute | solution.py:228
  15.2 1.3 %collective-permute-start.1 = (f32[256,128]{1,0:T(8,128)S(1)}, f32[256,128]{1,0:T(8,128)}, u32[]{:S(2)}, u32[]{:S(2)}) collective-permute-start(f32[256,128]{1,0:T(8,128)S(1)} %get-tuple-element.8), channel_id=1, source_target_pairs={{4,0},{8,4},{12,8},{16,12},{20,16},{24,20},{28,24},{32,28},{36,32}... | collective-permute-start | bytes 393224 | tf_op jit(solution)/shard_map/ppermute | solution.py:228
  16.5 17.4 %all-to-all-start = ((f32[256,4,128]{2,1,0:T(4,128)}), f32[256,4,128]{2,1,0:T(4,128)S(1)}, u32[]{:S(2)}, u32[]{:S(2)}) async-start(f32[256,4,128]{2,1,0:T(4,128)} %bitcast.2), calls=%async_computation | async-start | bytes 1048576 | tf_op jit(solution)/shard_map/all_to_all | solution.py:249
  33.9 1.8 %copy.22 = f32[27,2,64,64]{2,3,0,1:T(8,128)S(1)} copy(f32[27,2,64,64]{3,2,1,0:T(8,128)} %param.21) | data formatting | bytes 1769472 | tf_op args[3]
  36.5 1.6 %constant_dynamic-update-slice_fusion.2 = f32[768,128]{1,0:T(8,128)} fusion(f32[256,128]{1,0:T(8,128)} %collective-permute-done), kind=kLoop, calls=%fused_computation.6 | loop fusion | bytes 262144
  38.7 1.6 %constant_dynamic-update-slice_fusion = f32[768,128]{1,0:T(8,128)} fusion(f32[768,128]{1,0:T(8,128)} %constant_dynamic-update-slice_fusion.1, f32[256,128]{1,0:T(8,128)} %collective-permute-done.1), kind=kLoop, calls=%fused_computation.4 | loop fusion | bytes 262144 | tf_op jit(solution)/shard_map/concatenate | solution.py:248
  40.3 4.0 %collective-permute-start.3 = (f32[768,128]{1,0:T(8,128)}, f32[768,128]{1,0:T(8,128)}, u32[]{:S(2)}, u32[]{:S(2)}) collective-permute-start(f32[768,128]{1,0:T(8,128)} %constant_dynamic-update-slice_fusion), channel_id=1, source_target_pairs={{1,0},{2,1},{3,2},{5,4},{6,5},{7,6},{9,8},{10,9},{11,10},{13,12},{... | collective-permute-start | bytes 1179656 | tf_op jit(solution)/shard_map/ppermute | solution.py:228
  44.3 1.9 %collective-permute-start.2 = (f32[768,128]{1,0:T(8,128)}, f32[768,128]{1,0:T(8,128)}, u32[]{:S(2)}, u32[]{:S(2)}) collective-permute-start(f32[768,128]{1,0:T(8,128)} %constant_dynamic-update-slice_fusion), channel_id=1, source_target_pairs={{0,1},{1,2},{2,3},{4,5},{5,6},{6,7},{8,9},{9,10},{10,11},{12,13},{... | collective-permute-start | bytes 1179656 | tf_op jit(solution)/shard_map/ppermute | solution.py:228
  46.2 8.8 %all-to-all-done = f32[256,4,128]{2,1,0:T(4,128)S(1)} async-done(((f32[256,4,128]{2,1,0:T(4,128)}), f32[256,4,128]{2,1,0:T(4,128)S(1)}, u32[]{:S(2)}, u32[]{:S(2)}) %all-to-all-start) | async-done | bytes 524320 | tf_op jit(solution)/shard_map/all_to_all | solution.py:249
  55.1 1.6 %copy-done = f32[2,1,512,512]{3,2,1,0:T(8,128)S(1)} copy-done((f32[2,1,512,512]{3,2,1,0:T(8,128)S(1)}, f32[2,1,512,512]{3,2,1,0:T(8,128)}, u32[]{:S(2)}) %copy-start) | copy-done | bytes 2097176
  56.7 1.2 %copy-done.7 = bf16[512,1024]{1,0:T(8,128)(2,1)S(1)} copy-done((bf16[512,1024]{1,0:T(8,128)(2,1)S(1)}, bf16[512,1024]{1,0:T(8,128)(2,1)}, u32[]{:S(2)}) %copy-start.7) | copy-done | bytes 1048600
  57.9 1.2 %copy-done.8 = bf16[1024,512]{1,0:T(8,128)(2,1)S(1)} copy-done((bf16[1024,512]{1,0:T(8,128)(2,1)S(1)}, bf16[1024,512]{1,0:T(8,128)(2,1)}, u32[]{:S(2)}) %copy-start.8) | copy-done | bytes 1048600
  59.1 1.2 %copy-done.9 = bf16[1024,512]{1,0:T(8,128)(2,1)S(1)} copy-done((bf16[1024,512]{1,0:T(8,128)(2,1)S(1)}, bf16[1024,512]{1,0:T(8,128)(2,1)}, u32[]{:S(2)}) %copy-start.9) | copy-done | bytes 1048600
  60.4 1.2 %copy-done.10 = bf16[512,1024]{1,0:T(8,128)(2,1)S(1)} copy-done((bf16[512,1024]{1,0:T(8,128)(2,1)S(1)}, bf16[512,1024]{1,0:T(8,128)(2,1)}, u32[]{:S(2)}) %copy-start.10) | copy-done | bytes 1048600
  61.6 1.2 %copy-done.11 = bf16[512,1024]{1,0:T(8,128)(2,1)S(1)} copy-done((bf16[512,1024]{1,0:T(8,128)(2,1)S(1)}, bf16[512,1024]{1,0:T(8,128)(2,1)}, u32[]{:S(2)}) %copy-start.11) | copy-done | bytes 1048600
  62.8 6.3 %convolve.1 = f32[1024,128]{1,0:T(8,128)} custom-call(f32[1024,128]{1,0:T(8,128)S(1)} %bitcast.26, f32[2,512,512]{2,1,0:T(8,128)S(1)} %bitcast.28, bf16[512,1024]{1,0:T(8,128)(2,1)S(1)} %copy-done.6, bf16[512,1024]{1,0:T(8,128)(2,1)S(1)} %copy-done.7, bf16[1024,512]{1,0:T(8,128)(2,1)S(1)} %copy-done.8, bf16[1024,512]{1,0:T(8,128)(2,1)S(1)} %copy-done.9, ...), custom_call_target="tpu_custom_call" | custom-call | flops 5000000000 | bytes 9437184 | tf_op jit(solution)/shard_map/convolve/pallas_call | solution.py:213
  69.1 5.4 %all-to-all-start.1 = ((f32[256,4,128]{2,1,0:T(4,128)}), f32[256,4,128]{2,1,0:T(4,128)S(1)}, u32[]{:S(2)}, u32[]{:S(2)}) async-start(f32[256,4,128]{2,1,0:T(4,128)} %bitcast.5), calls=%async_computation.1 | async-start | bytes 1048576 | tf_op jit(solution)/shard_map/all_to_all | solution.py:258
  74.6 1.3 %pad_maximum_fusion = f32[3,3,256,128]{3,2,1,0:T(8,128)S(1)} fusion(f32[3,1,256,128]{3,2,1,0:T(8,128)} %bitcast.12, f32[3,1,256,128]{3,2,1,0:T(8,128)} %bitcast.10, f32[3,1,256,128]{3,2,1,0:T(8,128)} %bitcast.8), kind=kLoop, calls=%fused_computation.1 | loop fusion | flops 589824 | bytes 2359296 | tf_op jit(solution)/shard_map/stack | solution.py:259
  76.0 8.2 %near.1.near_ref = f32[128,256]{1,0:T(8,128)S(1)} custom-call(s32[6912]{0:T(1024)S(1)} %reshape.37.index_ref, f32[2304,128]{1,0:T(8,128)S(1)} %bitcast.25, f32[27,128,128]{2,1,0:T(8,128)S(1)} %maximum_maximum_fusion.table_ref), custom_call_target="tpu_custom_call" | custom-call | flops 10000000000 | bytes 41943040 | tf_op jit(solution)/shard_map/near/pallas_call | solution.py:213
  84.1 11.8 %all-to-all-done.1 = f32[256,4,128]{2,1,0:T(4,128)S(1)} async-done(((f32[256,4,128]{2,1,0:T(4,128)}), f32[256,4,128]{2,1,0:T(4,128)S(1)}, u32[]{:S(2)}, u32[]{:S(2)}) %all-to-all-start.1) | async-done | bytes 524320 | tf_op jit(solution)/shard_map/all_to_all | solution.py:258
  95.9 2.8 %from_grid.1 = f32[128,256]{1,0:T(8,128)} custom-call(s32[1]{0:T(128)S(6)} %copy.25.count_ref, s32[1,256]{1,0:T(1,128)S(1)} %bitcast.31, f32[1024,128]{1,0:T(8,128)S(1)} %bitcast.27, f32[64,64]{1,0:T(8,128)S(1)} %copy-done.3, bf16[128,2048]{1,0:T(8,128)(2,1)S(1)} %copy-done.13, bf16[128,512]{1,0:T(8,128)(2,1)S(1)} %copy-done.14, ...), custom_call_target="tpu_custom_call" | custom-call | flops 2000000000 | bytes 2097152 | tf_op jit(solution)/shard_map/from_grid/pallas_call | solution.py:213
  (39 shorter events, 4.7 us)
Async XLA Ops:
  0.7 0.9 copy-start.1
  1.6 0.8 copy-start.2
  3.0 1.0 %copy-start.12 = (bf16[128,2048]{1,0:T(8,128)(2,1)S(1)}, bf16[128,2048]{1,0:T(8,128)(2,1)}, u32[]{:S(2)}) copy-start(bf16[128,2048]{1,0:T(8,128)(2,1)} %constant.22.clone.expand_ref) | copy-start | bytes 1572868
  4.0 0.9 copy-start.16
  4.9 0.9 copy-start.17
  10.6 25.9 %collective-permute-start = (f32[256,128]{1,0:T(8,128)S(1)}, f32[256,128]{1,0:T(8,128)}, u32[]{:S(2)}, u32[]{:S(2)}) collective-permute-start(f32[256,128]{1,0:T(8,128)S(1)} %get-tuple-element.8), channel_id=1, source_target_pairs={{0,4},{4,8},{8,12},{12,16},{16,20},{20,24},{24,28},{28,32},{32,36}... | collective-permute-start | bytes 393224 | tf_op jit(solution)/shard_map/ppermute | solution.py:228
  15.2 23.5 %collective-permute-start.1 = (f32[256,128]{1,0:T(8,128)S(1)}, f32[256,128]{1,0:T(8,128)}, u32[]{:S(2)}, u32[]{:S(2)}) collective-permute-start(f32[256,128]{1,0:T(8,128)S(1)} %get-tuple-element.8), channel_id=1, source_target_pairs={{4,0},{8,4},{12,8},{16,12},{20,16},{24,20},{28,24},{32,28},{36,32}... | collective-permute-start | bytes 393224 | tf_op jit(solution)/shard_map/ppermute | solution.py:228
  16.5 38.6 %all-to-all-start = ((f32[256,4,128]{2,1,0:T(4,128)}), f32[256,4,128]{2,1,0:T(4,128)S(1)}, u32[]{:S(2)}, u32[]{:S(2)}) async-start(f32[256,4,128]{2,1,0:T(4,128)} %bitcast.2), calls=%async_computation | async-start | bytes 1048576 | tf_op jit(solution)/shard_map/all_to_all | solution.py:249
  33.9 1.8 %copy-start.18 = (s32[27,256]{1,0:T(8,128)S(1)}, s32[27,256]{1,0:T(8,128)}, u32[]{:S(2)}) copy-start(s32[27,256]{1,0:T(8,128)} %param.24) | copy-start | bytes 82948
  35.9 19.2 %copy-start.6 = (bf16[512,1024]{1,0:T(8,128)(2,1)S(1)}, bf16[512,1024]{1,0:T(8,128)(2,1)}, u32[]{:S(2)}) copy-start(bf16[512,1024]{1,0:T(8,128)(2,1)} %constant.25.clone.yh_ref) | copy-start | bytes 3145732
  40.3 34.3 %collective-permute-start.3 = (f32[768,128]{1,0:T(8,128)}, f32[768,128]{1,0:T(8,128)}, u32[]{:S(2)}, u32[]{:S(2)}) collective-permute-start(f32[768,128]{1,0:T(8,128)} %constant_dynamic-update-slice_fusion), channel_id=1, source_target_pairs={{1,0},{2,1},{3,2},{5,4},{6,5},{7,6},{9,8},{10,9},{11,10},{13,12},{... | collective-permute-start | bytes 1179656 | tf_op jit(solution)/shard_map/ppermute | solution.py:228
  44.3 30.2 %collective-permute-start.2 = (f32[768,128]{1,0:T(8,128)}, f32[768,128]{1,0:T(8,128)}, u32[]{:S(2)}, u32[]{:S(2)}) collective-permute-start(f32[768,128]{1,0:T(8,128)} %constant_dynamic-update-slice_fusion), channel_id=1, source_target_pairs={{0,1},{1,2},{2,3},{4,5},{5,6},{6,7},{8,9},{9,10},{10,11},{12,13},{... | collective-permute-start | bytes 1179656 | tf_op jit(solution)/shard_map/ppermute | solution.py:228
  55.1 1.6 %copy-start = (f32[2,1,512,512]{3,2,1,0:T(8,128)S(1)}, f32[2,1,512,512]{3,2,1,0:T(8,128)}, u32[]{:S(2)}) copy-start(f32[2,1,512,512]{3,2,1,0:T(8,128)} %param.20) | copy-start | bytes 6291460
  56.7 1.2 %copy-start.7 = (bf16[512,1024]{1,0:T(8,128)(2,1)S(1)}, bf16[512,1024]{1,0:T(8,128)(2,1)}, u32[]{:S(2)}) copy-start(bf16[512,1024]{1,0:T(8,128)(2,1)} %constant.26.clone.yl_ref) | copy-start | bytes 3145732
  57.9 1.2 %copy-start.8 = (bf16[1024,512]{1,0:T(8,128)(2,1)S(1)}, bf16[1024,512]{1,0:T(8,128)(2,1)}, u32[]{:S(2)}) copy-start(bf16[1024,512]{1,0:T(8,128)(2,1)} %constant.27.clone.xh_ref) | copy-start | bytes 3145732
  59.1 1.2 %copy-start.9 = (bf16[1024,512]{1,0:T(8,128)(2,1)S(1)}, bf16[1024,512]{1,0:T(8,128)(2,1)}, u32[]{:S(2)}) copy-start(bf16[1024,512]{1,0:T(8,128)(2,1)} %constant.28.clone.xl_ref) | copy-start | bytes 3145732
  60.4 1.2 %copy-start.10 = (bf16[512,1024]{1,0:T(8,128)(2,1)S(1)}, bf16[512,1024]{1,0:T(8,128)(2,1)}, u32[]{:S(2)}) copy-start(bf16[512,1024]{1,0:T(8,128)(2,1)} %constant.29.clone.ih_ref) | copy-start | bytes 3145732
  61.6 1.2 %copy-start.11 = (bf16[512,1024]{1,0:T(8,128)(2,1)S(1)}, bf16[512,1024]{1,0:T(8,128)(2,1)}, u32[]{:S(2)}) copy-start(bf16[512,1024]{1,0:T(8,128)(2,1)} %constant.30.clone.il_ref) | copy-start | bytes 3145732
  69.1 26.8 %all-to-all-start.1 = ((f32[256,4,128]{2,1,0:T(4,128)}), f32[256,4,128]{2,1,0:T(4,128)S(1)}, u32[]{:S(2)}, u32[]{:S(2)}) async-start(f32[256,4,128]{2,1,0:T(4,128)} %bitcast.5), calls=%async_computation.1 | async-start | bytes 1048576 | tf_op jit(solution)/shard_map/all_to_all | solution.py:258
  75.9 20.0 %copy-start.3 = (f32[64,64]{1,0:T(8,128)S(1)}, f32[64,64]{1,0:T(8,128)}, u32[]{:S(2)}) copy-start(f32[64,64]{1,0:T(8,128)} %proj_ref.3) | copy-start | bytes 49156
  75.9 20.0 %copy-start.5 = (s32[256]{0:T(256)S(1)}, s32[256]{0:T(256)}, u32[]{:S(2)}) copy-start(s32[256]{0:T(256)} %param.22) | copy-start | bytes 3076
  75.9 20.0 %copy-start.13 = (bf16[128,2048]{1,0:T(8,128)(2,1)S(1)}, bf16[128,2048]{1,0:T(8,128)(2,1)}, u32[]{:S(2)}) copy-start(bf16[128,2048]{1,0:T(8,128)(2,1)} %constant.22.clone.expand_ref) | copy-start | bytes 1572868
  75.9 20.0 %copy-start.14 = (bf16[128,512]{1,0:T(8,128)(2,1)S(1)}, bf16[128,512]{1,0:T(8,128)(2,1)}, u32[]{:S(2)}) copy-start(bf16[128,512]{1,0:T(8,128)(2,1)} %constant.31.clone.fh_ref) | copy-start | bytes 393220
  75.9 20.0 %copy-start.15 = (bf16[128,512]{1,0:T(8,128)(2,1)S(1)}, bf16[128,512]{1,0:T(8,128)(2,1)}, u32[]{:S(2)}) copy-start(bf16[128,512]{1,0:T(8,128)(2,1)} %constant.32.clone.fl_ref) | copy-start | bytes 393220
  (1 other events, 0.7 us)
where the time goes:
time: 99.6 us; the launch traced here: 98.8 us
  starting transfers between devices  34.7 us (35%)
  Pallas kernels  22.1 us (22%)
  waiting for transfers between devices  20.6 us (21%)
  local copies, waits for them, and re-layouts  18.7 us (19%)
  other arithmetic  1.91 us (2%)
    pallas_call x4, Pallas kernels, call(): pl.pallas_call(kernel, out_shape=outs, in_specs=specs, out_specs=pl.Block...  22.1 us
    all_to_all x1, starting transfers between devices, per_device(): lax.all_to_all(sent.reshape(256, 4, 128), BOTH, split_axis=0, concat_axis...  17.4 us
    unnamed x41, local copies, waits for them, and re-layouts  17 us
    ppermute x4, starting transfers between devices, neighbours(): return (lax.ppermute(array, axis, up), lax.ppermute(array, axis, down))  11.8 us
    all_to_all x1, waiting for transfers between devices, per_device(): lax.all_to_all(back.reshape(256, 4, 128), BOTH, split_axis=0, concat_axis...  11.8 us
    all_to_all x1, waiting for transfers between devices, per_device(): lax.all_to_all(sent.reshape(256, 4, 128), BOTH, split_axis=0, concat_axis...  8.83 us
    all_to_all x1, starting transfers between devices, per_device(): lax.all_to_all(back.reshape(256, 4, 128), BOTH, split_axis=0, concat_axis...  5.43 us
  transfers between devices with their start and end apart: 6, of which 2 were waited for; matrix products, arithmetic and copies ran while one was open for 8% of the time, Pallas kernels for 15%

commit v1 on v0

v1 whole, which is shorter than its diff:
```python
import numpy as np

import jax
import jax.numpy as jnp
from jax import lax
from jax.experimental import pallas as pl
from jax.experimental.pallas import tpu as pltpu
from jax.sharding import PartitionSpec as P

W = 64
N = 4
F32 = jnp.float32
BF16 = jnp.bfloat16
VMEM = pltpu.VMEM
BOTH = ("wide", "narrow")


def halves(table):
    high = table.astype(jnp.bfloat16)
    low = (table - high.astype(np.float64)).astype(jnp.bfloat16)
    return high, low


def split(value):
    high = value.astype(BF16)
    return high, (value - high.astype(F32)).astype(BF16)


def dot(left, right):
    return lax.dot_general(left, right, (((1,), (0,)), ((), ())), preferred_element_type=F32)


def dot_t(left, right):
    return lax.dot_general(left, right, (((1,), (1,)), ((), ())), preferred_element_type=F32)


def dot3(lh, ll, rh, rl):
    return dot(lh, rh) + (dot(lh, rl) + dot(ll, rh))


def tables():
    z = np.arange(128)
    z_of = 4 * (z % 32) + z // 32
    kz = np.arange(256)
    ang = 2 * np.pi * ((kz[:, None] * z_of[None, :]) % 256) / 256
    forward_z = np.concatenate([np.cos(ang), np.sin(ang)], 1)
    inverse_z = np.concatenate([np.cos(ang).T, -np.sin(ang).T], 1) * 2.0**-26
    lane = np.arange(2048)
    group, inner = lane // 128, lane % 128
    ez, ex = group // 4, group % 4
    r, ey = inner // 64, inner // 16 % 2 * 2 + inner // 32 % 2
    row = r * 64 + 16 * ex + 4 * ey + ez
    expand = (np.arange(128)[:, None] == row[None, :]).astype(np.float32)
    k = np.arange(256)
    i = np.arange(256)
    real = (i // 64 % 2 == 0)[:, None]
    along = []
    for p in range(2):
        y = 64 * (i // 128 * 2 + i // 32 % 2) + 4 * (i % 16) + 2 * (i // 16 % 2) + p
        ang = 2 * np.pi * ((y[:, None] * k[None, :]) % 512) / 512
        c, s = np.cos(ang), np.sin(ang)
        along.append(np.concatenate([np.where(real, c, s), np.where(real, -s, c)], 1))
    across = []
    j = np.arange(128)
    for p in range(2):
        x = 4 * (j % 64) + 2 * (j // 64) + p
        ang = 2 * np.pi * ((k[:, None] * x[None, :]) % 512) / 512
        c, s = np.cos(ang), np.sin(ang)
        across.append(np.block([[c, s], [-s, c]]))
    return forward_z, inverse_z, expand, np.stack(along), np.stack(across)


def swap(value):
    lanes = value.shape[1]
    rolled = jnp.concatenate(
        [pltpu.roll(value[:, i : i + 128], 64, 1) for i in range(0, lanes, 128)], axis=1
    )
    sign = jnp.where(lax.broadcasted_iota(jnp.int32, (1, lanes), 1) % 128 < 64, 1.0, -1.0)
    return rolled * sign


def site_masks(count, site):
    rows = lax.broadcasted_iota(jnp.int32, (32, 256), 0)
    line = jnp.where(rows == site % 32, 1.0, 0.0)
    lanes = lax.broadcasted_iota(jnp.int32, (128, 256), 0)
    slots = lax.broadcasted_iota(jnp.int32, (128, 256), 1)
    plane = jnp.where((lanes % 16 == site // 32) & (slots < count), 1.0, 0.0)
    return line, plane.T


def fetch(pairs, sems):
    copies = [pltpu.make_async_copy(s, d, sems.at[i]) for i, (s, d) in enumerate(pairs)]
    for copy in copies:
        copy.start()
    return copies


def to_grid(count_ref, charges_any, site_any, proj_any, expand_any, fh_any, fl_any, out_ref,
            charges_ref, site_ref, proj_ref, expand_ref, fh_ref, fl_ref, sems):
    copies = fetch(
        [(charges_any, charges_ref), (proj_any, proj_ref), (site_any, site_ref),
         (expand_any, expand_ref), (fh_any, fh_ref), (fl_any, fl_ref)], sems)
    count = count_ref[0]
    slots = lax.broadcasted_iota(jnp.int32, (128, 256), 1)
    for copy in copies[:3]:
        copy.wait()
    line, plane = site_masks(count, site_ref[...])
    turned = jnp.where(slots < count, charges_ref[...], 0.0).T
    ph, plo = split(proj_ref[...])
    parts = []
    for r in range(2):
        mh, ml = split(turned[:, 64 * r : 64 * r + 64])
        parts.append(dot_t(mh, ph) + (dot_t(mh, plo) + dot_t(ml, ph)))
    both = jnp.concatenate(split(jnp.concatenate(parts, axis=1)), axis=0)
    plane = jnp.concatenate([plane, plane], axis=1)
    line = line.astype(BF16)
    line = jnp.concatenate([line, line], axis=1)
    copies[3].wait()
    rows = []
    for ez in range(4):
        cols = []
        for e in range(2):
            lo = (ez * 4 + 2 * e) * 128
            spread = dot(both, expand_ref[:, lo : lo + 256])
            high = (spread[:256] * plane).astype(BF16)
            low = (spread[256:] * plane).astype(BF16)
            cols.append(dot(line, jnp.concatenate([high, low], axis=0)))
        rows.append(jnp.concatenate(cols, axis=1))
    grid = jnp.concatenate(rows, axis=0)
    gh, gl = split(jnp.concatenate([grid, swap(grid)], axis=0))
    copies[4].wait()
    copies[5].wait()
    for e in range(2):
        c = slice(256 * e, 256 * e + 256)
        planes = dot3(fh_ref[...], fl_ref[...], gh[:, c], gl[:, c])
        out_ref[pl.ds(2 * e, 256, stride=4), :] = planes[:, :128]
        out_ref[pl.ds(2 * e + 1, 256, stride=4), :] = planes[:, 128:]


def turn(count_ref, charges_ref, after_any, out_ref):
    slots = lax.broadcasted_iota(jnp.int32, (128, 256), 1)
    out_ref[...] = jnp.where(slots < count_ref[0], charges_ref[...], 0.0).T


def join(a_any, b_any, c_any, out_any, sems):
    copies = fetch([(r, out_any.at[pl.ds(256 * i, 256), :]) for i, r in enumerate((a_any, b_any, c_any))], sems)
    for copy in copies:
        copy.wait()


def convolve(in_any, green_any, yh_any, yl_any, xh_any, xl_any, ih_any, il_any, after_any, out_ref,
             in_ref, green_ref, yh, yl, xh, xl, ih, il, ah, al, sh, sl, qh, ql, bh, bl, sems):
    (arrived,) = fetch([(in_any, in_ref)], sems)
    copies = fetch(
        [(yh_any, yh), (yl_any, yl), (xh_any, xh), (xl_any, xl), (green_any, green_ref), (ih_any, ih), (il_any, il)],
        sems.at[pl.ds(1, 7)])
    arrived.wait()
    first = lax.broadcasted_iota(jnp.int32, (64, 128), 1) % 64 < 32
    order = (0, 2, 1, 3)
    for i, ex in enumerate(order):
        a = slice(64 * i, 64 * i + 64)
        for m in range(2):
            c = slice(128 * m, 128 * m + 128)
            d0 = in_ref[pl.ds(8 * m + ex, 64, stride=16), :]
            d1 = in_ref[pl.ds(8 * m + 4 + ex, 64, stride=16), :]
            ah[0, a, c], al[0, a, c] = split(jnp.where(first, d0, pltpu.roll(d1, 32, 1)))
            ah[1, a, c], al[1, a, c] = split(jnp.where(first, pltpu.roll(d0, 96, 1), d1))
    copies[0].wait()
    copies[1].wait()
    for xp in range(2):
        a = slice(128 * xp, 128 * xp + 128)
        for r in range(2):
            c = slice(256 * r, 256 * r + 256)
            even = dot3(ah[0, a, :], al[0, a, :], yh[0, :, c], yl[0, :, c])
            odd = dot3(ah[1, a, :], al[1, a, :], yh[1, :, c], yl[1, :, c])
            o = slice(128 * r, 128 * r + 128)
            sh[xp, o, 0:256], sl[xp, o, 0:256] = split(even + odd)
            sh[xp, o, 256:512], sl[xp, o, 256:512] = split(even - odd)
    copies[2].wait()
    copies[3].wait()
    copies[4].wait()
    for j in range(2):
        c = slice(256 * j, 256 * j + 256)
        for i in range(2):
            lo = slice(128 * i, 128 * i + 128)
            hi = slice(256 + 128 * i, 384 + 128 * i)
            part = [[dot3(xh[xp, a, :], xl[xp, a, :], sh[xp, :, c], sl[xp, :, c]) for xp in range(2)] for a in (lo, hi)]
            (re0, re1), (im0, im1) = part
            re, im = re0 + re1, im0 + im1
            gr, gi = green_ref[0, lo, c], green_ref[1, lo, c]
            p_re, p_im = gr * re - gi * im, gr * im + gi * re
            re, im = re0 - re1, im0 - im1
            gr, gi = green_ref[0, hi, c], green_ref[1, hi, c]
            q_re, q_im = gr * re - gi * im, gr * im + gi * re
            qh[0, lo, c], ql[0, lo, c] = split(p_re + q_re)
            qh[1, lo, c], ql[1, lo, c] = split(p_re - q_re)
            qh[0, hi, c], ql[0, hi, c] = split(p_im + q_im)
            qh[1, hi, c], ql[1, hi, c] = split(p_im - q_im)
    copies[5].wait()
    copies[6].wait()
    for xp in range(2):
        for r in range(2):
            a = slice(128 * r, 128 * r + 128)
            u0, u1 = [
                dot3(ih[xp, a, :], il[xp, a, :], qh[xp, :, c], ql[xp, :, c]) for c in (slice(0, 256), slice(256, 512))
            ]
            rows, o = slice(128 * xp, 128 * xp + 128), slice(256 * r, 256 * r + 256)
            bh[0, rows, o], bl[0, rows, o] = split(u0 + u1)
            bh[1, rows, o], bl[1, rows, o] = split(u0 - u1)
    for xp in range(2):
        a = slice(128 * xp, 128 * xp + 128)
        even, odd = [
            dot_t(bh[p, a, :], yh[p]) + (dot_t(bh[p, a, :], yl[p]) + dot_t(bl[p, a, :], yh[p])) for p in range(2)
        ]
        for e in range(2):
            ex = order[2 * xp + e]
            rows = slice(64 * e, 64 * e + 64)
            for m in range(2):
                c = slice(128 * m, 128 * m + 128)
                ve, vo = even[rows, c], odd[rows, c]
                out_ref[pl.ds(8 * m + ex, 64, stride=16), :] = jnp.where(first, ve, pltpu.roll(vo, 32, 1))
                out_ref[pl.ds(8 * m + 4 + ex, 64, stride=16), :] = jnp.where(first, pltpu.roll(ve, 96, 1), vo)


def from_grid(count_ref, site_ref, in_ref, proj_ref, expand_ref, fh_ref, fl_ref, near_ref, out_ref):
    count = count_ref[0]
    line, plane = site_masks(count, site_ref[...])
    field = jnp.concatenate([in_ref[pl.ds(ex, 256, stride=4), :] for ex in range(4)], axis=1)
    vh, vl = split(jnp.concatenate([field, swap(field)], axis=0))
    points = dot3(fh_ref[...], fl_ref[...], vh, vl)
    bh, bl = split(points)
    pick = line.T.astype(BF16)
    total = jnp.zeros((256, 128), F32)
    for ez in range(4):
        rows = slice(32 * ez, 32 * ez + 32)
        for ex in range(4):
            c = slice(128 * ex, 128 * ex + 128)
            high = (dot(pick, bh[rows, c]) * plane).astype(BF16)
            low = (dot(pick, bl[rows, c]) * plane).astype(BF16)
            lo = (ez * 4 + ex) * 128
            e = expand_ref[:, lo : lo + 128]
            total = total + (dot_t(high, e) + dot_t(low, e))
    th, tl = split(total)
    ph, plo = split(proj_ref[...])
    parts = []
    for r in range(2):
        c = slice(64 * r, 64 * r + 64)
        parts.append(dot3(th[:, c], tl[:, c], ph, plo))
    far = jnp.concatenate(parts, axis=1).T
    slots = lax.broadcasted_iota(jnp.int32, (128, 256), 1)
    out_ref[...] = far + jnp.where(slots < count, near_ref[...], 0.0)


CLASSES = 27


def near_tables(table_ref, after_any, high_ref, low_ref):
    for k in range(CLASSES):
        re, im = table_ref[k, 0], table_ref[k, 1]
        for r, (a, b) in enumerate(((re, -im), (im, re))):
            rows = slice(64 * r, 64 * r + 64)
            high_ref[k, rows, :], low_ref[k, rows, :] = split(jnp.concatenate([a, b], axis=1))


def near(index_ref, left_any, own_any, right_any, high_any, low_any, out_ref, source_ref, picked, high_ref, low_ref, sems):
    sources = [(r, source_ref.at[pl.ds(768 * i, 768), :]) for i, r in enumerate((left_any, own_any, right_any))]
    copies = fetch(sources + [(high_any, high_ref), (low_any, low_ref)], sems)
    for copy in copies[:3]:
        copy.wait()

    def one(k, carry):
        for b in range(256):
            i = index_ref[k * 256 + b]
            picked[k, pl.ds(b, 1), :] = source_ref[pl.ds(i, 1), :]
        return carry

    lax.fori_loop(0, CLASSES, one, 0)
    for copy in copies[3:]:
        copy.wait()
    total = jnp.zeros((256, 128), F32)
    for k in range(CLASSES):
        gh, gl = split(picked[k])
        th, tl = high_ref[k], low_ref[k]
        total = total + (dot_t(gh, th) + (dot_t(gh, tl) + dot_t(gl, th)))
    out_ref[...] = total.T


def call(kernel, outs, args, kinds, scratch=(), copies=0, flops=0, bytes_accessed=0, name=None, out_kind="v", room=40):
    spaces = {"s": pltpu.SMEM, "v": VMEM, "h": pltpu.HBM}
    single = not isinstance(outs, (tuple, list))
    out_spec = pl.BlockSpec(memory_space=spaces[out_kind])
    scratch = list(scratch) + ([pltpu.SemaphoreType.DMA((copies,))] if copies else [])
    return pl.pallas_call(
        kernel,
        out_shape=outs,
        in_specs=[pl.BlockSpec(memory_space=spaces[k]) for k in kinds],
        out_specs=out_spec if single else tuple(out_spec for _ in outs),
        scratch_shapes=scratch,
        compiler_params=pltpu.CompilerParams(vmem_limit_bytes=room << 20),
        cost_estimate=pl.CostEstimate(flops=flops, bytes_accessed=bytes_accessed, transcendentals=0),
        name=name,
    )(*args)


def neighbours(array, axis, size):
    up = [(i, i + 1) for i in range(size - 1)]
    down = [(i + 1, i) for i in range(size - 1)]
    return lax.ppermute(array, axis, up), lax.ppermute(array, axis, down)


def per_device(charges, projection, green_hat, near_table, block_site, block_count, near_source):
    forward_z, inverse_z, expand, along, across = tables()
    fzh, fzl = halves(forward_z)
    izh, izl = halves(inverse_z)
    yh, yl = halves(along)
    xh, xl = halves(across)
    ih, il = halves(np.ascontiguousarray(across.transpose(0, 2, 1)))
    expand = expand.astype(jnp.bfloat16)
    site = block_site.reshape(1, 256)
    shape = lambda *s: jax.ShapeDtypeStruct(s, F32)

    cells = charges.reshape(128, 256)
    sent = call(
        to_grid, shape(1024, 128), (block_count, cells, site, projection, expand, fzh, fzl), "shhhhhh",
        scratch=[VMEM((128, 256), F32), VMEM((1, 256), jnp.int32), VMEM((64, 64), F32), VMEM((128, 2048), BF16)]
        + [VMEM((256, 256), BF16)] * 2,
        copies=6, flops=2 * 10**9, bytes_accessed=2 << 20, name="to_grid", room=63,
    )
    planes = lax.all_to_all(sent.reshape(256, 4, 128), BOTH, split_axis=0, concat_axis=0, tiled=True)
    masked = call(turn, shape(256, 128), (block_count, cells, sent), "svh", bytes_accessed=1 << 20, name="turn", room=63)
    before, after = neighbours(masked, "wide", W)
    own = call(join, shape(768, 128), (before, masked, after), "hhh", copies=3, bytes_accessed=2 << 20, name="join", out_kind="h", room=63)
    left, right = neighbours(own, "narrow", N)
    table = jax.ShapeDtypeStruct((CLASSES, 128, 128), BF16)
    table_high, table_low = call(near_tables, (table, table), (near_table, sent), "vh", bytes_accessed=4 << 20,
                                  name="near_tables", room=63)
    back = call(
        convolve, shape(1024, 128),
        (planes.reshape(1024, 128), green_hat.reshape(2, 512, 512), yh, yl, xh, xl, ih, il, table_high), "hhhhhhhhh",
        scratch=[VMEM((1024, 128), F32), VMEM((2, 512, 512), F32)] + [VMEM((2, 256, 512), BF16)] * 2 + [VMEM((2, 512, 256), BF16)] * 2
        + [VMEM((2, 256, 512), BF16)] * 2 + [VMEM((2, 256, 256), BF16)] * 2 + [VMEM((2, 256, 512), BF16)] * 2
        + [VMEM((2, 512, 512), BF16)] * 2 + [VMEM((2, 256, 512), BF16)] * 2,
        copies=8, flops=5 * 10**9, bytes_accessed=9 << 20, name="convolve", room=63,
    )
    field = lax.all_to_all(back.reshape(256, 4, 128), BOTH, split_axis=0, concat_axis=0, tiled=True)
    step_wide, step_narrow, slot = near_source // 768, near_source // 256 % 3, near_source % 256
    index = (step_narrow * 768 + step_wide * 256 + slot).reshape(CLASSES * 256)
    beside = call(
        near, shape(128, 256), (index, left, own, right, table_high, table_low), "shhhhh",
        scratch=[VMEM((2304, 128), F32), VMEM((CLASSES, 256, 128), F32)] + [VMEM((CLASSES, 128, 128), BF16)] * 2,
        copies=5, flops=10**10, bytes_accessed=40 << 20, name="near", room=63,
    )
    result = call(
        from_grid, shape(128, 256),
        (block_count, site, field.reshape(1024, 128), projection, expand, izh, izl, beside), "svvvvvvv",
        flops=2 * 10**9, bytes_accessed=2 << 20, name="from_grid", room=16,
    )
    return result.reshape(2, 64, 256)


def solution(mesh):
    placed = (
        P(None, None, BOTH),
        P(),
        P(None, BOTH, None, None),
        P(),
        P(BOTH),
        P(BOTH),
        P(None, BOTH),
    )
    return jax.shard_map(
        per_device,
        mesh=mesh,
        in_specs=placed,
        out_specs=P(None, None, BOTH),
        check_vma=False,
    )
```

time: 99.6 us -> 107 us (1.074)
  Pallas kernels: 22.1 us -> 42.8 us
  local copies, waits for them, and re-layouts: 18.7 us -> 4.76 us
  starting transfers between devices: 34.7 us -> 44.3 us
  waiting for transfers between devices: 20.6 us -> 13.3 us
  other arithmetic: 1.91 us -> 0.07 us
    pallas_call x4 -> x7, Pallas kernels: 22.1 us -> 42.8 us  [call(): pl.pallas_call(kernel, out_shape=outs, in_specs=[pl.BlockSpec(memory_spac...]
    unnamed x41 -> x22, local copies, waits for them, and re-layouts: 17 us -> 4.16 us
    all_to_all x1, starting transfers between devices: 5.43 us -> 18.2 us  [per_device(): lax.all_to_all(back.reshape(256, 4, 128), BOTH, split_axis=0, concat_axis...]
    all_to_all x1, waiting for transfers between devices: 8.83 us -> 0.01 us  [per_device(): lax.all_to_all(sent.reshape(256, 4, 128), BOTH, split_axis=0, concat_axis...]
    ppermute x4, waiting for transfers between devices: 0.01 us -> 3.92 us  [neighbours(): return (lax.ppermute(array, axis, up), lax.ppermute(array, axis, down))]
    all_to_all x1, waiting for transfers between devices: 11.8 us -> 9.4 us  [per_device(): lax.all_to_all(back.reshape(256, 4, 128), BOTH, split_axis=0, concat_axis...]
    all_to_all x1, starting transfers between devices: 17.4 us -> 15.7 us  [per_device(): lax.all_to_all(sent.reshape(256, 4, 128), BOTH, split_axis=0, concat_axis...]
    concatenate x1 -> x0, local copies, waits for them, and re-layouts: 1.57 us -> none  [per_device(): own = jnp.concatenate([before, masked, after], axis=0)]
  transfers between devices with their start and end apart: 6 -> 6, of which waited for: 2 -> 2; matrix products, arithmetic and copies ran while one was open for 8% -> 1% of each run, Pallas kernels for 15% -> 33%
where the time goes in v1:
time: 107 us; the launch traced here: 106 us
  starting transfers between devices  44.3 us (41%)
  Pallas kernels  42.8 us (40%)
  waiting for transfers between devices  13.3 us (12%)
  local copies, waits for them, and re-layouts  4.76 us (4%)
    pallas_call x7, Pallas kernels, call(): pl.pallas_call(kernel, out_shape=outs, in_specs=[pl.BlockSpec(memory_spac...  42.8 us
    all_to_all x1, starting transfers between devices, per_device(): lax.all_to_all(back.reshape(256, 4, 128), BOTH, split_axis=0, concat_axis...  18.2 us
    all_to_all x1, starting transfers between devices, per_device(): lax.all_to_all(sent.reshape(256, 4, 128), BOTH, split_axis=0, concat_axis...  15.7 us
    ppermute x4, starting transfers between devices, neighbours(): return (lax.ppermute(array, axis, up), lax.ppermute(array, axis, down))  10.4 us
    all_to_all x1, waiting for transfers between devices, per_device(): lax.all_to_all(back.reshape(256, 4, 128), BOTH, split_axis=0, concat_axis...  9.4 us
    unnamed x22, local copies, waits for them, and re-layouts  4.16 us
    ppermute x4, waiting for transfers between devices, neighbours(): return (lax.ppermute(array, axis, up), lax.ppermute(array, axis, down))  3.92 us
  transfers between devices with their start and end apart: 6, of which 2 were waited for; matrix products, arithmetic and copies ran while one was open for 1% of the time, Pallas kernels for 33%

profile of v1, /device:TPU:1, one launch (start us, length us, event | category | flops | bytes accessed | tf_op | source)
XLA Modules:
  0.0 106.1 jit_solution(9736223401941562471)
XLA Ops:
  0.7 5.0 %to_grid.1.after_any = f32[1024,128]{1,0:T(8,128)} custom-call(s32[1]{0:T(128)S(6)} %copy.19.count_ref, f32[128,256]{1,0:T(8,128)} %bitcast.14, s32[1,256]{1,0:T(1,128)} %bitcast.9, f32[64,64]{1,0:T(8,128)} %proj_ref.1, bf16[128,2048]{1,0:T(8,128)(2,1)} %constant.66.clone.expand_any.expand_ref, bf16[256,256]{1,0:T(8,128)(2,1)} %constant.67.clone.fh_any, ...), custom_call_target="tpu_custom_call" | custom-call | flops 2000000000 | bytes 2097152 | tf_op jit(solution)/shard_map/to_grid/pallas_call | solution.py:293
  5.6 15.7 %all-to-all-start = ((f32[256,4,128]{2,1,0:T(4,128)}), f32[256,4,128]{2,1,0:T(4,128)S(1)}, u32[]{:S(2)}, u32[]{:S(2)}) async-start(f32[256,4,128]{2,1,0:T(4,128)} %bitcast.11), calls=%async_computation | async-start | bytes 1048576 | tf_op jit(solution)/shard_map/all_to_all | solution.py:329
  21.3 1.7 %turn.1.b_any = f32[256,128]{1,0:T(8,128)} custom-call(s32[1]{0:T(128)S(6)} %copy.19.count_ref, f32[128,256]{1,0:T(8,128)} %bitcast.15, f32[1024,128]{1,0:T(8,128)} %to_grid.1.after_any), custom_call_target="tpu_custom_call" | custom-call | bytes 1048576 | tf_op jit(solution)/shard_map/turn/pallas_call | solution.py:293
  23.0 3.3 %collective-permute-start = (f32[256,128]{1,0:T(8,128)}, f32[256,128]{1,0:T(8,128)S(1)}, u32[]{:S(2)}, u32[]{:S(2)}) collective-permute-start(f32[256,128]{1,0:T(8,128)} %turn.1.b_any), channel_id=1, source_target_pairs={{0,4},{4,8},{8,12},{12,16},{16,20},{20,24},{24,28},{28,32},{32,36}... | collective-permute-start | bytes 393224 | tf_op jit(solution)/shard_map/ppermute | solution.py:308
  26.2 1.3 %collective-permute-start.1 = (f32[256,128]{1,0:T(8,128)}, f32[256,128]{1,0:T(8,128)S(1)}, u32[]{:S(2)}, u32[]{:S(2)}) collective-permute-start(f32[256,128]{1,0:T(8,128)} %turn.1.b_any), channel_id=1, source_target_pairs={{4,0},{8,4},{12,8},{16,12},{20,16},{24,20},{28,24},{32,28},{36,32}... | collective-permute-start | bytes 393224 | tf_op jit(solution)/shard_map/ppermute | solution.py:308
  27.5 3.3 %near_tables.1 = (bf16[27,128,128]{2,1,0:T(8,128)(2,1)}, bf16[27,128,128]{2,1,0:T(8,128)(2,1)}) custom-call(f32[27,2,64,64]{3,2,1,0:T(8,128)} %table_ref.1, f32[1024,128]{1,0:T(8,128)} %to_grid.1.after_any), custom_call_target="tpu_custom_call" | custom-call | bytes 4194304 | tf_op jit(solution)/shard_map/near_tables/pallas_call | solution.py:293
  30.8 0.0 collective-permute-done.a_any
  30.8 3.9 %collective-permute-done.1.c_any = f32[256,128]{1,0:T(8,128)S(1)} collective-permute-done((f32[256,128]{1,0:T(8,128)}, f32[256,128]{1,0:T(8,128)S(1)}, u32[]{:S(2)}, u32[]{:S(2)}) %collective-permute-start.1) | collective-permute-done | bytes 131104 | tf_op jit(solution)/shard_map/ppermute | solution.py:308
  34.7 0.7 copy-done.8
  35.4 13.0 %join.1.own_any = f32[768,128]{1,0:T(8,128)} custom-call(f32[256,128]{1,0:T(8,128)} %copy-done.7, f32[256,128]{1,0:T(8,128)} %turn.1.b_any, f32[256,128]{1,0:T(8,128)} %copy-done.8), custom_call_target="tpu_custom_call" | custom-call | bytes 2097152 | tf_op jit(solution)/shard_map/join/pallas_call | solution.py:293
  48.4 3.9 %collective-permute-start.2 = (f32[768,128]{1,0:T(8,128)}, f32[768,128]{1,0:T(8,128)S(1)}, u32[]{:S(2)}, u32[]{:S(2)}) collective-permute-start(f32[768,128]{1,0:T(8,128)} %join.1.own_any), channel_id=1, source_target_pairs={{0,1},{1,2},{2,3},{4,5},{5,6},{6,7},{8,9},{9,10},{10,11},{12,13},{... | collective-permute-start | bytes 1179656 | tf_op jit(solution)/shard_map/ppermute | solution.py:308
  52.3 1.9 %collective-permute-start.3 = (f32[768,128]{1,0:T(8,128)}, f32[768,128]{1,0:T(8,128)}, u32[]{:S(2)}, u32[]{:S(2)}) collective-permute-start(f32[768,128]{1,0:T(8,128)} %join.1.own_any), channel_id=1, source_target_pairs={{1,0},{2,1},{3,2},{5,4},{6,5},{7,6},{9,8},{10,9},{11,10},{13,12},{... | collective-permute-start | bytes 1179656 | tf_op jit(solution)/shard_map/ppermute | solution.py:308
  54.3 0.8 copy-done.6
  55.1 6.7 %convolve.1 = f32[1024,128]{1,0:T(8,128)} custom-call(f32[1024,128]{1,0:T(8,128)} %bitcast.12, f32[2,512,512]{2,1,0:T(8,128)} %bitcast.16, bf16[2,256,512]{2,1,0:T(8,128)(2,1)} %constant.69.clone.yh_any, bf16[2,256,512]{2,1,0:T(8,128)(2,1)} %constant.70.clone.yl_any, bf16[2,512,256]{2,1,0:T(8,128)(2,1)} %constant.71.clone.xh_any, ...), custom_call_target="tpu_custom_call" | custom-call | flops 5000000000 | bytes 9437184 | tf_op jit(solution)/shard_map/convolve/pallas_call | solution.py:293
  61.8 18.2 %all-to-all-start.1 = ((f32[256,4,128]{2,1,0:T(4,128)}), f32[256,4,128]{2,1,0:T(4,128)S(1)}, u32[]{:S(2)}, u32[]{:S(2)}) async-start(f32[256,4,128]{2,1,0:T(4,128)} %bitcast.13), calls=%async_computation.1 | async-start | bytes 1048576 | tf_op jit(solution)/shard_map/all_to_all | solution.py:345
  80.1 0.1 fusion.3
  80.2 0.6 reshape.34.index_ref
  80.8 0.7 copy-done.10
  81.5 10.4 %near.1.near_ref = f32[128,256]{1,0:T(8,128)} custom-call(s32[6912]{0:T(1024)} %reshape.34.index_ref, f32[768,128]{1,0:T(8,128)} %copy-done.10, f32[768,128]{1,0:T(8,128)} %join.1.own_any, f32[768,128]{1,0:T(8,128)} %collective-permute-done.3.right_any, bf16[27,128,128]{2,1,0:T(8,128)(2,1)} %get-tuple-element.7.after_any.high_any, ...), custom_call_target="tpu_custom_call" | custom-call | flops 10000000000 | bytes 41943040 | tf_op jit(solution)/shard_map/near/pallas_call | solution.py:293
  91.9 9.4 %all-to-all-done.1 = f32[256,4,128]{2,1,0:T(4,128)S(1)} async-done(((f32[256,4,128]{2,1,0:T(4,128)}), f32[256,4,128]{2,1,0:T(4,128)S(1)}, u32[]{:S(2)}, u32[]{:S(2)}) %all-to-all-start.1) | async-done | bytes 524320 | tf_op jit(solution)/shard_map/all_to_all | solution.py:345
  101.3 0.0 copy-start.2
  101.3 1.0 copy-done.2
  102.4 0.9 copy-done.5
  103.3 2.8 %from_grid.1 = f32[128,256]{1,0:T(8,128)} custom-call(s32[1]{0:T(128)S(6)} %copy.19.count_ref, s32[1,256]{1,0:T(1,128)S(1)} %bitcast.10, f32[1024,128]{1,0:T(8,128)S(1)} %bitcast.8, f32[64,64]{1,0:T(8,128)S(1)} %copy-done, bf16[128,2048]{1,0:T(8,128)(2,1)S(1)} %copy-done.2, bf16[128,512]{1,0:T(8,128)(2,1)S(1)} %copy-done.3, bf16[128,512]{1,0:T(8,128)(2,1)S(1)} %copy-done.4, ...), custom_call_target="tpu_custom_call" | custom-call | flops 2000000000 | bytes 2097152 | tf_op jit(solution)/shard_map/from_grid/pallas_call | solution.py:293
  (19 shorter events, 0.0 us)
Async XLA Ops:
  5.6 48.7 %all-to-all-start = ((f32[256,4,128]{2,1,0:T(4,128)}), f32[256,4,128]{2,1,0:T(4,128)S(1)}, u32[]{:S(2)}, u32[]{:S(2)}) async-start(f32[256,4,128]{2,1,0:T(4,128)} %bitcast.11), calls=%async_computation | async-start | bytes 1048576 | tf_op jit(solution)/shard_map/all_to_all | solution.py:329
  23.0 7.9 %collective-permute-start = (f32[256,128]{1,0:T(8,128)}, f32[256,128]{1,0:T(8,128)S(1)}, u32[]{:S(2)}, u32[]{:S(2)}) collective-permute-start(f32[256,128]{1,0:T(8,128)} %turn.1.b_any), channel_id=1, source_target_pairs={{0,4},{4,8},{8,12},{12,16},{16,20},{20,24},{24,28},{28,32},{32,36}... | collective-permute-start | bytes 393224 | tf_op jit(solution)/shard_map/ppermute | solution.py:308
  26.2 8.5 %collective-permute-start.1 = (f32[256,128]{1,0:T(8,128)}, f32[256,128]{1,0:T(8,128)S(1)}, u32[]{:S(2)}, u32[]{:S(2)}) collective-permute-start(f32[256,128]{1,0:T(8,128)} %turn.1.b_any), channel_id=1, source_target_pairs={{4,0},{8,4},{12,8},{16,12},{20,16},{24,20},{28,24},{32,28},{36,32}... | collective-permute-start | bytes 393224 | tf_op jit(solution)/shard_map/ppermute | solution.py:308
  30.8 3.9 %copy-start.7 = (f32[256,128]{1,0:T(8,128)}, f32[256,128]{1,0:T(8,128)S(1)}, u32[]{:S(2)}) copy-start(f32[256,128]{1,0:T(8,128)S(1)} %collective-permute-done.a_any) | copy-start | bytes 393220
  34.7 0.7 copy-start.8
  48.4 32.3 %collective-permute-start.2 = (f32[768,128]{1,0:T(8,128)}, f32[768,128]{1,0:T(8,128)S(1)}, u32[]{:S(2)}, u32[]{:S(2)}) collective-permute-start(f32[768,128]{1,0:T(8,128)} %join.1.own_any), channel_id=1, source_target_pairs={{0,1},{1,2},{2,3},{4,5},{5,6},{6,7},{8,9},{9,10},{10,11},{12,13},{... | collective-permute-start | bytes 1179656 | tf_op jit(solution)/shard_map/ppermute | solution.py:308
  52.3 28.4 %collective-permute-start.3 = (f32[768,128]{1,0:T(8,128)}, f32[768,128]{1,0:T(8,128)}, u32[]{:S(2)}, u32[]{:S(2)}) collective-permute-start(f32[768,128]{1,0:T(8,128)} %join.1.own_any), channel_id=1, source_target_pairs={{1,0},{2,1},{3,2},{5,4},{6,5},{7,6},{9,8},{10,9},{11,10},{13,12},{... | collective-permute-start | bytes 1179656 | tf_op jit(solution)/shard_map/ppermute | solution.py:308
  54.3 0.8 copy-start.6
  55.1 25.0 %copy-start.9 = (s32[27,256]{1,0:T(8,128)S(1)}, s32[27,256]{1,0:T(8,128)}, u32[]{:S(2)}) copy-start(s32[27,256]{1,0:T(8,128)} %param.24) | copy-start | bytes 82948
  61.8 39.5 %all-to-all-start.1 = ((f32[256,4,128]{2,1,0:T(4,128)}), f32[256,4,128]{2,1,0:T(4,128)S(1)}, u32[]{:S(2)}, u32[]{:S(2)}) async-start(f32[256,4,128]{2,1,0:T(4,128)} %bitcast.13), calls=%async_computation.1 | async-start | bytes 1048576 | tf_op jit(solution)/shard_map/all_to_all | solution.py:345
  80.8 0.7 copy-start.10
  81.5 19.8 %copy-start = (f32[64,64]{1,0:T(8,128)S(1)}, f32[64,64]{1,0:T(8,128)}, u32[]{:S(2)}) copy-start(f32[64,64]{1,0:T(8,128)} %proj_ref.1) | copy-start | bytes 49156
  81.5 19.8 %copy-start.1 = (s32[256]{0:T(256)S(1)}, s32[256]{0:T(256)}, u32[]{:S(2)}) copy-start(s32[256]{0:T(256)} %param.22) | copy-start | bytes 3076
  81.5 19.8 %copy-start.3 = (bf16[128,512]{1,0:T(8,128)(2,1)S(1)}, bf16[128,512]{1,0:T(8,128)(2,1)}, u32[]{:S(2)}) copy-start(bf16[128,512]{1,0:T(8,128)(2,1)} %constant.75.clone.fh_ref) | copy-start | bytes 393220
  81.5 19.8 %copy-start.4 = (bf16[128,512]{1,0:T(8,128)(2,1)S(1)}, bf16[128,512]{1,0:T(8,128)(2,1)}, u32[]{:S(2)}) copy-start(bf16[128,512]{1,0:T(8,128)(2,1)} %constant.76.clone.fl_ref) | copy-start | bytes 393220
  101.3 1.0 copy-start.2
  102.4 0.9 copy-start.5

commit v2 on v1

--- a/solution.py
+++ b/solution.py
@@ -142,13 +142,12 @@
     out_ref[...] = jnp.where(slots < count_ref[0], charges_ref[...], 0.0).T
 
 
-def join(a_any, b_any, c_any, out_any, sems):
-    copies = fetch([(r, out_any.at[pl.ds(256 * i, 256), :]) for i, r in enumerate((a_any, b_any, c_any))], sems)
-    for copy in copies:
-        copy.wait()
-
-
-def convolve(in_any, green_any, yh_any, yl_any, xh_any, xl_any, ih_any, il_any, after_any, out_ref,
+def join(a_ref, b_ref, c_ref, out_ref):
+    for i, ref in enumerate((a_ref, b_ref, c_ref)):
+        out_ref[256 * i : 256 * i + 256, :] = ref[...]
+
+
+def convolve(in_any, green_any, yh_any, yl_any, xh_any, xl_any, ih_any, il_any, out_ref,
              in_ref, green_ref, yh, yl, xh, xl, ih, il, ah, al, sh, sl, qh, ql, bh, bl, sems):
     (arrived,) = fetch([(in_any, in_ref)], sems)
     copies = fetch(
@@ -254,19 +253,9 @@
 CLASSES = 27
 
 
-def near_tables(table_ref, after_any, high_ref, low_ref):
-    for k in range(CLASSES):
-        re, im = table_ref[k, 0], table_ref[k, 1]
-        for r, (a, b) in enumerate(((re, -im), (im, re))):
-            rows = slice(64 * r, 64 * r + 64)
-            high_ref[k, rows, :], low_ref[k, rows, :] = split(jnp.concatenate([a, b], axis=1))
-
-
-def near(index_ref, left_any, own_any, right_any, high_any, low_any, out_ref, source_ref, picked, high_ref, low_ref, sems):
-    sources = [(r, source_ref.at[pl.ds(768 * i, 768), :]) for i, r in enumerate((left_any, own_any, right_any))]
-    copies = fetch(sources + [(high_any, high_ref), (low_any, low_ref)], sems)
-    for copy in copies[:3]:
-        copy.wait()
+def near(index_ref, left_ref, own_ref, right_ref, table_ref, out_ref, source_ref, picked):
+    for i, ref in enumerate((left_ref, own_ref, right_ref)):
+        source_ref[768 * i : 768 * i + 768, :] = ref[...]
 
     def one(k, carry):
         for b in range(256):
@@ -275,12 +264,12 @@
         return carry
 
     lax.fori_loop(0, CLASSES, one, 0)
-    for copy in copies[3:]:
-        copy.wait()
     total = jnp.zeros((256, 128), F32)
     for k in range(CLASSES):
         gh, gl = split(picked[k])
-        th, tl = high_ref[k], low_ref[k]
+        re, im = table_ref[k, 0], table_ref[k, 1]
+        rows = [jnp.concatenate([re, -im], axis=1), jnp.concatenate([im, re], axis=1)]
+        th, tl = split(jnp.concatenate(rows, axis=0))
         total = total + (dot_t(gh, th) + (dot_t(gh, tl) + dot_t(gl, th)))
     out_ref[...] = total.T
 
@@ -327,16 +316,13 @@
         copies=6, flops=2 * 10**9, bytes_accessed=2 << 20, name="to_grid", room=63,
     )
     planes = lax.all_to_all(sent.reshape(256, 4, 128), BOTH, split_axis=0, concat_axis=0, tiled=True)
-    masked = call(turn, shape(256, 128), (block_count, cells, sent), "svh", bytes_accessed=1 << 20, name="turn", room=63)
+    masked = call(turn, shape(256, 128), (block_count, cells, sent), "svh", bytes_accessed=1 << 20, name="turn", room=16)
     before, after = neighbours(masked, "wide", W)
-    own = call(join, shape(768, 128), (before, masked, after), "hhh", copies=3, bytes_accessed=2 << 20, name="join", out_kind="h", room=63)
+    own = call(join, shape(768, 128), (before, masked, after), "vvv", bytes_accessed=2 << 20, name="join", room=16)
     left, right = neighbours(own, "narrow", N)
-    table = jax.ShapeDtypeStruct((CLASSES, 128, 128), BF16)
-    table_high, table_low = call(near_tables, (table, table), (near_table, sent), "vh", bytes_accessed=4 << 20,
-                                  name="near_tables", room=63)
     back = call(
         convolve, shape(1024, 128),
-        (planes.reshape(1024, 128), green_hat.reshape(2, 512, 512), yh, yl, xh, xl, ih, il, table_high), "hhhhhhhhh",
+        (planes.reshape(1024, 128), green_hat.reshape(2, 512, 512), yh, yl, xh, xl, ih, il), "hhhhhhhh",
         scratch=[VMEM((1024, 128), F32), VMEM((2, 512, 512), F32)] + [VMEM((2, 256, 512), BF16)] * 2 + [VMEM((2, 512, 256), BF16)] * 2
         + [VMEM((2, 256, 512), BF16)] * 2 + [VMEM((2, 256, 256), BF16)] * 2 + [VMEM((2, 256, 512), BF16)] * 2
         + [VMEM((2, 512, 512), BF16)] * 2 + [VMEM((2, 256, 512), BF16)] * 2,
@@ -346,9 +332,9 @@
     step_wide, step_narrow, slot = near_source // 768, near_source // 256 % 3, near_source % 256
     index = (step_narrow * 768 + step_wide * 256 + slot).reshape(CLASSES * 256)
     beside = call(
-        near, shape(128, 256), (index, left, own, right, table_high, table_low), "shhhhh",
-        scratch=[VMEM((2304, 128), F32), VMEM((CLASSES, 256, 128), F32)] + [VMEM((CLASSES, 128, 128), BF16)] * 2,
-        copies=5, flops=10**10, bytes_accessed=40 << 20, name="near", room=63,
+        near, shape(128, 256), (index, left, own, right, near_table), "svvvv",
+        scratch=[VMEM((2304, 128), F32), VMEM((CLASSES, 256, 128), F32)],
+        flops=10**10, bytes_accessed=40 << 20, name="near",
     )
     result = call(
         from_grid, shape(128, 256),

time: 107 us -> 91.5 us (0.86)
  Pallas kernels: 42.8 us -> 23.1 us
  waiting for transfers between devices: 13.3 us -> 16.9 us
    pallas_call x7 -> x6, Pallas kernels: 42.8 us -> 23.1 us  [call(): pl.pallas_call(kernel, out_shape=outs, in_specs=[pl.BlockSpec(memory_spac...]
    all_to_all x1, waiting for transfers between devices: 0.01 us -> 3.49 us  [per_device(): lax.all_to_all(sent.reshape(256, 4, 128), BOTH, split_axis=0, concat_axis...]
    all_to_all x1, starting transfers between devices: 18.2 us -> 15.6 us  [per_device(): lax.all_to_all(back.reshape(256, 4, 128), BOTH, split_axis=0, concat_axis...]
    ppermute x4, starting transfers between devices: 10.4 us -> 12.7 us  [neighbours(): return (lax.ppermute(array, axis, up), lax.ppermute(array, axis, down))]
    all_to_all x1, waiting for transfers between devices: 9.4 us -> 10.5 us  [per_device(): lax.all_to_all(back.reshape(256, 4, 128), BOTH, split_axis=0, concat_axis...]
  transfers between devices with their start and end apart: 6 -> 6, of which waited for: 2 -> 4; matrix products, arithmetic and copies ran while one was open for 1% -> 0% of each run, Pallas kernels for 33% -> 17%
where the time goes in v2:
time: 91.5 us; the launch traced here: 91.1 us
  starting transfers between devices  45 us (49%)
  Pallas kernels  23.1 us (25%)
  waiting for transfers between devices  16.9 us (18%)
  local copies, waits for them, and re-layouts  5.16 us (6%)
    pallas_call x6, Pallas kernels, call(): pl.pallas_call(kernel, out_shape=outs, in_specs=[pl.BlockSpec(memory_spac...  23.1 us
    all_to_all x1, starting transfers between devices, per_device(): lax.all_to_all(sent.reshape(256, 4, 128), BOTH, split_axis=0, concat_axis...  16.7 us
    all_to_all x1, starting transfers between devices, per_device(): lax.all_to_all(back.reshape(256, 4, 128), BOTH, split_axis=0, concat_axis...  15.6 us
    ppermute x4, starting transfers between devices, neighbours(): return (lax.ppermute(array, axis, up), lax.ppermute(array, axis, down))  12.7 us
    all_to_all x1, waiting for transfers between devices, per_device(): lax.all_to_all(back.reshape(256, 4, 128), BOTH, split_axis=0, concat_axis...  10.5 us
    unnamed x22, local copies, waits for them, and re-layouts  5.15 us
    all_to_all x1, waiting for transfers between devices, per_device(): lax.all_to_all(sent.reshape(256, 4, 128), BOTH, split_axis=0, concat_axis...  3.49 us
    ppermute x4, waiting for transfers between devices, neighbours(): return (lax.ppermute(array, axis, up), lax.ppermute(array, axis, down))  2.86 us
  transfers between devices with their start and end apart: 6, of which 4 were waited for; matrix products, arithmetic and copies ran while one was open for 0% of the time, Pallas kernels for 17%

profile of v2, /device:TPU:1, one launch (start us, length us, event | category | flops | bytes accessed | tf_op | source)
XLA Modules:
  0.0 91.1 jit_solution(12937106292607784853)
XLA Ops:
  0.7 5.0 %to_grid.1.after_any = f32[1024,128]{1,0:T(8,128)} custom-call(s32[1]{0:T(128)S(6)} %copy.19.count_ref, f32[128,256]{1,0:T(8,128)} %bitcast.10, s32[1,256]{1,0:T(1,128)} %bitcast.12, f32[64,64]{1,0:T(8,128)} %proj_ref.1, bf16[128,2048]{1,0:T(8,128)(2,1)} %constant.66.clone.expand_any.expand_ref, bf16[256,256]{1,0:T(8,128)(2,1)} %constant.67.clone.fh_any, ...), custom_call_target="tpu_custom_call" | custom-call | flops 2000000000 | bytes 2097152 | tf_op jit(solution)/shard_map/to_grid/pallas_call | solution.py:282
  5.7 16.7 %all-to-all-start = ((f32[256,4,128]{2,1,0:T(4,128)}), f32[256,4,128]{2,1,0:T(4,128)}, u32[]{:S(2)}, u32[]{:S(2)}) async-start(f32[256,4,128]{2,1,0:T(4,128)} %bitcast.8), calls=%async_computation | async-start | bytes 1048576 | tf_op jit(solution)/shard_map/all_to_all | solution.py:318
  22.4 1.1 %copy-done = f32[1024,128]{1,0:T(8,128)S(1)} copy-done((f32[1024,128]{1,0:T(8,128)S(1)}, f32[1024,128]{1,0:T(8,128)}, u32[]{:S(2)}) %copy-start) | copy-done | bytes 524312
  23.4 0.1 turn.1.b_ref
  23.6 1.3 %collective-permute-start.1 = (f32[256,128]{1,0:T(8,128)S(1)}, f32[256,128]{1,0:T(8,128)S(1)}, u32[]{:S(2)}, u32[]{:S(2)}) collective-permute-start(f32[256,128]{1,0:T(8,128)S(1)} %turn.1.b_ref), channel_id=1, source_target_pairs={{4,0},{8,4},{12,8},{16,12},{20,16},{24,20},{28,24},{32,28},{36,32}... | collective-permute-start | bytes 393224 | tf_op jit(solution)/shard_map/ppermute | solution.py:297
  24.9 4.0 %collective-permute-start = (f32[256,128]{1,0:T(8,128)S(1)}, f32[256,128]{1,0:T(8,128)S(1)}, u32[]{:S(2)}, u32[]{:S(2)}) collective-permute-start(f32[256,128]{1,0:T(8,128)S(1)} %turn.1.b_ref), channel_id=1, source_target_pairs={{0,4},{4,8},{8,12},{12,16},{16,20},{20,24},{24,28},{28,32},{32,36}... | collective-permute-start | bytes 393224 | tf_op jit(solution)/shard_map/ppermute | solution.py:297
  28.9 1.9 %collective-permute-done.1.c_ref = f32[256,128]{1,0:T(8,128)S(1)} collective-permute-done((f32[256,128]{1,0:T(8,128)S(1)}, f32[256,128]{1,0:T(8,128)S(1)}, u32[]{:S(2)}, u32[]{:S(2)}) %collective-permute-start.1) | collective-permute-done | bytes 131104 | tf_op jit(solution)/shard_map/ppermute | solution.py:297
  30.7 1.0 %collective-permute-done.a_ref = f32[256,128]{1,0:T(8,128)S(1)} collective-permute-done((f32[256,128]{1,0:T(8,128)S(1)}, f32[256,128]{1,0:T(8,128)S(1)}, u32[]{:S(2)}, u32[]{:S(2)}) %collective-permute-start) | collective-permute-done | bytes 131104 | tf_op jit(solution)/shard_map/ppermute | solution.py:297
  31.7 4.8 %collective-permute-start.3 = (f32[768,128]{1,0:T(8,128)S(1)}, f32[768,128]{1,0:T(8,128)S(1)}, u32[]{:S(2)}, u32[]{:S(2)}) collective-permute-start(f32[768,128]{1,0:T(8,128)S(1)} %join.1.own_ref), channel_id=1, source_target_pairs={{1,0},{2,1},{3,2},{5,4},{6,5},{7,6},{9,8},{10,9},{11,10},{13,12},{... | collective-permute-start | bytes 1179656 | tf_op jit(solution)/shard_map/ppermute | solution.py:297
  36.5 2.7 %collective-permute-start.2 = (f32[768,128]{1,0:T(8,128)S(1)}, f32[768,128]{1,0:T(8,128)}, u32[]{:S(2)}, u32[]{:S(2)}) collective-permute-start(f32[768,128]{1,0:T(8,128)S(1)} %join.1.own_ref), channel_id=1, source_target_pairs={{0,1},{1,2},{2,3},{4,5},{5,6},{6,7},{8,9},{9,10},{10,11},{12,13},{... | collective-permute-start | bytes 1179656 | tf_op jit(solution)/shard_map/ppermute | solution.py:297
  39.2 3.5 %all-to-all-done = f32[256,4,128]{2,1,0:T(4,128)} async-done(((f32[256,4,128]{2,1,0:T(4,128)}), f32[256,4,128]{2,1,0:T(4,128)}, u32[]{:S(2)}, u32[]{:S(2)}) %all-to-all-start) | async-done | bytes 524320 | tf_op jit(solution)/shard_map/all_to_all | solution.py:318
  42.7 6.7 %convolve.1 = f32[1024,128]{1,0:T(8,128)} custom-call(f32[1024,128]{1,0:T(8,128)} %bitcast.3.in_any, f32[2,512,512]{2,1,0:T(8,128)} %bitcast.15, bf16[2,256,512]{2,1,0:T(8,128)(2,1)} %constant.69.clone.yh_any, bf16[2,256,512]{2,1,0:T(8,128)(2,1)} %constant.70.clone.yl_any, bf16[2,512,256]{2,1,0:T(8,128)(2,1)} %constant.71.clone.xh_any, ...), custom_call_target="tpu_custom_call" | custom-call | flops 5000000000 | bytes 9437184 | tf_op jit(solution)/shard_map/convolve/pallas_call | solution.py:282
  49.4 15.6 %all-to-all-start.1 = ((f32[256,4,128]{2,1,0:T(4,128)}), f32[256,4,128]{2,1,0:T(4,128)S(1)}, u32[]{:S(2)}, u32[]{:S(2)}) async-start(f32[256,4,128]{2,1,0:T(4,128)} %bitcast.14), calls=%async_computation.1 | async-start | bytes 1048576 | tf_op jit(solution)/shard_map/all_to_all | solution.py:331
  65.0 0.1 fusion.3
  65.1 0.0 copy-start.3
  65.1 0.0 copy-start.4
  65.2 1.5 %copy-done.2 = f32[27,2,64,64]{3,2,1,0:T(8,128)S(1)} copy-done((f32[27,2,64,64]{3,2,1,0:T(8,128)S(1)}, f32[27,2,64,64]{3,2,1,0:T(8,128)}, u32[]{:S(2)}) %copy-start.2) | copy-done | bytes 884760
  66.7 8.4 %near.1.near_ref = f32[128,256]{1,0:T(8,128)S(1)} custom-call(s32[6912]{0:T(1024)S(1)} %reshape.34.index_ref, f32[768,128]{1,0:T(8,128)} %collective-permute-done.2.left_ref, f32[768,128]{1,0:T(8,128)S(1)} %join.1.own_ref, f32[768,128]{1,0:T(8,128)S(1)} %collective-permute-done.3.right_ref, f32[27,2,64,64]{3,2,1,0:T(8,128)S(1)} %copy-done.2), custom_call_target="tpu_custom_call" | custom-call | flops 10000000000 | bytes 41943040 | tf_op jit(solution)/shard_map/near/pallas_call | solution.py:282
  75.1 0.6 copy-done.8
  75.7 10.5 %all-to-all-done.1 = f32[256,4,128]{2,1,0:T(4,128)S(1)} async-done(((f32[256,4,128]{2,1,0:T(4,128)}), f32[256,4,128]{2,1,0:T(4,128)S(1)}, u32[]{:S(2)}, u32[]{:S(2)}) %all-to-all-start.1) | async-done | bytes 524320 | tf_op jit(solution)/shard_map/all_to_all | solution.py:331
  86.3 0.0 copy-start.5
  86.3 1.0 %copy-done.5 = bf16[128,2048]{1,0:T(8,128)(2,1)S(1)} copy-done((bf16[128,2048]{1,0:T(8,128)(2,1)S(1)}, bf16[128,2048]{1,0:T(8,128)(2,1)}, u32[]{:S(2)}) %copy-start.5) | copy-done | bytes 524312
  87.3 0.9 copy-done.9
  88.2 2.8 %from_grid.1 = f32[128,256]{1,0:T(8,128)} custom-call(s32[1]{0:T(128)S(6)} %copy.19.count_ref, s32[1,256]{1,0:T(1,128)S(1)} %bitcast.13, f32[1024,128]{1,0:T(8,128)S(1)} %bitcast.9, f32[64,64]{1,0:T(8,128)S(1)} %copy-done.3, bf16[128,2048]{1,0:T(8,128)(2,1)S(1)} %copy-done.5, bf16[128,512]{1,0:T(8,128)(2,1)S(1)} %copy-done.7, ...), custom_call_target="tpu_custom_call" | custom-call | flops 2000000000 | bytes 2097152 | tf_op jit(solution)/shard_map/from_grid/pallas_call | solution.py:282
  (18 shorter events, 0.1 us)
Async XLA Ops:
  0.7 21.7 %copy-start.1 = (f32[2,64,256]{2,1,0:T(8,128)S(1)}, f32[2,64,256]{2,1,0:T(8,128)}, u32[]{:S(2)}) copy-start(f32[2,64,256]{2,1,0:T(8,128)} %param.18) | copy-start | bytes 393220
  5.7 37.0 %all-to-all-start = ((f32[256,4,128]{2,1,0:T(4,128)}), f32[256,4,128]{2,1,0:T(4,128)}, u32[]{:S(2)}, u32[]{:S(2)}) async-start(f32[256,4,128]{2,1,0:T(4,128)} %bitcast.8), calls=%async_computation | async-start | bytes 1048576 | tf_op jit(solution)/shard_map/all_to_all | solution.py:318
  22.4 1.1 %copy-start = (f32[1024,128]{1,0:T(8,128)S(1)}, f32[1024,128]{1,0:T(8,128)}, u32[]{:S(2)}) copy-start(f32[1024,128]{1,0:T(8,128)} %to_grid.1.after_any) | copy-start | bytes 1572868
  23.6 7.2 %collective-permute-start.1 = (f32[256,128]{1,0:T(8,128)S(1)}, f32[256,128]{1,0:T(8,128)S(1)}, u32[]{:S(2)}, u32[]{:S(2)}) collective-permute-start(f32[256,128]{1,0:T(8,128)S(1)} %turn.1.b_ref), channel_id=1, source_target_pairs={{4,0},{8,4},{12,8},{16,12},{20,16},{24,20},{28,24},{32,28},{36,32}... | collective-permute-start | bytes 393224 | tf_op jit(solution)/shard_map/ppermute | solution.py:297
  24.9 6.9 %collective-permute-start = (f32[256,128]{1,0:T(8,128)S(1)}, f32[256,128]{1,0:T(8,128)S(1)}, u32[]{:S(2)}, u32[]{:S(2)}) collective-permute-start(f32[256,128]{1,0:T(8,128)S(1)} %turn.1.b_ref), channel_id=1, source_target_pairs={{0,4},{4,8},{8,12},{12,16},{16,20},{20,24},{24,28},{28,32},{32,36}... | collective-permute-start | bytes 393224 | tf_op jit(solution)/shard_map/ppermute | solution.py:297
  31.7 33.4 %collective-permute-start.3 = (f32[768,128]{1,0:T(8,128)S(1)}, f32[768,128]{1,0:T(8,128)S(1)}, u32[]{:S(2)}, u32[]{:S(2)}) collective-permute-start(f32[768,128]{1,0:T(8,128)S(1)} %join.1.own_ref), channel_id=1, source_target_pairs={{1,0},{2,1},{3,2},{5,4},{6,5},{7,6},{9,8},{10,9},{11,10},{13,12},{... | collective-permute-start | bytes 1179656 | tf_op jit(solution)/shard_map/ppermute | solution.py:297
  36.5 28.7 %collective-permute-start.2 = (f32[768,128]{1,0:T(8,128)S(1)}, f32[768,128]{1,0:T(8,128)}, u32[]{:S(2)}, u32[]{:S(2)}) collective-permute-start(f32[768,128]{1,0:T(8,128)S(1)} %join.1.own_ref), channel_id=1, source_target_pairs={{0,1},{1,2},{2,3},{4,5},{5,6},{6,7},{8,9},{9,10},{10,11},{12,13},{... | collective-permute-start | bytes 1179656 | tf_op jit(solution)/shard_map/ppermute | solution.py:297
  42.7 22.3 %copy-start.10 = (s32[27,256]{1,0:T(8,128)S(1)}, s32[27,256]{1,0:T(8,128)}, u32[]{:S(2)}) copy-start(s32[27,256]{1,0:T(8,128)} %param.24) | copy-start | bytes 82948
  49.4 36.8 %all-to-all-start.1 = ((f32[256,4,128]{2,1,0:T(4,128)}), f32[256,4,128]{2,1,0:T(4,128)S(1)}, u32[]{:S(2)}, u32[]{:S(2)}) async-start(f32[256,4,128]{2,1,0:T(4,128)} %bitcast.14), calls=%async_computation.1 | async-start | bytes 1048576 | tf_op jit(solution)/shard_map/all_to_all | solution.py:331
  65.1 21.1 %copy-start.3 = (f32[64,64]{1,0:T(8,128)S(1)}, f32[64,64]{1,0:T(8,128)}, u32[]{:S(2)}) copy-start(f32[64,64]{1,0:T(8,128)} %proj_ref.1) | copy-start | bytes 49156
  65.1 21.1 %copy-start.4 = (s32[256]{0:T(256)S(1)}, s32[256]{0:T(256)}, u32[]{:S(2)}) copy-start(s32[256]{0:T(256)} %param.22) | copy-start | bytes 3076
  65.2 1.5 %copy-start.2 = (f32[27,2,64,64]{3,2,1,0:T(8,128)S(1)}, f32[27,2,64,64]{3,2,1,0:T(8,128)}, u32[]{:S(2)}) copy-start(f32[27,2,64,64]{3,2,1,0:T(8,128)} %table_ref.1) | copy-start | bytes 2654212
  66.7 19.6 %copy-start.6 = (bf16[128,512]{1,0:T(8,128)(2,1)S(1)}, bf16[128,512]{1,0:T(8,128)(2,1)}, u32[]{:S(2)}) copy-start(bf16[128,512]{1,0:T(8,128)(2,1)} %constant.76.clone.fl_ref) | copy-start | bytes 393220
  66.7 19.6 %copy-start.7 = (bf16[128,512]{1,0:T(8,128)(2,1)S(1)}, bf16[128,512]{1,0:T(8,128)(2,1)}, u32[]{:S(2)}) copy-start(bf16[128,512]{1,0:T(8,128)(2,1)} %constant.75.clone.fh_ref) | copy-start | bytes 393220
  75.1 0.7 copy-start.8
  86.3 1.0 %copy-start.5 = (bf16[128,2048]{1,0:T(8,128)(2,1)S(1)}, bf16[128,2048]{1,0:T(8,128)(2,1)}, u32[]{:S(2)}) copy-start(bf16[128,2048]{1,0:T(8,128)(2,1)} %constant.66.clone.expand_any.expand_ref) | copy-start | bytes 1572868
  87.3 0.9 copy-start.9

commit v3 on v2

--- a/solution.py
+++ b/solution.py
@@ -95,11 +95,12 @@
     return copies
 
 
-def to_grid(count_ref, charges_any, site_any, proj_any, expand_any, fh_any, fl_any, out_ref,
+def to_grid(count_ref, charges_any, site_any, proj_any, expand_any, fh_any, fl_any, out_ref, token_ref,
             charges_ref, site_ref, proj_ref, expand_ref, fh_ref, fl_ref, sems):
     copies = fetch(
         [(charges_any, charges_ref), (proj_any, proj_ref), (site_any, site_ref),
          (expand_any, expand_ref), (fh_any, fh_ref), (fl_any, fl_ref)], sems)
+    token_ref[...] = jnp.zeros((8, 128), F32)
     count = count_ref[0]
     slots = lax.broadcasted_iota(jnp.int32, (128, 256), 1)
     for copy in copies[:3]:
@@ -137,7 +138,7 @@
         out_ref[pl.ds(2 * e + 1, 256, stride=4), :] = planes[:, 128:]
 
 
-def turn(count_ref, charges_ref, after_any, out_ref):
+def turn(count_ref, charges_ref, after_ref, out_ref):
     slots = lax.broadcasted_iota(jnp.int32, (128, 256), 1)
     out_ref[...] = jnp.where(slots < count_ref[0], charges_ref[...], 0.0).T
 
@@ -309,14 +310,14 @@
     shape = lambda *s: jax.ShapeDtypeStruct(s, F32)
 
     cells = charges.reshape(128, 256)
-    sent = call(
-        to_grid, shape(1024, 128), (block_count, cells, site, projection, expand, fzh, fzl), "shhhhhh",
+    sent, token = call(
+        to_grid, (shape(1024, 128), shape(8, 128)), (block_count, cells, site, projection, expand, fzh, fzl), "shhhhhh",
         scratch=[VMEM((128, 256), F32), VMEM((1, 256), jnp.int32), VMEM((64, 64), F32), VMEM((128, 2048), BF16)]
         + [VMEM((256, 256), BF16)] * 2,
         copies=6, flops=2 * 10**9, bytes_accessed=2 << 20, name="to_grid", room=63,
     )
     planes = lax.all_to_all(sent.reshape(256, 4, 128), BOTH, split_axis=0, concat_axis=0, tiled=True)
-    masked = call(turn, shape(256, 128), (block_count, cells, sent), "svh", bytes_accessed=1 << 20, name="turn", room=16)
+    masked = call(turn, shape(256, 128), (block_count, cells, token), "svv", bytes_accessed=1 << 20, name="turn", room=16)
     before, after = neighbours(masked, "wide", W)
     own = call(join, shape(768, 128), (before, masked, after), "vvv", bytes_accessed=2 << 20, name="join", room=16)
     left, right = neighbours(own, "narrow", N)
@@ -328,18 +329,19 @@
         + [VMEM((2, 512, 512), BF16)] * 2 + [VMEM((2, 256, 512), BF16)] * 2,
         copies=8, flops=5 * 10**9, bytes_accessed=9 << 20, name="convolve", room=63,
     )
+    back, left, right = lax.optimization_barrier((back, left, right))
     field = lax.all_to_all(back.reshape(256, 4, 128), BOTH, split_axis=0, concat_axis=0, tiled=True)
     step_wide, step_narrow, slot = near_source // 768, near_source // 256 % 3, near_source % 256
     index = (step_narrow * 768 + step_wide * 256 + slot).reshape(CLASSES * 256)
     beside = call(
         near, shape(128, 256), (index, left, own, right, near_table), "svvvv",
         scratch=[VMEM((2304, 128), F32), VMEM((CLASSES, 256, 128), F32)],
-        flops=10**10, bytes_accessed=40 << 20, name="near",
+        flops=10**10, bytes_accessed=40 << 20, name="near", room=16,
     )
     result = call(
         from_grid, shape(128, 256),
         (block_count, site, field.reshape(1024, 128), projection, expand, izh, izl, beside), "svvvvvvv",
-        flops=2 * 10**9, bytes_accessed=2 << 20, name="from_grid", room=16,
+        flops=2 * 10**9, bytes_accessed=2 << 20, name="from_grid", room=12,
     )
     return result.reshape(2, 64, 256)
 

time: 91.5 us -> 89.2 us (0.975)
  local copies, waits for them, and re-layouts: 5.16 us -> 2.19 us
  waiting for transfers between devices: 16.9 us -> 17.9 us
    unnamed x22 -> x18, local copies, waits for them, and re-layouts: 5.15 us -> 2.18 us
where the time goes in v3:
time: 89.2 us; the launch traced here: 88.8 us
  starting transfers between devices  44.7 us (50%)
  Pallas kernels  23.1 us (26%)
  waiting for transfers between devices  17.9 us (20%)
  local copies, waits for them, and re-layouts  2.19 us (2%)
    pallas_call x6, Pallas kernels, call(): pl.pallas_call(kernel, out_shape=outs, in_specs=[pl.BlockSpec(memory_spac...  23.1 us
    all_to_all x1, starting transfers between devices, per_device(): lax.all_to_all(sent.reshape(256, 4, 128), BOTH, split_axis=0, concat_axis...  16.7 us
    all_to_all x1, starting transfers between devices, per_device(): lax.all_to_all(back.reshape(256, 4, 128), BOTH, split_axis=0, concat_axis...  15.2 us
    ppermute x4, starting transfers between devices, neighbours(): return (lax.ppermute(array, axis, up), lax.ppermute(array, axis, down))  12.8 us
    all_to_all x1, waiting for transfers between devices, per_device(): lax.all_to_all(back.reshape(256, 4, 128), BOTH, split_axis=0, concat_axis...  11.2 us
    all_to_all x1, waiting for transfers between devices, per_device(): lax.all_to_all(sent.reshape(256, 4, 128), BOTH, split_axis=0, concat_axis...  3.86 us
    ppermute x4, waiting for transfers between devices, neighbours(): return (lax.ppermute(array, axis, up), lax.ppermute(array, axis, down))  2.81 us
    unnamed x18, local copies, waits for them, and re-layouts  2.18 us
  transfers between devices with their start and end apart: 6, of which 4 were waited for; matrix products, arithmetic and copies ran while one was open for 0% of the time, Pallas kernels for 17%

profile of v3, /device:TPU:1, one launch (start us, length us, event | category | flops | bytes accessed | tf_op | source)
XLA Modules:
  0.0 88.8 jit_solution(17596570080564732549)
XLA Ops:
  0.7 5.0 %to_grid.1 = (f32[1024,128]{1,0:T(8,128)}, f32[8,128]{1,0:T(8,128)}) custom-call(s32[1]{0:T(128)S(6)} %copy.19.count_ref, f32[128,256]{1,0:T(8,128)} %bitcast.9, s32[1,256]{1,0:T(1,128)} %bitcast.11, f32[64,64]{1,0:T(8,128)} %proj_ref.1, bf16[128,2048]{1,0:T(8,128)(2,1)} %constant.66.clone.expand_any.expand_ref, bf16[256,256]{1,0:T(8,128)(2,1)} %constant.67.clone.fh_any, ...), custom_call_target="tpu_custom_call" | custom-call | flops 2000000000 | bytes 2097152 | tf_op jit(solution)/shard_map/to_grid/pallas_call | solution.py:283
  5.7 16.7 %all-to-all-start = ((f32[256,4,128]{2,1,0:T(4,128)}), f32[256,4,128]{2,1,0:T(4,128)}, u32[]{:S(2)}, u32[]{:S(2)}) async-start(f32[256,4,128]{2,1,0:T(4,128)} %bitcast.13), calls=%async_computation | async-start | bytes 1048576 | tf_op jit(solution)/shard_map/all_to_all | solution.py:319
  22.4 0.0 copy-start.1
  22.4 0.7 copy-done.1
  23.1 0.1 turn.1.b_ref
  23.2 1.3 %collective-permute-start.1 = (f32[256,128]{1,0:T(8,128)S(1)}, f32[256,128]{1,0:T(8,128)S(1)}, u32[]{:S(2)}, u32[]{:S(2)}) collective-permute-start(f32[256,128]{1,0:T(8,128)S(1)} %turn.1.b_ref), channel_id=1, source_target_pairs={{4,0},{8,4},{12,8},{16,12},{20,16},{24,20},{28,24},{32,28},{36,32}... | collective-permute-start | bytes 393224 | tf_op jit(solution)/shard_map/ppermute | solution.py:298
  24.5 4.0 %collective-permute-start = (f32[256,128]{1,0:T(8,128)S(1)}, f32[256,128]{1,0:T(8,128)S(1)}, u32[]{:S(2)}, u32[]{:S(2)}) collective-permute-start(f32[256,128]{1,0:T(8,128)S(1)} %turn.1.b_ref), channel_id=1, source_target_pairs={{0,4},{4,8},{8,12},{12,16},{16,20},{20,24},{24,28},{28,32},{32,36}... | collective-permute-start | bytes 393224 | tf_op jit(solution)/shard_map/ppermute | solution.py:298
  28.5 2.0 %collective-permute-done.1.c_ref = f32[256,128]{1,0:T(8,128)S(1)} collective-permute-done((f32[256,128]{1,0:T(8,128)S(1)}, f32[256,128]{1,0:T(8,128)S(1)}, u32[]{:S(2)}, u32[]{:S(2)}) %collective-permute-start.1) | collective-permute-done | bytes 131104 | tf_op jit(solution)/shard_map/ppermute | solution.py:298
  30.5 0.8 collective-permute-done.a_ref
  31.3 4.9 %collective-permute-start.3 = (f32[768,128]{1,0:T(8,128)S(1)}, f32[768,128]{1,0:T(8,128)S(1)}, u32[]{:S(2)}, u32[]{:S(2)}) collective-permute-start(f32[768,128]{1,0:T(8,128)S(1)} %join.1.own_ref), channel_id=1, source_target_pairs={{1,0},{2,1},{3,2},{5,4},{6,5},{7,6},{9,8},{10,9},{11,10},{13,12},{... | collective-permute-start | bytes 1179656 | tf_op jit(solution)/shard_map/ppermute | solution.py:298
  36.2 2.7 %collective-permute-start.2 = (f32[768,128]{1,0:T(8,128)S(1)}, f32[768,128]{1,0:T(8,128)}, u32[]{:S(2)}, u32[]{:S(2)}) collective-permute-start(f32[768,128]{1,0:T(8,128)S(1)} %join.1.own_ref), channel_id=1, source_target_pairs={{0,1},{1,2},{2,3},{4,5},{5,6},{6,7},{8,9},{9,10},{10,11},{12,13},{... | collective-permute-start | bytes 1179656 | tf_op jit(solution)/shard_map/ppermute | solution.py:298
  38.8 3.9 %all-to-all-done = f32[256,4,128]{2,1,0:T(4,128)} async-done(((f32[256,4,128]{2,1,0:T(4,128)}), f32[256,4,128]{2,1,0:T(4,128)}, u32[]{:S(2)}, u32[]{:S(2)}) %all-to-all-start) | async-done | bytes 524320 | tf_op jit(solution)/shard_map/all_to_all | solution.py:319
  42.7 6.7 %convolve.1 = f32[1024,128]{1,0:T(8,128)} custom-call(f32[1024,128]{1,0:T(8,128)} %bitcast.3.in_any, f32[2,512,512]{2,1,0:T(8,128)} %bitcast.15, bf16[2,256,512]{2,1,0:T(8,128)(2,1)} %constant.69.clone.yh_any, bf16[2,256,512]{2,1,0:T(8,128)(2,1)} %constant.70.clone.yl_any, bf16[2,512,256]{2,1,0:T(8,128)(2,1)} %constant.71.clone.xh_any, ...), custom_call_target="tpu_custom_call" | custom-call | flops 5000000000 | bytes 9437184 | tf_op jit(solution)/shard_map/convolve/pallas_call | solution.py:283
  49.4 0.0 collective-permute-done.3.right_ref
  49.4 0.0 collective-permute-done.2.left_ref
  49.5 15.2 %all-to-all-start.1 = ((f32[256,4,128]{2,1,0:T(4,128)}), f32[256,4,128]{2,1,0:T(4,128)S(1)}, u32[]{:S(2)}, u32[]{:S(2)}) async-start(f32[256,4,128]{2,1,0:T(4,128)} %bitcast.14), calls=%async_computation.1 | async-start | bytes 1048576 | tf_op jit(solution)/shard_map/all_to_all | solution.py:333
  64.7 0.1 fusion.3
  64.8 0.0 copy-start.2
  64.8 1.5 %copy-done.2 = f32[27,2,64,64]{3,2,1,0:T(8,128)S(1)} copy-done((f32[27,2,64,64]{3,2,1,0:T(8,128)S(1)}, f32[27,2,64,64]{3,2,1,0:T(8,128)}, u32[]{:S(2)}) %copy-start.2) | copy-done | bytes 884760
  66.3 0.0 copy-start.7
  66.3 8.4 %near.1.near_ref = f32[128,256]{1,0:T(8,128)S(1)} custom-call(s32[6912]{0:T(1024)S(1)} %reshape.34.index_ref, f32[768,128]{1,0:T(8,128)} %collective-permute-done.2.left_ref, f32[768,128]{1,0:T(8,128)S(1)} %join.1.own_ref, f32[768,128]{1,0:T(8,128)S(1)} %collective-permute-done.3.right_ref, f32[27,2,64,64]{3,2,1,0:T(8,128)S(1)} %copy-done.2), custom_call_target="tpu_custom_call" | custom-call | flops 10000000000 | bytes 41943040 | tf_op jit(solution)/shard_map/near/pallas_call | solution.py:283
  74.7 11.2 %all-to-all-done.1 = f32[256,4,128]{2,1,0:T(4,128)S(1)} async-done(((f32[256,4,128]{2,1,0:T(4,128)}), f32[256,4,128]{2,1,0:T(4,128)S(1)}, u32[]{:S(2)}, u32[]{:S(2)}) %all-to-all-start.1) | async-done | bytes 524320 | tf_op jit(solution)/shard_map/all_to_all | solution.py:333
  85.9 0.0 copy-done.5
  85.9 2.8 %from_grid.1 = f32[128,256]{1,0:T(8,128)} custom-call(s32[1]{0:T(128)S(6)} %copy.19.count_ref, s32[1,256]{1,0:T(1,128)S(1)} %bitcast.12, f32[1024,128]{1,0:T(8,128)S(1)} %bitcast.8, f32[64,64]{1,0:T(8,128)S(1)} %copy-done.3, bf16[128,2048]{1,0:T(8,128)(2,1)S(1)} %copy-done.5, bf16[128,512]{1,0:T(8,128)(2,1)S(1)} %copy-done.7, ...), custom_call_target="tpu_custom_call" | custom-call | flops 2000000000 | bytes 2097152 | tf_op jit(solution)/shard_map/from_grid/pallas_call | solution.py:283
  (14 shorter events, 0.1 us)
Async XLA Ops:
  0.7 21.7 %copy-start = (f32[2,64,256]{2,1,0:T(8,128)S(1)}, f32[2,64,256]{2,1,0:T(8,128)}, u32[]{:S(2)}) copy-start(f32[2,64,256]{2,1,0:T(8,128)} %param.18) | copy-start | bytes 393220
  5.7 37.0 %all-to-all-start = ((f32[256,4,128]{2,1,0:T(4,128)}), f32[256,4,128]{2,1,0:T(4,128)}, u32[]{:S(2)}, u32[]{:S(2)}) async-start(f32[256,4,128]{2,1,0:T(4,128)} %bitcast.13), calls=%async_computation | async-start | bytes 1048576 | tf_op jit(solution)/shard_map/all_to_all | solution.py:319
  22.4 0.7 copy-start.1
  23.2 7.3 %collective-permute-start.1 = (f32[256,128]{1,0:T(8,128)S(1)}, f32[256,128]{1,0:T(8,128)S(1)}, u32[]{:S(2)}, u32[]{:S(2)}) collective-permute-start(f32[256,128]{1,0:T(8,128)S(1)} %turn.1.b_ref), channel_id=1, source_target_pairs={{4,0},{8,4},{12,8},{16,12},{20,16},{24,20},{28,24},{32,28},{36,32}... | collective-permute-start | bytes 393224 | tf_op jit(solution)/shard_map/ppermute | solution.py:298
  24.5 6.8 %collective-permute-start = (f32[256,128]{1,0:T(8,128)S(1)}, f32[256,128]{1,0:T(8,128)S(1)}, u32[]{:S(2)}, u32[]{:S(2)}) collective-permute-start(f32[256,128]{1,0:T(8,128)S(1)} %turn.1.b_ref), channel_id=1, source_target_pairs={{0,4},{4,8},{8,12},{12,16},{16,20},{20,24},{24,28},{28,32},{32,36}... | collective-permute-start | bytes 393224 | tf_op jit(solution)/shard_map/ppermute | solution.py:298
  31.3 18.1 %collective-permute-start.3 = (f32[768,128]{1,0:T(8,128)S(1)}, f32[768,128]{1,0:T(8,128)S(1)}, u32[]{:S(2)}, u32[]{:S(2)}) collective-permute-start(f32[768,128]{1,0:T(8,128)S(1)} %join.1.own_ref), channel_id=1, source_target_pairs={{1,0},{2,1},{3,2},{5,4},{6,5},{7,6},{9,8},{10,9},{11,10},{13,12},{... | collective-permute-start | bytes 1179656 | tf_op jit(solution)/shard_map/ppermute | solution.py:298
  36.2 13.3 %collective-permute-start.2 = (f32[768,128]{1,0:T(8,128)S(1)}, f32[768,128]{1,0:T(8,128)}, u32[]{:S(2)}, u32[]{:S(2)}) collective-permute-start(f32[768,128]{1,0:T(8,128)S(1)} %join.1.own_ref), channel_id=1, source_target_pairs={{0,1},{1,2},{2,3},{4,5},{5,6},{6,7},{8,9},{9,10},{10,11},{12,13},{... | collective-permute-start | bytes 1179656 | tf_op jit(solution)/shard_map/ppermute | solution.py:298
  42.7 22.0 %copy-start.8 = (s32[27,256]{1,0:T(8,128)S(1)}, s32[27,256]{1,0:T(8,128)}, u32[]{:S(2)}) copy-start(s32[27,256]{1,0:T(8,128)} %param.24) | copy-start | bytes 82948
  49.5 36.4 %all-to-all-start.1 = ((f32[256,4,128]{2,1,0:T(4,128)}), f32[256,4,128]{2,1,0:T(4,128)S(1)}, u32[]{:S(2)}, u32[]{:S(2)}) async-start(f32[256,4,128]{2,1,0:T(4,128)} %bitcast.14), calls=%async_computation.1 | async-start | bytes 1048576 | tf_op jit(solution)/shard_map/all_to_all | solution.py:333
  64.8 1.5 %copy-start.2 = (f32[27,2,64,64]{3,2,1,0:T(8,128)S(1)}, f32[27,2,64,64]{3,2,1,0:T(8,128)}, u32[]{:S(2)}) copy-start(f32[27,2,64,64]{3,2,1,0:T(8,128)} %table_ref.1) | copy-start | bytes 2654212
  66.3 19.6 %copy-start.3 = (f32[64,64]{1,0:T(8,128)S(1)}, f32[64,64]{1,0:T(8,128)}, u32[]{:S(2)}) copy-start(f32[64,64]{1,0:T(8,128)} %proj_ref.1) | copy-start | bytes 49156
  66.3 19.6 %copy-start.4 = (s32[256]{0:T(256)S(1)}, s32[256]{0:T(256)}, u32[]{:S(2)}) copy-start(s32[256]{0:T(256)} %param.22) | copy-start | bytes 3076
  66.3 19.6 %copy-start.5 = (bf16[128,2048]{1,0:T(8,128)(2,1)S(1)}, bf16[128,2048]{1,0:T(8,128)(2,1)}, u32[]{:S(2)}) copy-start(bf16[128,2048]{1,0:T(8,128)(2,1)} %constant.66.clone.expand_any.expand_ref) | copy-start | bytes 1572868
  66.3 19.6 %copy-start.6 = (bf16[128,512]{1,0:T(8,128)(2,1)S(1)}, bf16[128,512]{1,0:T(8,128)(2,1)}, u32[]{:S(2)}) copy-start(bf16[128,512]{1,0:T(8,128)(2,1)} %constant.76.clone.fl_ref) | copy-start | bytes 393220
  66.3 19.6 %copy-start.7 = (bf16[128,512]{1,0:T(8,128)(2,1)S(1)}, bf16[128,512]{1,0:T(8,128)(2,1)}, u32[]{:S(2)}) copy-start(bf16[128,512]{1,0:T(8,128)(2,1)} %constant.75.clone.fh_ref) | copy-start | bytes 393220

commit v4 on v3

--- a/solution.py
+++ b/solution.py
@@ -318,9 +318,9 @@
     )
     planes = lax.all_to_all(sent.reshape(256, 4, 128), BOTH, split_axis=0, concat_axis=0, tiled=True)
     masked = call(turn, shape(256, 128), (block_count, cells, token), "svv", bytes_accessed=1 << 20, name="turn", room=16)
-    before, after = neighbours(masked, "wide", W)
+    before, after = neighbours(masked, "narrow", N)
     own = call(join, shape(768, 128), (before, masked, after), "vvv", bytes_accessed=2 << 20, name="join", room=16)
-    left, right = neighbours(own, "narrow", N)
+    left, right = neighbours(own, "wide", W)
     back = call(
         convolve, shape(1024, 128),
         (planes.reshape(1024, 128), green_hat.reshape(2, 512, 512), yh, yl, xh, xl, ih, il), "hhhhhhhh",
@@ -329,10 +329,8 @@
         + [VMEM((2, 512, 512), BF16)] * 2 + [VMEM((2, 256, 512), BF16)] * 2,
         copies=8, flops=5 * 10**9, bytes_accessed=9 << 20, name="convolve", room=63,
     )
-    back, left, right = lax.optimization_barrier((back, left, right))
     field = lax.all_to_all(back.reshape(256, 4, 128), BOTH, split_axis=0, concat_axis=0, tiled=True)
-    step_wide, step_narrow, slot = near_source // 768, near_source // 256 % 3, near_source % 256
-    index = (step_narrow * 768 + step_wide * 256 + slot).reshape(CLASSES * 256)
+    index = near_source.reshape(CLASSES * 256)
     beside = call(
         near, shape(128, 256), (index, left, own, right, near_table), "svvvv",
         scratch=[VMEM((2304, 128), F32), VMEM((CLASSES, 256, 128), F32)],

time: 89.2 us -> 88.4 us (level)
  starting transfers between devices: 44.7 us -> 43.2 us
    ppermute x4, waiting for transfers between devices: 2.81 us -> 5.96 us  [neighbours(): return (lax.ppermute(array, axis, up), lax.ppermute(array, axis, down))]
    all_to_all x1, waiting for transfers between devices: 3.86 us -> 1.46 us  [per_device(): lax.all_to_all(sent.reshape(256, 4, 128), BOTH, split_axis=0, concat_axis...]
  transfers between devices with their start and end apart: 6 -> 6, of which waited for: 4 -> 3; matrix products, arithmetic and copies ran while one was open for 0% -> 0% of each run, Pallas kernels for 17% -> 17%
where the time goes in v4:
time: 88.4 us; the launch traced here: 88 us
  starting transfers between devices  43.2 us (49%)
  Pallas kernels  23.1 us (26%)
  waiting for transfers between devices  18.7 us (21%)
  local copies, waits for them, and re-layouts  2.19 us (2%)
    pallas_call x6, Pallas kernels, call(): pl.pallas_call(kernel, out_shape=outs, in_specs=[pl.BlockSpec(memory_spac...  23.1 us
    all_to_all x1, starting transfers between devices, per_device(): lax.all_to_all(sent.reshape(256, 4, 128), BOTH, split_axis=0, concat_axis...  16.7 us
    all_to_all x1, starting transfers between devices, per_device(): lax.all_to_all(back.reshape(256, 4, 128), BOTH, split_axis=0, concat_axis...  14.4 us
    ppermute x4, starting transfers between devices, neighbours(): return (lax.ppermute(array, axis, up), lax.ppermute(array, axis, down))  12.1 us
    all_to_all x1, waiting for transfers between devices, per_device(): lax.all_to_all(back.reshape(256, 4, 128), BOTH, split_axis=0, concat_axis...  11.2 us
    ppermute x4, waiting for transfers between devices, neighbours(): return (lax.ppermute(array, axis, up), lax.ppermute(array, axis, down))  5.96 us
    unnamed x18, local copies, waits for them, and re-layouts  2.19 us
  transfers between devices with their start and end apart: 6, of which 3 were waited for; matrix products, arithmetic and copies ran while one was open for 0% of the time, Pallas kernels for 17%

profile of v4, /device:TPU:1, one launch (start us, length us, event | category | flops | bytes accessed | tf_op | source)
XLA Modules:
  0.0 88.0 jit_solution(10782185201681525620)
XLA Ops:
  0.7 5.0 %to_grid.1 = (f32[1024,128]{1,0:T(8,128)}, f32[8,128]{1,0:T(8,128)}) custom-call(s32[1]{0:T(128)S(6)} %copy.19.count_ref, f32[128,256]{1,0:T(8,128)} %bitcast.9, s32[1,256]{1,0:T(1,128)} %bitcast.11, f32[64,64]{1,0:T(8,128)} %proj_ref.1, bf16[128,2048]{1,0:T(8,128)(2,1)} %constant.22.clone.expand_any.expand_ref, bf16[256,256]{1,0:T(8,128)(2,1)} %constant.23.clone.fh_any, ...), custom_call_target="tpu_custom_call" | custom-call | flops 2000000000 | bytes 2097152 | tf_op jit(solution)/shard_map/to_grid/pallas_call | solution.py:283
  5.7 16.7 %all-to-all-start = ((f32[256,4,128]{2,1,0:T(4,128)}), f32[256,4,128]{2,1,0:T(4,128)}, u32[]{:S(2)}, u32[]{:S(2)}) async-start(f32[256,4,128]{2,1,0:T(4,128)} %bitcast.13), calls=%async_computation | async-start | bytes 1048576 | tf_op jit(solution)/shard_map/all_to_all | solution.py:319
  22.4 0.0 copy-done
  22.4 0.0 copy-start.1
  22.4 0.7 copy-done.1
  23.1 0.1 turn.1.b_ref
  23.2 4.1 %collective-permute-start.1 = (f32[256,128]{1,0:T(8,128)S(1)}, f32[256,128]{1,0:T(8,128)S(1)}, u32[]{:S(2)}, u32[]{:S(2)}) collective-permute-start(f32[256,128]{1,0:T(8,128)S(1)} %turn.1.b_ref), channel_id=1, source_target_pairs={{1,0},{2,1},{3,2},{5,4},{6,5},{7,6},{9,8},{10,9},{11,10},{13,12},{... | collective-permute-start | bytes 393224 | tf_op jit(solution)/shard_map/ppermute | solution.py:298
  27.3 1.9 %collective-permute-start = (f32[256,128]{1,0:T(8,128)S(1)}, f32[256,128]{1,0:T(8,128)S(1)}, u32[]{:S(2)}, u32[]{:S(2)}) collective-permute-start(f32[256,128]{1,0:T(8,128)S(1)} %turn.1.b_ref), channel_id=1, source_target_pairs={{0,1},{1,2},{2,3},{4,5},{5,6},{6,7},{8,9},{9,10},{10,11},{12,13},{... | collective-permute-start | bytes 393224 | tf_op jit(solution)/shard_map/ppermute | solution.py:298
  29.2 6.0 %collective-permute-done.1.c_ref = f32[256,128]{1,0:T(8,128)S(1)} collective-permute-done((f32[256,128]{1,0:T(8,128)S(1)}, f32[256,128]{1,0:T(8,128)S(1)}, u32[]{:S(2)}, u32[]{:S(2)}) %collective-permute-start.1) | collective-permute-done | bytes 131104 | tf_op jit(solution)/shard_map/ppermute | solution.py:298
  35.2 0.0 collective-permute-done.a_ref
  35.2 1.3 %collective-permute-start.3 = (f32[768,128]{1,0:T(8,128)S(1)}, f32[768,128]{1,0:T(8,128)S(1)}, u32[]{:S(2)}, u32[]{:S(2)}) collective-permute-start(f32[768,128]{1,0:T(8,128)S(1)} %join.1.own_ref), channel_id=1, source_target_pairs={{4,0},{8,4},{12,8},{16,12},{20,16},{24,20},{28,24},{32,28},{36,32}... | collective-permute-start | bytes 1179656 | tf_op jit(solution)/shard_map/ppermute | solution.py:298
  36.5 4.8 %collective-permute-start.2 = (f32[768,128]{1,0:T(8,128)S(1)}, f32[768,128]{1,0:T(8,128)}, u32[]{:S(2)}, u32[]{:S(2)}) collective-permute-start(f32[768,128]{1,0:T(8,128)S(1)} %join.1.own_ref), channel_id=1, source_target_pairs={{0,4},{4,8},{8,12},{12,16},{16,20},{20,24},{24,28},{28,32},{32,36}... | collective-permute-start | bytes 1179656 | tf_op jit(solution)/shard_map/ppermute | solution.py:298
  41.3 1.5 %all-to-all-done = f32[256,4,128]{2,1,0:T(4,128)} async-done(((f32[256,4,128]{2,1,0:T(4,128)}), f32[256,4,128]{2,1,0:T(4,128)}, u32[]{:S(2)}, u32[]{:S(2)}) %all-to-all-start) | async-done | bytes 524320 | tf_op jit(solution)/shard_map/all_to_all | solution.py:319
  42.8 6.7 %convolve.1 = f32[1024,128]{1,0:T(8,128)} custom-call(f32[1024,128]{1,0:T(8,128)} %bitcast.3.in_any, f32[2,512,512]{2,1,0:T(8,128)} %bitcast.15, bf16[2,256,512]{2,1,0:T(8,128)(2,1)} %constant.25.clone.yh_any, bf16[2,256,512]{2,1,0:T(8,128)(2,1)} %constant.26.clone.yl_any, bf16[2,512,256]{2,1,0:T(8,128)(2,1)} %constant.27.clone.xh_any, ...), custom_call_target="tpu_custom_call" | custom-call | flops 5000000000 | bytes 9437184 | tf_op jit(solution)/shard_map/convolve/pallas_call | solution.py:283
  49.5 14.4 %all-to-all-start.1 = ((f32[256,4,128]{2,1,0:T(4,128)}), f32[256,4,128]{2,1,0:T(4,128)S(1)}, u32[]{:S(2)}, u32[]{:S(2)}) async-start(f32[256,4,128]{2,1,0:T(4,128)} %bitcast.14), calls=%async_computation.1 | async-start | bytes 1048576 | tf_op jit(solution)/shard_map/all_to_all | solution.py:332
  63.9 0.0 copy-start.3
  63.9 0.0 copy-start.4
  63.9 0.0 collective-permute-done.3.right_ref
  63.9 0.0 collective-permute-done.2.left_ref
  64.0 0.0 copy-start.2
  64.0 1.5 %copy-done.2 = f32[27,2,64,64]{3,2,1,0:T(8,128)S(1)} copy-done((f32[27,2,64,64]{3,2,1,0:T(8,128)S(1)}, f32[27,2,64,64]{3,2,1,0:T(8,128)}, u32[]{:S(2)}) %copy-start.2) | copy-done | bytes 884760
  65.4 8.4 %near.1.near_ref = f32[128,256]{1,0:T(8,128)S(1)} custom-call(s32[6912]{0:T(1024)S(1)} %reshape.34.index_ref, f32[768,128]{1,0:T(8,128)} %collective-permute-done.2.left_ref, f32[768,128]{1,0:T(8,128)S(1)} %join.1.own_ref, f32[768,128]{1,0:T(8,128)S(1)} %collective-permute-done.3.right_ref, f32[27,2,64,64]{3,2,1,0:T(8,128)S(1)} %copy-done.2), custom_call_target="tpu_custom_call" | custom-call | flops 10000000000 | bytes 41943040 | tf_op jit(solution)/shard_map/near/pallas_call | solution.py:283
  73.9 11.2 %all-to-all-done.1 = f32[256,4,128]{2,1,0:T(4,128)S(1)} async-done(((f32[256,4,128]{2,1,0:T(4,128)}), f32[256,4,128]{2,1,0:T(4,128)S(1)}, u32[]{:S(2)}, u32[]{:S(2)}) %all-to-all-start.1) | async-done | bytes 524320 | tf_op jit(solution)/shard_map/all_to_all | solution.py:332
  85.1 2.9 %from_grid.1 = f32[128,256]{1,0:T(8,128)} custom-call(s32[1]{0:T(128)S(6)} %copy.19.count_ref, s32[1,256]{1,0:T(1,128)S(1)} %bitcast.12, f32[1024,128]{1,0:T(8,128)S(1)} %bitcast.8, f32[64,64]{1,0:T(8,128)S(1)} %copy-done.3, bf16[128,2048]{1,0:T(8,128)(2,1)S(1)} %copy-done.5, bf16[128,512]{1,0:T(8,128)(2,1)S(1)} %copy-done.7, ...), custom_call_target="tpu_custom_call" | custom-call | flops 2000000000 | bytes 2097152 | tf_op jit(solution)/shard_map/from_grid/pallas_call | solution.py:283
  (13 shorter events, 0.1 us)
Async XLA Ops:
  0.7 21.7 %copy-start = (f32[2,64,256]{2,1,0:T(8,128)S(1)}, f32[2,64,256]{2,1,0:T(8,128)}, u32[]{:S(2)}) copy-start(f32[2,64,256]{2,1,0:T(8,128)} %param.18) | copy-start | bytes 393220
  5.7 37.1 %all-to-all-start = ((f32[256,4,128]{2,1,0:T(4,128)}), f32[256,4,128]{2,1,0:T(4,128)}, u32[]{:S(2)}, u32[]{:S(2)}) async-start(f32[256,4,128]{2,1,0:T(4,128)} %bitcast.13), calls=%async_computation | async-start | bytes 1048576 | tf_op jit(solution)/shard_map/all_to_all | solution.py:319
  22.4 0.7 copy-start.1
  23.2 12.0 %collective-permute-start.1 = (f32[256,128]{1,0:T(8,128)S(1)}, f32[256,128]{1,0:T(8,128)S(1)}, u32[]{:S(2)}, u32[]{:S(2)}) collective-permute-start(f32[256,128]{1,0:T(8,128)S(1)} %turn.1.b_ref), channel_id=1, source_target_pairs={{1,0},{2,1},{3,2},{5,4},{6,5},{7,6},{9,8},{10,9},{11,10},{13,12},{... | collective-permute-start | bytes 393224 | tf_op jit(solution)/shard_map/ppermute | solution.py:298
  27.3 7.9 %collective-permute-start = (f32[256,128]{1,0:T(8,128)S(1)}, f32[256,128]{1,0:T(8,128)S(1)}, u32[]{:S(2)}, u32[]{:S(2)}) collective-permute-start(f32[256,128]{1,0:T(8,128)S(1)} %turn.1.b_ref), channel_id=1, source_target_pairs={{0,1},{1,2},{2,3},{4,5},{5,6},{6,7},{8,9},{9,10},{10,11},{12,13},{... | collective-permute-start | bytes 393224 | tf_op jit(solution)/shard_map/ppermute | solution.py:298
  35.2 28.7 %collective-permute-start.3 = (f32[768,128]{1,0:T(8,128)S(1)}, f32[768,128]{1,0:T(8,128)S(1)}, u32[]{:S(2)}, u32[]{:S(2)}) collective-permute-start(f32[768,128]{1,0:T(8,128)S(1)} %join.1.own_ref), channel_id=1, source_target_pairs={{4,0},{8,4},{12,8},{16,12},{20,16},{24,20},{28,24},{32,28},{36,32}... | collective-permute-start | bytes 1179656 | tf_op jit(solution)/shard_map/ppermute | solution.py:298
  36.5 27.4 %collective-permute-start.2 = (f32[768,128]{1,0:T(8,128)S(1)}, f32[768,128]{1,0:T(8,128)}, u32[]{:S(2)}, u32[]{:S(2)}) collective-permute-start(f32[768,128]{1,0:T(8,128)S(1)} %join.1.own_ref), channel_id=1, source_target_pairs={{0,4},{4,8},{8,12},{12,16},{16,20},{20,24},{24,28},{28,32},{32,36}... | collective-permute-start | bytes 1179656 | tf_op jit(solution)/shard_map/ppermute | solution.py:298
  42.8 21.1 %copy-start.8 = (s32[27,256]{1,0:T(8,128)S(1)}, s32[27,256]{1,0:T(8,128)}, u32[]{:S(2)}) copy-start(s32[27,256]{1,0:T(8,128)} %param.24) | copy-start | bytes 82948
  49.5 35.6 %all-to-all-start.1 = ((f32[256,4,128]{2,1,0:T(4,128)}), f32[256,4,128]{2,1,0:T(4,128)S(1)}, u32[]{:S(2)}, u32[]{:S(2)}) async-start(f32[256,4,128]{2,1,0:T(4,128)} %bitcast.14), calls=%async_computation.1 | async-start | bytes 1048576 | tf_op jit(solution)/shard_map/all_to_all | solution.py:332
  63.9 21.2 %copy-start.3 = (f32[64,64]{1,0:T(8,128)S(1)}, f32[64,64]{1,0:T(8,128)}, u32[]{:S(2)}) copy-start(f32[64,64]{1,0:T(8,128)} %proj_ref.1) | copy-start | bytes 49156
  63.9 21.2 %copy-start.4 = (s32[256]{0:T(256)S(1)}, s32[256]{0:T(256)}, u32[]{:S(2)}) copy-start(s32[256]{0:T(256)} %param.22) | copy-start | bytes 3076
  64.0 1.5 %copy-start.2 = (f32[27,2,64,64]{3,2,1,0:T(8,128)S(1)}, f32[27,2,64,64]{3,2,1,0:T(8,128)}, u32[]{:S(2)}) copy-start(f32[27,2,64,64]{3,2,1,0:T(8,128)} %table_ref.1) | copy-start | bytes 2654212
  65.4 19.7 %copy-start.5 = (bf16[128,2048]{1,0:T(8,128)(2,1)S(1)}, bf16[128,2048]{1,0:T(8,128)(2,1)}, u32[]{:S(2)}) copy-start(bf16[128,2048]{1,0:T(8,128)(2,1)} %constant.22.clone.expand_any.expand_ref) | copy-start | bytes 1572868
  65.4 19.7 %copy-start.6 = (bf16[128,512]{1,0:T(8,128)(2,1)S(1)}, bf16[128,512]{1,0:T(8,128)(2,1)}, u32[]{:S(2)}) copy-start(bf16[128,512]{1,0:T(8,128)(2,1)} %constant.32.clone.fl_ref) | copy-start | bytes 393220
  65.4 19.7 %copy-start.7 = (bf16[128,512]{1,0:T(8,128)(2,1)S(1)}, bf16[128,512]{1,0:T(8,128)(2,1)}, u32[]{:S(2)}) copy-start(bf16[128,512]{1,0:T(8,128)(2,1)} %constant.31.clone.fh_ref) | copy-start | bytes 393220

commit v5 on v4

--- a/solution.py
+++ b/solution.py
@@ -167,59 +167,48 @@
             ah[1, a, c], al[1, a, c] = split(jnp.where(first, pltpu.roll(d0, 96, 1), d1))
     copies[0].wait()
     copies[1].wait()
-    for xp in range(2):
-        a = slice(128 * xp, 128 * xp + 128)
-        for r in range(2):
-            c = slice(256 * r, 256 * r + 256)
-            even = dot3(ah[0, a, :], al[0, a, :], yh[0, :, c], yl[0, :, c])
-            odd = dot3(ah[1, a, :], al[1, a, :], yh[1, :, c], yl[1, :, c])
-            o = slice(128 * r, 128 * r + 128)
-            sh[xp, o, 0:256], sl[xp, o, 0:256] = split(even + odd)
-            sh[xp, o, 256:512], sl[xp, o, 256:512] = split(even - odd)
+    for r in range(2):
+        c = slice(256 * r, 256 * r + 256)
+        o = slice(128 * r, 128 * r + 128)
+        even = dot3(ah[0], al[0], yh[0, :, c], yl[0, :, c])
+        odd = dot3(ah[1], al[1], yh[1, :, c], yl[1, :, c])
+        for half, (h, l) in enumerate((split(even + odd), split(even - odd))):
+            k = slice(256 * half, 256 * half + 256)
+            for xp in range(2):
+                sh[xp, o, k] = h[128 * xp : 128 * xp + 128]
+                sl[xp, o, k] = l[128 * xp : 128 * xp + 128]
     copies[2].wait()
     copies[3].wait()
     copies[4].wait()
     for j in range(2):
         c = slice(256 * j, 256 * j + 256)
-        for i in range(2):
-            lo = slice(128 * i, 128 * i + 128)
-            hi = slice(256 + 128 * i, 384 + 128 * i)
-            part = [[dot3(xh[xp, a, :], xl[xp, a, :], sh[xp, :, c], sl[xp, :, c]) for xp in range(2)] for a in (lo, hi)]
-            (re0, re1), (im0, im1) = part
-            re, im = re0 + re1, im0 + im1
-            gr, gi = green_ref[0, lo, c], green_ref[1, lo, c]
-            p_re, p_im = gr * re - gi * im, gr * im + gi * re
-            re, im = re0 - re1, im0 - im1
-            gr, gi = green_ref[0, hi, c], green_ref[1, hi, c]
-            q_re, q_im = gr * re - gi * im, gr * im + gi * re
-            qh[0, lo, c], ql[0, lo, c] = split(p_re + q_re)
-            qh[1, lo, c], ql[1, lo, c] = split(p_re - q_re)
-            qh[0, hi, c], ql[0, hi, c] = split(p_im + q_im)
-            qh[1, hi, c], ql[1, hi, c] = split(p_im - q_im)
+        part = [dot3(xh[xp], xl[xp], sh[xp, :, c], sl[xp, :, c]) for xp in range(2)]
+        sums, diffs = part[0] + part[1], part[0] - part[1]
+        gr, gi = green_ref[0, 0:256, c], green_ref[1, 0:256, c]
+        p_re, p_im = gr * sums[:256] - gi * sums[256:], gr * sums[256:] + gi * sums[:256]
+        gr, gi = green_ref[0, 256:512, c], green_ref[1, 256:512, c]
+        q_re, q_im = gr * diffs[:256] - gi * diffs[256:], gr * diffs[256:] + gi * diffs[:256]
+        qh[0, 0:256, c], ql[0, 0:256, c] = split(p_re + q_re)
+        qh[1, 0:256, c], ql[1, 0:256, c] = split(p_re - q_re)
+        qh[0, 256:512, c], ql[0, 256:512, c] = split(p_im + q_im)
+        qh[1, 256:512, c], ql[1, 256:512, c] = split(p_im - q_im)
     copies[5].wait()
     copies[6].wait()
     for xp in range(2):
-        for r in range(2):
-            a = slice(128 * r, 128 * r + 128)
-            u0, u1 = [
-                dot3(ih[xp, a, :], il[xp, a, :], qh[xp, :, c], ql[xp, :, c]) for c in (slice(0, 256), slice(256, 512))
-            ]
-            rows, o = slice(128 * xp, 128 * xp + 128), slice(256 * r, 256 * r + 256)
-            bh[0, rows, o], bl[0, rows, o] = split(u0 + u1)
-            bh[1, rows, o], bl[1, rows, o] = split(u0 - u1)
-    for xp in range(2):
-        a = slice(128 * xp, 128 * xp + 128)
-        even, odd = [
-            dot_t(bh[p, a, :], yh[p]) + (dot_t(bh[p, a, :], yl[p]) + dot_t(bl[p, a, :], yh[p])) for p in range(2)
-        ]
-        for e in range(2):
-            ex = order[2 * xp + e]
-            rows = slice(64 * e, 64 * e + 64)
-            for m in range(2):
-                c = slice(128 * m, 128 * m + 128)
-                ve, vo = even[rows, c], odd[rows, c]
-                out_ref[pl.ds(8 * m + ex, 64, stride=16), :] = jnp.where(first, ve, pltpu.roll(vo, 32, 1))
-                out_ref[pl.ds(8 * m + 4 + ex, 64, stride=16), :] = jnp.where(first, pltpu.roll(ve, 96, 1), vo)
+        u0, u1 = [dot3(ih[xp], il[xp], qh[xp, :, c], ql[xp, :, c]) for c in (slice(0, 256), slice(256, 512))]
+        rows = slice(128 * xp, 128 * xp + 128)
+        for p, (h, l) in enumerate((split(u0 + u1), split(u0 - u1))):
+            for r in range(2):
+                bh[p, rows, 256 * r : 256 * r + 256] = h[128 * r : 128 * r + 128]
+                bl[p, rows, 256 * r : 256 * r + 256] = l[128 * r : 128 * r + 128]
+    even, odd = [dot_t(bh[p], yh[p]) + (dot_t(bh[p], yl[p]) + dot_t(bl[p], yh[p])) for p in range(2)]
+    for e, ex in enumerate(order):
+        rows = slice(64 * e, 64 * e + 64)
+        for m in range(2):
+            c = slice(128 * m, 128 * m + 128)
+            ve, vo = even[rows, c], odd[rows, c]
+            out_ref[pl.ds(8 * m + ex, 64, stride=16), :] = jnp.where(first, ve, pltpu.roll(vo, 32, 1))
+            out_ref[pl.ds(8 * m + 4 + ex, 64, stride=16), :] = jnp.where(first, pltpu.roll(ve, 96, 1), vo)
 
 
 def from_grid(count_ref, site_ref, in_ref, proj_ref, expand_ref, fh_ref, fl_ref, near_ref, out_ref):
@@ -320,7 +309,9 @@
     masked = call(turn, shape(256, 128), (block_count, cells, token), "svv", bytes_accessed=1 << 20, name="turn", room=16)
     before, after = neighbours(masked, "narrow", N)
     own = call(join, shape(768, 128), (before, masked, after), "vvv", bytes_accessed=2 << 20, name="join", room=16)
-    left, right = neighbours(own, "wide", W)
+    left, _ = neighbours(own, "wide", W)
+    later, planes = lax.optimization_barrier((own, planes))
+    _, right = neighbours(later, "wide", W)
     back = call(
         convolve, shape(1024, 128),
         (planes.reshape(1024, 128), green_hat.reshape(2, 512, 512), yh, yl, xh, xl, ih, il), "hhhhhhhh",

time: 88.4 us -> 85.9 us (0.972)
  starting transfers between devices: 43.2 us -> 38.2 us
  waiting for transfers between devices: 18.7 us -> 21.6 us
    all_to_all x1, starting transfers between devices: 14.4 us -> 11.1 us  [per_device(): lax.all_to_all(back.reshape(256, 4, 128), BOTH, split_axis=0, concat_axis...]
    all_to_all x1, waiting for transfers between devices: 1.46 us -> 4.39 us  [per_device(): lax.all_to_all(sent.reshape(256, 4, 128), BOTH, split_axis=0, concat_axis...]
    ppermute x4, starting transfers between devices: 12.1 us -> 10.5 us  [neighbours(): return (lax.ppermute(array, axis, up), lax.ppermute(array, axis, down))]
where the time goes in v5:
time: 85.9 us; the launch traced here: 85.5 us
  starting transfers between devices  38.2 us (44%)
  Pallas kernels  22.7 us (26%)
  waiting for transfers between devices  21.6 us (25%)
  local copies, waits for them, and re-layouts  2.19 us (3%)
    pallas_call x6, Pallas kernels, call(): pl.pallas_call(kernel, out_shape=outs, in_specs=[pl.BlockSpec(memory_spac...  22.7 us
    all_to_all x1, starting transfers between devices, per_device(): lax.all_to_all(sent.reshape(256, 4, 128), BOTH, split_axis=0, concat_axis...  16.7 us
    all_to_all x1, waiting for transfers between devices, per_device(): lax.all_to_all(back.reshape(256, 4, 128), BOTH, split_axis=0, concat_axis...  11.2 us
    all_to_all x1, starting transfers between devices, per_device(): lax.all_to_all(back.reshape(256, 4, 128), BOTH, split_axis=0, concat_axis...  11.1 us
    ppermute x4, starting transfers between devices, neighbours(): return (lax.ppermute(array, axis, up), lax.ppermute(array, axis, down))  10.5 us
    ppermute x4, waiting for transfers between devices, neighbours(): return (lax.ppermute(array, axis, up), lax.ppermute(array, axis, down))  5.96 us
    all_to_all x1, waiting for transfers between devices, per_device(): lax.all_to_all(sent.reshape(256, 4, 128), BOTH, split_axis=0, concat_axis...  4.39 us
    unnamed x18, local copies, waits for them, and re-layouts  2.19 us
  transfers between devices with their start and end apart: 6, of which 3 were waited for; matrix products, arithmetic and copies ran while one was open for 0% of the time, Pallas kernels for 17%

profile of v5, /device:TPU:1, one launch (start us, length us, event | category | flops | bytes accessed | tf_op | source)
XLA Modules:
  0.0 85.5 jit_solution(11351756563490834435)
XLA Ops:
  0.7 5.0 %to_grid.1 = (f32[1024,128]{1,0:T(8,128)}, f32[8,128]{1,0:T(8,128)}) custom-call(s32[1]{0:T(128)S(6)} %copy.19.count_ref, f32[128,256]{1,0:T(8,128)} %bitcast.9, s32[1,256]{1,0:T(1,128)} %bitcast.11, f32[64,64]{1,0:T(8,128)} %proj_ref.1, bf16[128,2048]{1,0:T(8,128)(2,1)} %constant.22.clone.expand_any.expand_ref, bf16[256,256]{1,0:T(8,128)(2,1)} %constant.23.clone.fh_any, ...), custom_call_target="tpu_custom_call" | custom-call | flops 2000000000 | bytes 2097152 | tf_op jit(solution)/shard_map/to_grid/pallas_call | solution.py:272
  5.7 16.7 %all-to-all-start = ((f32[256,4,128]{2,1,0:T(4,128)}), f32[256,4,128]{2,1,0:T(4,128)}, u32[]{:S(2)}, u32[]{:S(2)}) async-start(f32[256,4,128]{2,1,0:T(4,128)} %bitcast.13), calls=%async_computation | async-start | bytes 1048576 | tf_op jit(solution)/shard_map/all_to_all | solution.py:308
  22.4 0.0 copy-start.1
  22.4 0.7 copy-done.1
  23.1 0.1 turn.1.b_ref
  23.2 4.1 %collective-permute-start.1 = (f32[256,128]{1,0:T(8,128)S(1)}, f32[256,128]{1,0:T(8,128)S(1)}, u32[]{:S(2)}, u32[]{:S(2)}) collective-permute-start(f32[256,128]{1,0:T(8,128)S(1)} %turn.1.b_ref), channel_id=1, source_target_pairs={{1,0},{2,1},{3,2},{5,4},{6,5},{7,6},{9,8},{10,9},{11,10},{13,12},{... | collective-permute-start | bytes 393224 | tf_op jit(solution)/shard_map/ppermute | solution.py:287
  27.3 1.9 %collective-permute-start = (f32[256,128]{1,0:T(8,128)S(1)}, f32[256,128]{1,0:T(8,128)S(1)}, u32[]{:S(2)}, u32[]{:S(2)}) collective-permute-start(f32[256,128]{1,0:T(8,128)S(1)} %turn.1.b_ref), channel_id=1, source_target_pairs={{0,1},{1,2},{2,3},{4,5},{5,6},{6,7},{8,9},{9,10},{10,11},{12,13},{... | collective-permute-start | bytes 393224 | tf_op jit(solution)/shard_map/ppermute | solution.py:287
  29.2 6.0 %collective-permute-done.1.c_ref = f32[256,128]{1,0:T(8,128)S(1)} collective-permute-done((f32[256,128]{1,0:T(8,128)S(1)}, f32[256,128]{1,0:T(8,128)S(1)}, u32[]{:S(2)}, u32[]{:S(2)}) %collective-permute-start.1) | collective-permute-done | bytes 131104 | tf_op jit(solution)/shard_map/ppermute | solution.py:287
  35.2 0.0 collective-permute-done.a_ref
  35.2 3.1 %collective-permute-start.2 = (f32[768,128]{1,0:T(8,128)S(1)}, f32[768,128]{1,0:T(8,128)S(1)}, u32[]{:S(2)}, u32[]{:S(2)}) collective-permute-start(f32[768,128]{1,0:T(8,128)S(1)} %join.1.own_ref), channel_id=1, source_target_pairs={{0,4},{4,8},{8,12},{12,16},{16,20},{20,24},{24,28},{28,32},{32,36}... | collective-permute-start | bytes 1179656 | tf_op jit(solution)/shard_map/ppermute | solution.py:287
  38.4 4.4 %all-to-all-done = f32[256,4,128]{2,1,0:T(4,128)} async-done(((f32[256,4,128]{2,1,0:T(4,128)}), f32[256,4,128]{2,1,0:T(4,128)}, u32[]{:S(2)}, u32[]{:S(2)}) %all-to-all-start) | async-done | bytes 524320 | tf_op jit(solution)/shard_map/all_to_all | solution.py:308
  42.8 1.3 %collective-permute-start.3 = (f32[768,128]{1,0:T(8,128)S(1)}, f32[768,128]{1,0:T(8,128)}, u32[]{:S(2)}, u32[]{:S(2)}) collective-permute-start(f32[768,128]{1,0:T(8,128)S(1)} %join.1.own_ref), channel_id=1, source_target_pairs={{4,0},{8,4},{12,8},{16,12},{20,16},{24,20},{28,24},{32,28},{36,32}... | collective-permute-start | bytes 1179656 | tf_op jit(solution)/shard_map/ppermute | solution.py:287
  44.0 0.0 copy-start.8
  44.1 6.3 %convolve.1 = f32[1024,128]{1,0:T(8,128)} custom-call(f32[1024,128]{1,0:T(8,128)} %bitcast.3.in_any, f32[2,512,512]{2,1,0:T(8,128)} %bitcast.15, bf16[2,256,512]{2,1,0:T(8,128)(2,1)} %constant.25.clone.yh_any, bf16[2,256,512]{2,1,0:T(8,128)(2,1)} %constant.26.clone.yl_any, bf16[2,512,256]{2,1,0:T(8,128)(2,1)} %constant.27.clone.xh_any, ...), custom_call_target="tpu_custom_call" | custom-call | flops 5000000000 | bytes 9437184 | tf_op jit(solution)/shard_map/convolve/pallas_call | solution.py:272
  50.3 11.1 %all-to-all-start.1 = ((f32[256,4,128]{2,1,0:T(4,128)}), f32[256,4,128]{2,1,0:T(4,128)S(1)}, u32[]{:S(2)}, u32[]{:S(2)}) async-start(f32[256,4,128]{2,1,0:T(4,128)} %bitcast.14), calls=%async_computation.1 | async-start | bytes 1048576 | tf_op jit(solution)/shard_map/all_to_all | solution.py:323
  61.4 0.0 copy-start.3
  61.4 0.0 copy-start.4
  61.5 0.0 collective-permute-done.2.left_ref
  61.5 0.0 collective-permute-done.3.right_ref
  61.5 0.0 copy-start.2
  61.5 1.5 %copy-done.2 = f32[27,2,64,64]{3,2,1,0:T(8,128)S(1)} copy-done((f32[27,2,64,64]{3,2,1,0:T(8,128)S(1)}, f32[27,2,64,64]{3,2,1,0:T(8,128)}, u32[]{:S(2)}) %copy-start.2) | copy-done | bytes 884760
  63.0 8.4 %near.1.near_ref = f32[128,256]{1,0:T(8,128)S(1)} custom-call(s32[6912]{0:T(1024)S(1)} %reshape.34.index_ref, f32[768,128]{1,0:T(8,128)S(1)} %collective-permute-done.2.left_ref, f32[768,128]{1,0:T(8,128)S(1)} %join.1.own_ref, f32[768,128]{1,0:T(8,128)} %collective-permute-done.3.right_ref, f32[27,2,64,64]{3,2,1,0:T(8,128)S(1)} %copy-done.2), custom_call_target="tpu_custom_call" | custom-call | flops 10000000000 | bytes 41943040 | tf_op jit(solution)/shard_map/near/pallas_call | solution.py:272
  71.4 11.2 %all-to-all-done.1 = f32[256,4,128]{2,1,0:T(4,128)S(1)} async-done(((f32[256,4,128]{2,1,0:T(4,128)}), f32[256,4,128]{2,1,0:T(4,128)S(1)}, u32[]{:S(2)}, u32[]{:S(2)}) %all-to-all-start.1) | async-done | bytes 524320 | tf_op jit(solution)/shard_map/all_to_all | solution.py:323
  82.7 2.8 %from_grid.1 = f32[128,256]{1,0:T(8,128)} custom-call(s32[1]{0:T(128)S(6)} %copy.19.count_ref, s32[1,256]{1,0:T(1,128)S(1)} %bitcast.12, f32[1024,128]{1,0:T(8,128)S(1)} %bitcast.8, f32[64,64]{1,0:T(8,128)S(1)} %copy-done.3, bf16[128,2048]{1,0:T(8,128)(2,1)S(1)} %copy-done.5, bf16[128,512]{1,0:T(8,128)(2,1)S(1)} %copy-done.7, ...), custom_call_target="tpu_custom_call" | custom-call | flops 2000000000 | bytes 2097152 | tf_op jit(solution)/shard_map/from_grid/pallas_call | solution.py:272
  (13 shorter events, 0.1 us)
Async XLA Ops:
  0.7 21.7 %copy-start = (f32[2,64,256]{2,1,0:T(8,128)S(1)}, f32[2,64,256]{2,1,0:T(8,128)}, u32[]{:S(2)}) copy-start(f32[2,64,256]{2,1,0:T(8,128)} %param.18) | copy-start | bytes 393220
  5.7 37.1 %all-to-all-start = ((f32[256,4,128]{2,1,0:T(4,128)}), f32[256,4,128]{2,1,0:T(4,128)}, u32[]{:S(2)}, u32[]{:S(2)}) async-start(f32[256,4,128]{2,1,0:T(4,128)} %bitcast.13), calls=%async_computation | async-start | bytes 1048576 | tf_op jit(solution)/shard_map/all_to_all | solution.py:308
  22.4 0.7 copy-start.1
  23.2 12.0 %collective-permute-start.1 = (f32[256,128]{1,0:T(8,128)S(1)}, f32[256,128]{1,0:T(8,128)S(1)}, u32[]{:S(2)}, u32[]{:S(2)}) collective-permute-start(f32[256,128]{1,0:T(8,128)S(1)} %turn.1.b_ref), channel_id=1, source_target_pairs={{1,0},{2,1},{3,2},{5,4},{6,5},{7,6},{9,8},{10,9},{11,10},{13,12},{... | collective-permute-start | bytes 393224 | tf_op jit(solution)/shard_map/ppermute | solution.py:287
  27.3 7.9 %collective-permute-start = (f32[256,128]{1,0:T(8,128)S(1)}, f32[256,128]{1,0:T(8,128)S(1)}, u32[]{:S(2)}, u32[]{:S(2)}) collective-permute-start(f32[256,128]{1,0:T(8,128)S(1)} %turn.1.b_ref), channel_id=1, source_target_pairs={{0,1},{1,2},{2,3},{4,5},{5,6},{6,7},{8,9},{9,10},{10,11},{12,13},{... | collective-permute-start | bytes 393224 | tf_op jit(solution)/shard_map/ppermute | solution.py:287
  35.2 26.2 %collective-permute-start.2 = (f32[768,128]{1,0:T(8,128)S(1)}, f32[768,128]{1,0:T(8,128)S(1)}, u32[]{:S(2)}, u32[]{:S(2)}) collective-permute-start(f32[768,128]{1,0:T(8,128)S(1)} %join.1.own_ref), channel_id=1, source_target_pairs={{0,4},{4,8},{8,12},{12,16},{16,20},{20,24},{24,28},{28,32},{32,36}... | collective-permute-start | bytes 1179656 | tf_op jit(solution)/shard_map/ppermute | solution.py:287
  42.8 18.7 %collective-permute-start.3 = (f32[768,128]{1,0:T(8,128)S(1)}, f32[768,128]{1,0:T(8,128)}, u32[]{:S(2)}, u32[]{:S(2)}) collective-permute-start(f32[768,128]{1,0:T(8,128)S(1)} %join.1.own_ref), channel_id=1, source_target_pairs={{4,0},{8,4},{12,8},{16,12},{20,16},{24,20},{28,24},{32,28},{36,32}... | collective-permute-start | bytes 1179656 | tf_op jit(solution)/shard_map/ppermute | solution.py:287
  44.0 17.4 %copy-start.8 = (s32[27,256]{1,0:T(8,128)S(1)}, s32[27,256]{1,0:T(8,128)}, u32[]{:S(2)}) copy-start(s32[27,256]{1,0:T(8,128)} %param.24) | copy-start | bytes 82948
  50.3 32.3 %all-to-all-start.1 = ((f32[256,4,128]{2,1,0:T(4,128)}), f32[256,4,128]{2,1,0:T(4,128)S(1)}, u32[]{:S(2)}, u32[]{:S(2)}) async-start(f32[256,4,128]{2,1,0:T(4,128)} %bitcast.14), calls=%async_computation.1 | async-start | bytes 1048576 | tf_op jit(solution)/shard_map/all_to_all | solution.py:323
  61.4 21.2 %copy-start.3 = (f32[64,64]{1,0:T(8,128)S(1)}, f32[64,64]{1,0:T(8,128)}, u32[]{:S(2)}) copy-start(f32[64,64]{1,0:T(8,128)} %proj_ref.1) | copy-start | bytes 49156
  61.4 21.2 %copy-start.4 = (s32[256]{0:T(256)S(1)}, s32[256]{0:T(256)}, u32[]{:S(2)}) copy-start(s32[256]{0:T(256)} %param.22) | copy-start | bytes 3076
  61.5 1.5 %copy-start.2 = (f32[27,2,64,64]{3,2,1,0:T(8,128)S(1)}, f32[27,2,64,64]{3,2,1,0:T(8,128)}, u32[]{:S(2)}) copy-start(f32[27,2,64,64]{3,2,1,0:T(8,128)} %table_ref.1) | copy-start | bytes 2654212
  63.0 19.7 %copy-start.5 = (bf16[128,2048]{1,0:T(8,128)(2,1)S(1)}, bf16[128,2048]{1,0:T(8,128)(2,1)}, u32[]{:S(2)}) copy-start(bf16[128,2048]{1,0:T(8,128)(2,1)} %constant.22.clone.expand_any.expand_ref) | copy-start | bytes 1572868
  63.0 19.7 %copy-start.6 = (bf16[128,512]{1,0:T(8,128)(2,1)S(1)}, bf16[128,512]{1,0:T(8,128)(2,1)}, u32[]{:S(2)}) copy-start(bf16[128,512]{1,0:T(8,128)(2,1)} %constant.32.clone.fl_ref) | copy-start | bytes 393220
  63.0 19.7 %copy-start.7 = (bf16[128,512]{1,0:T(8,128)(2,1)S(1)}, bf16[128,512]{1,0:T(8,128)(2,1)}, u32[]{:S(2)}) copy-start(bf16[128,512]{1,0:T(8,128)(2,1)} %constant.31.clone.fh_ref) | copy-start | bytes 393220

commit v6 on v5

--- a/solution.py
+++ b/solution.py
@@ -95,18 +95,18 @@
     return copies
 
 
-def to_grid(count_ref, charges_any, site_any, proj_any, expand_any, fh_any, fl_any, out_ref, token_ref,
+def to_grid(count_ref, charges_any, site_any, proj_any, expand_any, fh_any, fl_any, out_ref, masked_ref,
             charges_ref, site_ref, proj_ref, expand_ref, fh_ref, fl_ref, sems):
     copies = fetch(
         [(charges_any, charges_ref), (proj_any, proj_ref), (site_any, site_ref),
          (expand_any, expand_ref), (fh_any, fh_ref), (fl_any, fl_ref)], sems)
-    token_ref[...] = jnp.zeros((8, 128), F32)
     count = count_ref[0]
     slots = lax.broadcasted_iota(jnp.int32, (128, 256), 1)
     for copy in copies[:3]:
         copy.wait()
     line, plane = site_masks(count, site_ref[...])
     turned = jnp.where(slots < count, charges_ref[...], 0.0).T
+    masked_ref[...] = turned
     ph, plo = split(proj_ref[...])
     parts = []
     for r in range(2):
@@ -136,11 +136,6 @@
         planes = dot3(fh_ref[...], fl_ref[...], gh[:, c], gl[:, c])
         out_ref[pl.ds(2 * e, 256, stride=4), :] = planes[:, :128]
         out_ref[pl.ds(2 * e + 1, 256, stride=4), :] = planes[:, 128:]
-
-
-def turn(count_ref, charges_ref, after_ref, out_ref):
-    slots = lax.broadcasted_iota(jnp.int32, (128, 256), 1)
-    out_ref[...] = jnp.where(slots < count_ref[0], charges_ref[...], 0.0).T
 
 
 def join(a_ref, b_ref, c_ref, out_ref):
@@ -299,19 +294,16 @@
     shape = lambda *s: jax.ShapeDtypeStruct(s, F32)
 
     cells = charges.reshape(128, 256)
-    sent, token = call(
-        to_grid, (shape(1024, 128), shape(8, 128)), (block_count, cells, site, projection, expand, fzh, fzl), "shhhhhh",
+    sent, masked = call(
+        to_grid, (shape(1024, 128), shape(256, 128)), (block_count, cells, site, projection, expand, fzh, fzl), "shhhhhh",
         scratch=[VMEM((128, 256), F32), VMEM((1, 256), jnp.int32), VMEM((64, 64), F32), VMEM((128, 2048), BF16)]
         + [VMEM((256, 256), BF16)] * 2,
         copies=6, flops=2 * 10**9, bytes_accessed=2 << 20, name="to_grid", room=63,
     )
     planes = lax.all_to_all(sent.reshape(256, 4, 128), BOTH, split_axis=0, concat_axis=0, tiled=True)
-    masked = call(turn, shape(256, 128), (block_count, cells, token), "svv", bytes_accessed=1 << 20, name="turn", room=16)
     before, after = neighbours(masked, "narrow", N)
     own = call(join, shape(768, 128), (before, masked, after), "vvv", bytes_accessed=2 << 20, name="join", room=16)
-    left, _ = neighbours(own, "wide", W)
-    later, planes = lax.optimization_barrier((own, planes))
-    _, right = neighbours(later, "wide", W)
+    left, right = neighbours(own, "wide", W)
     back = call(
         convolve, shape(1024, 128),
         (planes.reshape(1024, 128), green_hat.reshape(2, 512, 512), yh, yl, xh, xl, ih, il), "hhhhhhhh",

time: 85.9 us -> 88.7 us (1.033)
  starting transfers between devices: 38.2 us -> 44 us
  waiting for transfers between devices: 21.6 us -> 18.6 us
    all_to_all x1, starting transfers between devices: 11.1 us -> 15.3 us  [per_device(): lax.all_to_all(back.reshape(256, 4, 128), BOTH, split_axis=0, concat_axis...]
    all_to_all x1, waiting for transfers between devices: 4.39 us -> 0.56 us  [per_device(): lax.all_to_all(sent.reshape(256, 4, 128), BOTH, split_axis=0, concat_axis...]
    ppermute x4, starting transfers between devices: 10.5 us -> 12.1 us  [neighbours(): return (lax.ppermute(array, axis, up), lax.ppermute(array, axis, down))]
    unnamed x18 -> x16, local copies, waits for them, and re-layouts: 2.19 us -> 2.4 us
    pallas_call x6 -> x5, Pallas kernels: 22.7 us -> 22.5 us  [call(): pl.pallas_call(kernel, out_shape=outs, in_specs=[pl.BlockSpec(memory_spac...]
where the time goes in v6:
time: 88.7 us; the launch traced here: 88.3 us
  starting transfers between devices  44 us (50%)
  Pallas kernels  22.5 us (25%)
  waiting for transfers between devices  18.6 us (21%)
  local copies, waits for them, and re-layouts  2.41 us (3%)
    pallas_call x5, Pallas kernels, call(): pl.pallas_call(kernel, out_shape=outs, in_specs=[pl.BlockSpec(memory_spac...  22.5 us
    all_to_all x1, starting transfers between devices, per_device(): lax.all_to_all(sent.reshape(256, 4, 128), BOTH, split_axis=0, concat_axis...  16.7 us
    all_to_all x1, starting transfers between devices, per_device(): lax.all_to_all(back.reshape(256, 4, 128), BOTH, split_axis=0, concat_axis...  15.3 us
    ppermute x4, starting transfers between devices, neighbours(): return (lax.ppermute(array, axis, up), lax.ppermute(array, axis, down))  12.1 us
    all_to_all x1, waiting for transfers between devices, per_device(): lax.all_to_all(back.reshape(256, 4, 128), BOTH, split_axis=0, concat_axis...  11.2 us
    ppermute x4, waiting for transfers between devices, neighbours(): return (lax.ppermute(array, axis, up), lax.ppermute(array, axis, down))  6.77 us
    unnamed x16, local copies, waits for them, and re-layouts  2.4 us
  transfers between devices with their start and end apart: 6, of which 3 were waited for; matrix products, arithmetic and copies ran while one was open for 0% of the time, Pallas kernels for 17%

profile of v6, /device:TPU:1, one launch (start us, length us, event | category | flops | bytes accessed | tf_op | source)
XLA Modules:
  0.0 88.3 jit_solution(16715076200812839857)
XLA Ops:
  0.7 5.0 %to_grid.1 = (f32[1024,128]{1,0:T(8,128)}, f32[256,128]{1,0:T(8,128)}) custom-call(s32[1]{0:T(128)S(6)} %copy.19.count_ref, f32[128,256]{1,0:T(8,128)} %bitcast.14, s32[1,256]{1,0:T(1,128)} %bitcast.9, f32[64,64]{1,0:T(8,128)} %proj_ref.1, bf16[128,2048]{1,0:T(8,128)(2,1)} %constant.22.clone.expand_any.expand_ref, bf16[256,256]{1,0:T(8,128)(2,1)} %constant.23.clone.fh_any, ...), custom_call_target="tpu_custom_call" | custom-call | flops 2000000000 | bytes 2097152 | tf_op jit(solution)/shard_map/to_grid/pallas_call | solution.py:267
  5.6 16.7 %all-to-all-start = ((f32[256,4,128]{2,1,0:T(4,128)}), f32[256,4,128]{2,1,0:T(4,128)}, u32[]{:S(2)}, u32[]{:S(2)}) async-start(f32[256,4,128]{2,1,0:T(4,128)} %bitcast.11), calls=%async_computation | async-start | bytes 1048576 | tf_op jit(solution)/shard_map/all_to_all | solution.py:303
  22.3 4.1 %collective-permute-start.1 = (f32[256,128]{1,0:T(8,128)}, f32[256,128]{1,0:T(8,128)S(1)}, u32[]{:S(2)}, u32[]{:S(2)}) collective-permute-start(f32[256,128]{1,0:T(8,128)} %get-tuple-element.8.b_ref), channel_id=1, source_target_pairs={{1,0},{2,1},{3,2},{5,4},{6,5},{7,6},{9,8},{10,9},{11,10},{13,12},{... | collective-permute-start | bytes 393224 | tf_op jit(solution)/shard_map/ppermute | solution.py:282
  26.4 1.9 %collective-permute-start = (f32[256,128]{1,0:T(8,128)}, f32[256,128]{1,0:T(8,128)S(1)}, u32[]{:S(2)}, u32[]{:S(2)}) collective-permute-start(f32[256,128]{1,0:T(8,128)} %get-tuple-element.8.b_ref), channel_id=1, source_target_pairs={{0,1},{1,2},{2,3},{4,5},{5,6},{6,7},{8,9},{9,10},{10,11},{12,13},{... | collective-permute-start | bytes 393224 | tf_op jit(solution)/shard_map/ppermute | solution.py:282
  28.4 6.8 %collective-permute-done.1.c_ref = f32[256,128]{1,0:T(8,128)S(1)} collective-permute-done((f32[256,128]{1,0:T(8,128)}, f32[256,128]{1,0:T(8,128)S(1)}, u32[]{:S(2)}, u32[]{:S(2)}) %collective-permute-start.1) | collective-permute-done | bytes 131104 | tf_op jit(solution)/shard_map/ppermute | solution.py:282
  35.1 0.0 collective-permute-done.a_ref
  35.1 0.9 %copy-done = f32[256,128]{1,0:T(8,128)S(1)} copy-done((f32[256,128]{1,0:T(8,128)S(1)}, f32[256,128]{1,0:T(8,128)}, u32[]{:S(2)}) %copy-start) | copy-done | bytes 131096
  36.1 1.3 %collective-permute-start.3 = (f32[768,128]{1,0:T(8,128)S(1)}, f32[768,128]{1,0:T(8,128)S(1)}, u32[]{:S(2)}, u32[]{:S(2)}) collective-permute-start(f32[768,128]{1,0:T(8,128)S(1)} %join.1.own_ref), channel_id=1, source_target_pairs={{4,0},{8,4},{12,8},{16,12},{20,16},{24,20},{28,24},{32,28},{36,32}... | collective-permute-start | bytes 1179656 | tf_op jit(solution)/shard_map/ppermute | solution.py:282
  37.4 4.8 %collective-permute-start.2 = (f32[768,128]{1,0:T(8,128)S(1)}, f32[768,128]{1,0:T(8,128)}, u32[]{:S(2)}, u32[]{:S(2)}) collective-permute-start(f32[768,128]{1,0:T(8,128)S(1)} %join.1.own_ref), channel_id=1, source_target_pairs={{0,4},{4,8},{8,12},{12,16},{16,20},{20,24},{24,28},{28,32},{32,36}... | collective-permute-start | bytes 1179656 | tf_op jit(solution)/shard_map/ppermute | solution.py:282
  42.1 0.6 all-to-all-done
  42.7 6.3 %convolve.1 = f32[1024,128]{1,0:T(8,128)} custom-call(f32[1024,128]{1,0:T(8,128)} %bitcast.3.in_any, f32[2,512,512]{2,1,0:T(8,128)} %bitcast.13, bf16[2,256,512]{2,1,0:T(8,128)(2,1)} %constant.25.clone.yh_any, bf16[2,256,512]{2,1,0:T(8,128)(2,1)} %constant.26.clone.yl_any, bf16[2,512,256]{2,1,0:T(8,128)(2,1)} %constant.27.clone.xh_any, ...), custom_call_target="tpu_custom_call" | custom-call | flops 5000000000 | bytes 9437184 | tf_op jit(solution)/shard_map/convolve/pallas_call | solution.py:267
  49.0 15.3 %all-to-all-start.1 = ((f32[256,4,128]{2,1,0:T(4,128)}), f32[256,4,128]{2,1,0:T(4,128)S(1)}, u32[]{:S(2)}, u32[]{:S(2)}) async-start(f32[256,4,128]{2,1,0:T(4,128)} %bitcast.12), calls=%async_computation.1 | async-start | bytes 1048576 | tf_op jit(solution)/shard_map/all_to_all | solution.py:315
  64.2 0.0 copy-done.7
  64.2 0.0 copy-start.2
  64.3 0.0 copy-start.3
  64.3 0.0 collective-permute-done.3.right_ref
  64.3 0.0 collective-permute-done.2.left_ref
  64.3 0.0 copy-start.1
  64.3 1.5 %copy-done.1 = f32[27,2,64,64]{3,2,1,0:T(8,128)S(1)} copy-done((f32[27,2,64,64]{3,2,1,0:T(8,128)S(1)}, f32[27,2,64,64]{3,2,1,0:T(8,128)}, u32[]{:S(2)}) %copy-start.1) | copy-done | bytes 884760
  65.8 8.4 %near.1.near_ref = f32[128,256]{1,0:T(8,128)S(1)} custom-call(s32[6912]{0:T(1024)S(1)} %reshape.34.index_ref, f32[768,128]{1,0:T(8,128)} %collective-permute-done.2.left_ref, f32[768,128]{1,0:T(8,128)S(1)} %join.1.own_ref, f32[768,128]{1,0:T(8,128)S(1)} %collective-permute-done.3.right_ref, f32[27,2,64,64]{3,2,1,0:T(8,128)S(1)} %copy-done.1), custom_call_target="tpu_custom_call" | custom-call | flops 10000000000 | bytes 41943040 | tf_op jit(solution)/shard_map/near/pallas_call | solution.py:267
  74.2 11.2 %all-to-all-done.1 = f32[256,4,128]{2,1,0:T(4,128)S(1)} async-done(((f32[256,4,128]{2,1,0:T(4,128)}), f32[256,4,128]{2,1,0:T(4,128)S(1)}, u32[]{:S(2)}, u32[]{:S(2)}) %all-to-all-start.1) | async-done | bytes 524320 | tf_op jit(solution)/shard_map/all_to_all | solution.py:315
  85.5 0.0 copy-done.2
  85.5 0.0 copy-done.3
  85.5 2.8 %from_grid.1 = f32[128,256]{1,0:T(8,128)} custom-call(s32[1]{0:T(128)S(6)} %copy.19.count_ref, s32[1,256]{1,0:T(1,128)S(1)} %bitcast.10, f32[1024,128]{1,0:T(8,128)S(1)} %bitcast.8, f32[64,64]{1,0:T(8,128)S(1)} %copy-done.2, bf16[128,2048]{1,0:T(8,128)(2,1)S(1)} %copy-done.4, bf16[128,512]{1,0:T(8,128)(2,1)S(1)} %copy-done.6, ...), custom_call_target="tpu_custom_call" | custom-call | flops 2000000000 | bytes 2097152 | tf_op jit(solution)/shard_map/from_grid/pallas_call | solution.py:267
  (10 shorter events, 0.0 us)
Async XLA Ops:
  5.6 37.1 %all-to-all-start = ((f32[256,4,128]{2,1,0:T(4,128)}), f32[256,4,128]{2,1,0:T(4,128)}, u32[]{:S(2)}, u32[]{:S(2)}) async-start(f32[256,4,128]{2,1,0:T(4,128)} %bitcast.11), calls=%async_computation | async-start | bytes 1048576 | tf_op jit(solution)/shard_map/all_to_all | solution.py:303
  22.3 12.8 %collective-permute-start.1 = (f32[256,128]{1,0:T(8,128)}, f32[256,128]{1,0:T(8,128)S(1)}, u32[]{:S(2)}, u32[]{:S(2)}) collective-permute-start(f32[256,128]{1,0:T(8,128)} %get-tuple-element.8.b_ref), channel_id=1, source_target_pairs={{1,0},{2,1},{3,2},{5,4},{6,5},{7,6},{9,8},{10,9},{11,10},{13,12},{... | collective-permute-start | bytes 393224 | tf_op jit(solution)/shard_map/ppermute | solution.py:282
  26.4 8.7 %collective-permute-start = (f32[256,128]{1,0:T(8,128)}, f32[256,128]{1,0:T(8,128)S(1)}, u32[]{:S(2)}, u32[]{:S(2)}) collective-permute-start(f32[256,128]{1,0:T(8,128)} %get-tuple-element.8.b_ref), channel_id=1, source_target_pairs={{0,1},{1,2},{2,3},{4,5},{5,6},{6,7},{8,9},{9,10},{10,11},{12,13},{... | collective-permute-start | bytes 393224 | tf_op jit(solution)/shard_map/ppermute | solution.py:282
  35.1 0.9 %copy-start = (f32[256,128]{1,0:T(8,128)S(1)}, f32[256,128]{1,0:T(8,128)}, u32[]{:S(2)}) copy-start(f32[256,128]{1,0:T(8,128)} %get-tuple-element.8.b_ref) | copy-start | bytes 393220
  36.1 28.2 %collective-permute-start.3 = (f32[768,128]{1,0:T(8,128)S(1)}, f32[768,128]{1,0:T(8,128)S(1)}, u32[]{:S(2)}, u32[]{:S(2)}) collective-permute-start(f32[768,128]{1,0:T(8,128)S(1)} %join.1.own_ref), channel_id=1, source_target_pairs={{4,0},{8,4},{12,8},{16,12},{20,16},{24,20},{28,24},{32,28},{36,32}... | collective-permute-start | bytes 1179656 | tf_op jit(solution)/shard_map/ppermute | solution.py:282
  37.4 26.9 %collective-permute-start.2 = (f32[768,128]{1,0:T(8,128)S(1)}, f32[768,128]{1,0:T(8,128)}, u32[]{:S(2)}, u32[]{:S(2)}) collective-permute-start(f32[768,128]{1,0:T(8,128)S(1)} %join.1.own_ref), channel_id=1, source_target_pairs={{0,4},{4,8},{8,12},{12,16},{16,20},{20,24},{24,28},{28,32},{32,36}... | collective-permute-start | bytes 1179656 | tf_op jit(solution)/shard_map/ppermute | solution.py:282
  42.7 21.6 %copy-start.7 = (s32[27,256]{1,0:T(8,128)S(1)}, s32[27,256]{1,0:T(8,128)}, u32[]{:S(2)}) copy-start(s32[27,256]{1,0:T(8,128)} %param.24) | copy-start | bytes 82948
  49.0 36.5 %all-to-all-start.1 = ((f32[256,4,128]{2,1,0:T(4,128)}), f32[256,4,128]{2,1,0:T(4,128)S(1)}, u32[]{:S(2)}, u32[]{:S(2)}) async-start(f32[256,4,128]{2,1,0:T(4,128)} %bitcast.12), calls=%async_computation.1 | async-start | bytes 1048576 | tf_op jit(solution)/shard_map/all_to_all | solution.py:315
  64.2 21.2 %copy-start.2 = (f32[64,64]{1,0:T(8,128)S(1)}, f32[64,64]{1,0:T(8,128)}, u32[]{:S(2)}) copy-start(f32[64,64]{1,0:T(8,128)} %proj_ref.1) | copy-start | bytes 49156
  64.3 21.2 %copy-start.3 = (s32[256]{0:T(256)S(1)}, s32[256]{0:T(256)}, u32[]{:S(2)}) copy-start(s32[256]{0:T(256)} %param.22) | copy-start | bytes 3076
  64.3 1.5 %copy-start.1 = (f32[27,2,64,64]{3,2,1,0:T(8,128)S(1)}, f32[27,2,64,64]{3,2,1,0:T(8,128)}, u32[]{:S(2)}) copy-start(f32[27,2,64,64]{3,2,1,0:T(8,128)} %table_ref.1) | copy-start | bytes 2654212
  65.8 19.7 %copy-start.4 = (bf16[128,2048]{1,0:T(8,128)(2,1)S(1)}, bf16[128,2048]{1,0:T(8,128)(2,1)}, u32[]{:S(2)}) copy-start(bf16[128,2048]{1,0:T(8,128)(2,1)} %constant.22.clone.expand_any.expand_ref) | copy-start | bytes 1572868
  65.8 19.7 %copy-start.5 = (bf16[128,512]{1,0:T(8,128)(2,1)S(1)}, bf16[128,512]{1,0:T(8,128)(2,1)}, u32[]{:S(2)}) copy-start(bf16[128,512]{1,0:T(8,128)(2,1)} %constant.32.clone.fl_ref) | copy-start | bytes 393220
  65.8 19.7 %copy-start.6 = (bf16[128,512]{1,0:T(8,128)(2,1)S(1)}, bf16[128,512]{1,0:T(8,128)(2,1)}, u32[]{:S(2)}) copy-start(bf16[128,512]{1,0:T(8,128)(2,1)} %constant.31.clone.fh_ref) | copy-start | bytes 393220

commit v7 on v6

--- a/solution.py
+++ b/solution.py
@@ -138,18 +138,18 @@
         out_ref[pl.ds(2 * e + 1, 256, stride=4), :] = planes[:, 128:]
 
 
-def join(a_ref, b_ref, c_ref, out_ref):
-    for i, ref in enumerate((a_ref, b_ref, c_ref)):
-        out_ref[256 * i : 256 * i + 256, :] = ref[...]
-
-
-def convolve(in_any, green_any, yh_any, yl_any, xh_any, xl_any, ih_any, il_any, out_ref,
-             in_ref, green_ref, yh, yl, xh, xl, ih, il, ah, al, sh, sl, qh, ql, bh, bl, sems):
-    (arrived,) = fetch([(in_any, in_ref)], sems)
+def join(count_ref, before_ref, charges_ref, after_ref, out_ref):
+    slots = lax.broadcasted_iota(jnp.int32, (128, 256), 1)
+    out_ref[0:256, :] = before_ref[...]
+    out_ref[256:512, :] = jnp.where(slots < count_ref[0], charges_ref[...], 0.0).T
+    out_ref[512:768, :] = after_ref[...]
+
+
+def convolve(in_ref, green_any, yh_any, yl_any, xh_any, xl_any, ih_any, il_any, out_ref,
+             green_ref, yh, yl, xh, xl, ih, il, ah, al, sh, sl, qh, ql, bh, bl, sems):
     copies = fetch(
         [(yh_any, yh), (yl_any, yl), (xh_any, xh), (xl_any, xl), (green_any, green_ref), (ih_any, ih), (il_any, il)],
-        sems.at[pl.ds(1, 7)])
-    arrived.wait()
+        sems)
     first = lax.broadcasted_iota(jnp.int32, (64, 128), 1) % 64 < 32
     order = (0, 2, 1, 3)
     for i, ex in enumerate(order):
@@ -270,7 +270,7 @@
         in_specs=[pl.BlockSpec(memory_space=spaces[k]) for k in kinds],
         out_specs=out_spec if single else tuple(out_spec for _ in outs),
         scratch_shapes=scratch,
-        compiler_params=pltpu.CompilerParams(vmem_limit_bytes=room << 20),
+        compiler_params=pltpu.CompilerParams(vmem_limit_bytes=int(room * 2**20)),
         cost_estimate=pl.CostEstimate(flops=flops, bytes_accessed=bytes_accessed, transcendentals=0),
         name=name,
     )(*args)
@@ -302,27 +302,29 @@
     )
     planes = lax.all_to_all(sent.reshape(256, 4, 128), BOTH, split_axis=0, concat_axis=0, tiled=True)
     before, after = neighbours(masked, "narrow", N)
-    own = call(join, shape(768, 128), (before, masked, after), "vvv", bytes_accessed=2 << 20, name="join", room=16)
-    left, right = neighbours(own, "wide", W)
+    own = call(join, shape(768, 128), (block_count, before, cells, after), "svvv", bytes_accessed=2 << 20, name="join", room=16)
+    left, _ = neighbours(own, "wide", W)
+    later, planes = lax.optimization_barrier((own, planes))
+    _, right = neighbours(later, "wide", W)
     back = call(
         convolve, shape(1024, 128),
-        (planes.reshape(1024, 128), green_hat.reshape(2, 512, 512), yh, yl, xh, xl, ih, il), "hhhhhhhh",
-        scratch=[VMEM((1024, 128), F32), VMEM((2, 512, 512), F32)] + [VMEM((2, 256, 512), BF16)] * 2 + [VMEM((2, 512, 256), BF16)] * 2
+        (planes.reshape(1024, 128), green_hat.reshape(2, 512, 512), yh, yl, xh, xl, ih, il), "vhhhhhhh",
+        scratch=[VMEM((2, 512, 512), F32)] + [VMEM((2, 256, 512), BF16)] * 2 + [VMEM((2, 512, 256), BF16)] * 2
         + [VMEM((2, 256, 512), BF16)] * 2 + [VMEM((2, 256, 256), BF16)] * 2 + [VMEM((2, 256, 512), BF16)] * 2
         + [VMEM((2, 512, 512), BF16)] * 2 + [VMEM((2, 256, 512), BF16)] * 2,
-        copies=8, flops=5 * 10**9, bytes_accessed=9 << 20, name="convolve", room=63,
+        copies=7, flops=5 * 10**9, bytes_accessed=9 << 20, name="convolve", room=52.5,
     )
     field = lax.all_to_all(back.reshape(256, 4, 128), BOTH, split_axis=0, concat_axis=0, tiled=True)
     index = near_source.reshape(CLASSES * 256)
     beside = call(
         near, shape(128, 256), (index, left, own, right, near_table), "svvvv",
         scratch=[VMEM((2304, 128), F32), VMEM((CLASSES, 256, 128), F32)],
-        flops=10**10, bytes_accessed=40 << 20, name="near", room=16,
+        flops=10**10, bytes_accessed=40 << 20, name="near", room=52.5,
     )
     result = call(
         from_grid, shape(128, 256),
         (block_count, site, field.reshape(1024, 128), projection, expand, izh, izl, beside), "svvvvvvv",
-        flops=2 * 10**9, bytes_accessed=2 << 20, name="from_grid", room=12,
+        flops=2 * 10**9, bytes_accessed=2 << 20, name="from_grid", room=52.5,
     )
     return result.reshape(2, 64, 256)
 

time: 88.7 us -> 88.4 us (level)
  waiting for transfers between devices: 18.6 us -> 24.3 us
  starting transfers between devices: 44 us -> 39.7 us
  local copies, waits for them, and re-layouts: 2.41 us -> 0.05 us
    all_to_all x1, waiting for transfers between devices: 0.56 us -> 4.31 us  [per_device(): lax.all_to_all(sent.reshape(256, 4, 128), BOTH, split_axis=0, concat_axis...]
    unnamed x16 -> x14, local copies, waits for them, and re-layouts: 2.4 us -> 0.04 us
    ppermute x4, starting transfers between devices: 12.1 us -> 10.4 us  [neighbours(): return (lax.ppermute(array, axis, up), lax.ppermute(array, axis, down))]
    all_to_all x1, starting transfers between devices: 15.3 us -> 13.7 us  [per_device(): lax.all_to_all(back.reshape(256, 4, 128), BOTH, split_axis=0, concat_axis...]
    all_to_all x1, starting transfers between devices: 16.7 us -> 15.7 us  [per_device(): lax.all_to_all(sent.reshape(256, 4, 128), BOTH, split_axis=0, concat_axis...]
    all_to_all x1, waiting for transfers between devices: 11.2 us -> 12.2 us  [per_device(): lax.all_to_all(back.reshape(256, 4, 128), BOTH, split_axis=0, concat_axis...]
    ppermute x4, waiting for transfers between devices: 6.77 us -> 7.74 us  [neighbours(): return (lax.ppermute(array, axis, up), lax.ppermute(array, axis, down))]
where the time goes in v7:
time: 88.4 us; the launch traced here: 88 us
  starting transfers between devices  39.7 us (45%)
  waiting for transfers between devices  24.3 us (27%)
  Pallas kernels  23.1 us (26%)
    pallas_call x5, Pallas kernels, call(): pl.pallas_call(kernel, out_shape=outs, in_specs=[pl.BlockSpec(memory_spac...  23.1 us
    all_to_all x1, starting transfers between devices, per_device(): lax.all_to_all(sent.reshape(256, 4, 128), BOTH, split_axis=0, concat_axis...  15.7 us
    all_to_all x1, starting transfers between devices, per_device(): lax.all_to_all(back.reshape(256, 4, 128), BOTH, split_axis=0, concat_axis...  13.7 us
    all_to_all x1, waiting for transfers between devices, per_device(): lax.all_to_all(back.reshape(256, 4, 128), BOTH, split_axis=0, concat_axis...  12.2 us
    ppermute x4, starting transfers between devices, neighbours(): return (lax.ppermute(array, axis, up), lax.ppermute(array, axis, down))  10.4 us
    ppermute x4, waiting for transfers between devices, neighbours(): return (lax.ppermute(array, axis, up), lax.ppermute(array, axis, down))  7.74 us
    all_to_all x1, waiting for transfers between devices, per_device(): lax.all_to_all(sent.reshape(256, 4, 128), BOTH, split_axis=0, concat_axis...  4.31 us
  transfers between devices with their start and end apart: 6, of which 3 were waited for; matrix products, arithmetic and copies ran while one was open for 0% of the time, Pallas kernels for 17%

profile of v7, /device:TPU:1, one launch (start us, length us, event | category | flops | bytes accessed | tf_op | source)
XLA Modules:
  0.0 88.0 jit_solution(4123509946940781930)
XLA Ops:
  0.7 0.0 copy-start
  0.7 5.0 %to_grid.1 = (f32[1024,128]{1,0:T(8,128)}, f32[256,128]{1,0:T(8,128)}) custom-call(s32[1]{0:T(128)S(6)} %copy.19.count_ref, f32[128,256]{1,0:T(8,128)} %bitcast.10, s32[1,256]{1,0:T(1,128)} %bitcast.12, f32[64,64]{1,0:T(8,128)} %proj_ref.1, bf16[128,2048]{1,0:T(8,128)(2,1)} %constant.22.clone.expand_any.expand_ref, bf16[256,256]{1,0:T(8,128)(2,1)} %constant.23.clone.fh_any, ...), custom_call_target="tpu_custom_call" | custom-call | flops 2000000000 | bytes 2097152 | tf_op jit(solution)/shard_map/to_grid/pallas_call | solution.py:267
  5.7 15.7 %all-to-all-start = ((f32[256,4,128]{2,1,0:T(4,128)}), f32[256,4,128]{2,1,0:T(4,128)S(1)}, u32[]{:S(2)}, u32[]{:S(2)}) async-start(f32[256,4,128]{2,1,0:T(4,128)} %bitcast.14), calls=%async_computation | async-start | bytes 1048576 | tf_op jit(solution)/shard_map/all_to_all | solution.py:303
  21.4 4.1 %collective-permute-start.1 = (f32[256,128]{1,0:T(8,128)}, f32[256,128]{1,0:T(8,128)S(1)}, u32[]{:S(2)}, u32[]{:S(2)}) collective-permute-start(f32[256,128]{1,0:T(8,128)} %get-tuple-element.9), channel_id=1, source_target_pairs={{1,0},{2,1},{3,2},{5,4},{6,5},{7,6},{9,8},{10,9},{11,10},{13,12},{... | collective-permute-start | bytes 393224 | tf_op jit(solution)/shard_map/ppermute | solution.py:282
  25.4 1.9 %collective-permute-start = (f32[256,128]{1,0:T(8,128)}, f32[256,128]{1,0:T(8,128)S(1)}, u32[]{:S(2)}, u32[]{:S(2)}) collective-permute-start(f32[256,128]{1,0:T(8,128)} %get-tuple-element.9), channel_id=1, source_target_pairs={{0,1},{1,2},{2,3},{4,5},{5,6},{6,7},{8,9},{9,10},{10,11},{12,13},{... | collective-permute-start | bytes 393224 | tf_op jit(solution)/shard_map/ppermute | solution.py:282
  27.3 7.7 %collective-permute-done.1.after_ref = f32[256,128]{1,0:T(8,128)S(1)} collective-permute-done((f32[256,128]{1,0:T(8,128)}, f32[256,128]{1,0:T(8,128)S(1)}, u32[]{:S(2)}, u32[]{:S(2)}) %collective-permute-start.1) | collective-permute-done | bytes 131104 | tf_op jit(solution)/shard_map/ppermute | solution.py:282
  35.1 0.0 collective-permute-done.before_ref
  35.1 0.1 join.1.own_ref
  35.2 3.1 %collective-permute-start.2 = (f32[768,128]{1,0:T(8,128)S(1)}, f32[768,128]{1,0:T(8,128)S(1)}, u32[]{:S(2)}, u32[]{:S(2)}) collective-permute-start(f32[768,128]{1,0:T(8,128)S(1)} %join.1.own_ref), channel_id=1, source_target_pairs={{0,4},{4,8},{8,12},{12,16},{16,20},{20,24},{24,28},{28,32},{32,36}... | collective-permute-start | bytes 1179656 | tf_op jit(solution)/shard_map/ppermute | solution.py:282
  38.3 4.3 %all-to-all-done = f32[256,4,128]{2,1,0:T(4,128)S(1)} async-done(((f32[256,4,128]{2,1,0:T(4,128)}), f32[256,4,128]{2,1,0:T(4,128)S(1)}, u32[]{:S(2)}, u32[]{:S(2)}) %all-to-all-start) | async-done | bytes 524320 | tf_op jit(solution)/shard_map/all_to_all | solution.py:303
  42.6 1.3 %collective-permute-start.3 = (f32[768,128]{1,0:T(8,128)S(1)}, f32[768,128]{1,0:T(8,128)S(1)}, u32[]{:S(2)}, u32[]{:S(2)}) collective-permute-start(f32[768,128]{1,0:T(8,128)S(1)} %join.1.own_ref), channel_id=1, source_target_pairs={{4,0},{8,4},{12,8},{16,12},{20,16},{24,20},{28,24},{32,28},{36,32}... | collective-permute-start | bytes 1179656 | tf_op jit(solution)/shard_map/ppermute | solution.py:282
  43.9 0.0 copy-start.6
  43.9 6.3 %convolve.1 = f32[1024,128]{1,0:T(8,128)} custom-call(f32[1024,128]{1,0:T(8,128)S(1)} %bitcast.8, f32[2,512,512]{2,1,0:T(8,128)} %bitcast.15, bf16[2,256,512]{2,1,0:T(8,128)(2,1)} %constant.25.clone.yh_any, bf16[2,256,512]{2,1,0:T(8,128)(2,1)} %constant.26.clone.yl_any, bf16[2,512,256]{2,1,0:T(8,128)(2,1)} %constant.27.clone.xh_any, ...), custom_call_target="tpu_custom_call" | custom-call | flops 5000000000 | bytes 9437184 | tf_op jit(solution)/shard_map/convolve/pallas_call | solution.py:267
  50.2 13.7 %all-to-all-start.1 = ((f32[256,4,128]{2,1,0:T(4,128)}), f32[256,4,128]{2,1,0:T(4,128)S(1)}, u32[]{:S(2)}, u32[]{:S(2)}) async-start(f32[256,4,128]{2,1,0:T(4,128)} %bitcast.5), calls=%async_computation.1 | async-start | bytes 1048576 | tf_op jit(solution)/shard_map/all_to_all | solution.py:317
  64.0 0.0 copy-start.1
  64.0 0.0 copy-start.2
  64.0 0.0 copy-start.3
  64.0 0.0 copy-start.4
  64.0 0.0 copy-start.5
  64.0 0.0 collective-permute-done.2.left_ref
  64.0 0.0 collective-permute-done.3.right_ref
  64.0 8.9 %near.1.near_ref = f32[128,256]{1,0:T(8,128)S(1)} custom-call(s32[6912]{0:T(1024)S(1)} %reshape.34.index_ref, f32[768,128]{1,0:T(8,128)S(1)} %collective-permute-done.2.left_ref, f32[768,128]{1,0:T(8,128)S(1)} %join.1.own_ref, f32[768,128]{1,0:T(8,128)S(1)} %collective-permute-done.3.right_ref, f32[27,2,64,64]{3,2,1,0:T(8,128)} %table_ref.1), custom_call_target="tpu_custom_call" | custom-call | flops 10000000000 | bytes 41943040 | tf_op jit(solution)/shard_map/near/pallas_call | solution.py:267
  72.9 12.2 %all-to-all-done.1 = f32[256,4,128]{2,1,0:T(4,128)S(1)} async-done(((f32[256,4,128]{2,1,0:T(4,128)}), f32[256,4,128]{2,1,0:T(4,128)S(1)}, u32[]{:S(2)}, u32[]{:S(2)}) %all-to-all-start.1) | async-done | bytes 524320 | tf_op jit(solution)/shard_map/all_to_all | solution.py:317
  85.2 2.8 %from_grid.1 = f32[128,256]{1,0:T(8,128)} custom-call(s32[1]{0:T(128)S(6)} %copy.19.count_ref, s32[1,256]{1,0:T(1,128)S(1)} %bitcast.13, f32[1024,128]{1,0:T(8,128)S(1)} %bitcast.9, f32[64,64]{1,0:T(8,128)S(1)} %copy-done.1, bf16[128,2048]{1,0:T(8,128)(2,1)S(1)} %copy-done.3, bf16[128,512]{1,0:T(8,128)(2,1)S(1)} %copy-done.5, ...), custom_call_target="tpu_custom_call" | custom-call | flops 2000000000 | bytes 2097152 | tf_op jit(solution)/shard_map/from_grid/pallas_call | solution.py:267
  (8 shorter events, 0.0 us)
Async XLA Ops:
  0.7 34.4 %copy-start = (f32[2,64,256]{2,1,0:T(8,128)S(1)}, f32[2,64,256]{2,1,0:T(8,128)}, u32[]{:S(2)}) copy-start(f32[2,64,256]{2,1,0:T(8,128)} %param.18) | copy-start | bytes 393220
  5.7 36.9 %all-to-all-start = ((f32[256,4,128]{2,1,0:T(4,128)}), f32[256,4,128]{2,1,0:T(4,128)S(1)}, u32[]{:S(2)}, u32[]{:S(2)}) async-start(f32[256,4,128]{2,1,0:T(4,128)} %bitcast.14), calls=%async_computation | async-start | bytes 1048576 | tf_op jit(solution)/shard_map/all_to_all | solution.py:303
  21.4 13.7 %collective-permute-start.1 = (f32[256,128]{1,0:T(8,128)}, f32[256,128]{1,0:T(8,128)S(1)}, u32[]{:S(2)}, u32[]{:S(2)}) collective-permute-start(f32[256,128]{1,0:T(8,128)} %get-tuple-element.9), channel_id=1, source_target_pairs={{1,0},{2,1},{3,2},{5,4},{6,5},{7,6},{9,8},{10,9},{11,10},{13,12},{... | collective-permute-start | bytes 393224 | tf_op jit(solution)/shard_map/ppermute | solution.py:282
  25.4 9.7 %collective-permute-start = (f32[256,128]{1,0:T(8,128)}, f32[256,128]{1,0:T(8,128)S(1)}, u32[]{:S(2)}, u32[]{:S(2)}) collective-permute-start(f32[256,128]{1,0:T(8,128)} %get-tuple-element.9), channel_id=1, source_target_pairs={{0,1},{1,2},{2,3},{4,5},{5,6},{6,7},{8,9},{9,10},{10,11},{12,13},{... | collective-permute-start | bytes 393224 | tf_op jit(solution)/shard_map/ppermute | solution.py:282
  35.2 28.8 %collective-permute-start.2 = (f32[768,128]{1,0:T(8,128)S(1)}, f32[768,128]{1,0:T(8,128)S(1)}, u32[]{:S(2)}, u32[]{:S(2)}) collective-permute-start(f32[768,128]{1,0:T(8,128)S(1)} %join.1.own_ref), channel_id=1, source_target_pairs={{0,4},{4,8},{8,12},{12,16},{16,20},{20,24},{24,28},{28,32},{32,36}... | collective-permute-start | bytes 1179656 | tf_op jit(solution)/shard_map/ppermute | solution.py:282
  42.6 21.4 %collective-permute-start.3 = (f32[768,128]{1,0:T(8,128)S(1)}, f32[768,128]{1,0:T(8,128)S(1)}, u32[]{:S(2)}, u32[]{:S(2)}) collective-permute-start(f32[768,128]{1,0:T(8,128)S(1)} %join.1.own_ref), channel_id=1, source_target_pairs={{4,0},{8,4},{12,8},{16,12},{20,16},{24,20},{28,24},{32,28},{36,32}... | collective-permute-start | bytes 1179656 | tf_op jit(solution)/shard_map/ppermute | solution.py:282
  43.9 20.0 %copy-start.6 = (s32[27,256]{1,0:T(8,128)S(1)}, s32[27,256]{1,0:T(8,128)}, u32[]{:S(2)}) copy-start(s32[27,256]{1,0:T(8,128)} %param.24) | copy-start | bytes 82948
  50.2 34.9 %all-to-all-start.1 = ((f32[256,4,128]{2,1,0:T(4,128)}), f32[256,4,128]{2,1,0:T(4,128)S(1)}, u32[]{:S(2)}, u32[]{:S(2)}) async-start(f32[256,4,128]{2,1,0:T(4,128)} %bitcast.5), calls=%async_computation.1 | async-start | bytes 1048576 | tf_op jit(solution)/shard_map/all_to_all | solution.py:317
  64.0 21.2 %copy-start.1 = (f32[64,64]{1,0:T(8,128)S(1)}, f32[64,64]{1,0:T(8,128)}, u32[]{:S(2)}) copy-start(f32[64,64]{1,0:T(8,128)} %proj_ref.1) | copy-start | bytes 49156
  64.0 21.2 %copy-start.2 = (s32[256]{0:T(256)S(1)}, s32[256]{0:T(256)}, u32[]{:S(2)}) copy-start(s32[256]{0:T(256)} %param.22) | copy-start | bytes 3076
  64.0 21.2 %copy-start.3 = (bf16[128,2048]{1,0:T(8,128)(2,1)S(1)}, bf16[128,2048]{1,0:T(8,128)(2,1)}, u32[]{:S(2)}) copy-start(bf16[128,2048]{1,0:T(8,128)(2,1)} %constant.22.clone.expand_any.expand_ref) | copy-start | bytes 1572868
  64.0 21.2 %copy-start.4 = (bf16[128,512]{1,0:T(8,128)(2,1)S(1)}, bf16[128,512]{1,0:T(8,128)(2,1)}, u32[]{:S(2)}) copy-start(bf16[128,512]{1,0:T(8,128)(2,1)} %constant.32.clone.fl_ref) | copy-start | bytes 393220
  64.0 21.2 %copy-start.5 = (bf16[128,512]{1,0:T(8,128)(2,1)S(1)}, bf16[128,512]{1,0:T(8,128)(2,1)}, u32[]{:S(2)}) copy-start(bf16[128,512]{1,0:T(8,128)(2,1)} %constant.31.clone.fh_ref) | copy-start | bytes 393220

commit v8 on v7

--- a/solution.py
+++ b/solution.py
@@ -95,7 +95,7 @@
     return copies
 
 
-def to_grid(count_ref, charges_any, site_any, proj_any, expand_any, fh_any, fl_any, out_ref, masked_ref,
+def to_grid(count_ref, charges_any, site_any, proj_any, expand_any, fh_any, fl_any, out_ref,
             charges_ref, site_ref, proj_ref, expand_ref, fh_ref, fl_ref, sems):
     copies = fetch(
         [(charges_any, charges_ref), (proj_any, proj_ref), (site_any, site_ref),
@@ -106,7 +106,6 @@
         copy.wait()
     line, plane = site_masks(count, site_ref[...])
     turned = jnp.where(slots < count, charges_ref[...], 0.0).T
-    masked_ref[...] = turned
     ph, plo = split(proj_ref[...])
     parts = []
     for r in range(2):
@@ -136,6 +135,11 @@
         planes = dot3(fh_ref[...], fl_ref[...], gh[:, c], gl[:, c])
         out_ref[pl.ds(2 * e, 256, stride=4), :] = planes[:, :128]
         out_ref[pl.ds(2 * e + 1, 256, stride=4), :] = planes[:, 128:]
+
+
+def turn(count_ref, charges_ref, out_ref):
+    slots = lax.broadcasted_iota(jnp.int32, (128, 256), 1)
+    out_ref[...] = jnp.where(slots < count_ref[0], charges_ref[...], 0.0).T
 
 
 def join(count_ref, before_ref, charges_ref, after_ref, out_ref):
@@ -294,18 +298,18 @@
     shape = lambda *s: jax.ShapeDtypeStruct(s, F32)
 
     cells = charges.reshape(128, 256)
-    sent, masked = call(
-        to_grid, (shape(1024, 128), shape(256, 128)), (block_count, cells, site, projection, expand, fzh, fzl), "shhhhhh",
+    masked = call(turn, shape(256, 128), (block_count, cells), "sv", bytes_accessed=1 << 20, name="turn", room=16)
+    before, after = neighbours(masked, "narrow", N)
+    sent = call(
+        to_grid, shape(1024, 128), (block_count, cells, site, projection, expand, fzh, fzl), "shhhhhh",
         scratch=[VMEM((128, 256), F32), VMEM((1, 256), jnp.int32), VMEM((64, 64), F32), VMEM((128, 2048), BF16)]
         + [VMEM((256, 256), BF16)] * 2,
         copies=6, flops=2 * 10**9, bytes_accessed=2 << 20, name="to_grid", room=63,
     )
+    sent, before, after = lax.optimization_barrier((sent, before, after))
     planes = lax.all_to_all(sent.reshape(256, 4, 128), BOTH, split_axis=0, concat_axis=0, tiled=True)
-    before, after = neighbours(masked, "narrow", N)
     own = call(join, shape(768, 128), (block_count, before, cells, after), "svvv", bytes_accessed=2 << 20, name="join", room=16)
-    left, _ = neighbours(own, "wide", W)
-    later, planes = lax.optimization_barrier((own, planes))
-    _, right = neighbours(later, "wide", W)
+    left, right = neighbours(own, "wide", W)
     back = call(
         convolve, shape(1024, 128),
         (planes.reshape(1024, 128), green_hat.reshape(2, 512, 512), yh, yl, xh, xl, ih, il), "vhhhhhhh",

time: 88.4 us -> 90.4 us (1.023)
  waiting for transfers between devices: 24.3 us -> 28 us
  starting transfers between devices: 39.7 us -> 37 us
    all_to_all x1, waiting for transfers between devices: 4.31 us -> 15.8 us  [per_device(): lax.all_to_all(sent.reshape(256, 4, 128), BOTH, split_axis=0, concat_axis...]
    ppermute x4, waiting for transfers between devices: 7.74 us -> 0.01 us  [neighbours(): return (lax.ppermute(array, axis, up), lax.ppermute(array, axis, down))]
    all_to_all x1, starting transfers between devices: 13.7 us -> 11.1 us  [per_device(): lax.all_to_all(back.reshape(256, 4, 128), BOTH, split_axis=0, concat_axis...]
    all_to_all x1, starting transfers between devices: 15.7 us -> 13.6 us  [per_device(): lax.all_to_all(sent.reshape(256, 4, 128), BOTH, split_axis=0, concat_axis...]
    ppermute x4, starting transfers between devices: 10.4 us -> 12.4 us  [neighbours(): return (lax.ppermute(array, axis, up), lax.ppermute(array, axis, down))]
    pallas_call x5 -> x6, Pallas kernels: 23.1 us -> 23.2 us  [call(): pl.pallas_call(kernel, out_shape=outs, in_specs=[pl.BlockSpec(memory_spac...]
  transfers between devices with their start and end apart: 6 -> 6, of which waited for: 3 -> 2; matrix products, arithmetic and copies ran while one was open for 0% -> 0% of each run, Pallas kernels for 17% -> 23%
where the time goes in v8:
time: 90.4 us; the launch traced here: 90.1 us
  starting transfers between devices  37 us (41%)
  waiting for transfers between devices  28 us (31%)
  Pallas kernels  23.2 us (26%)
  local copies, waits for them, and re-layouts  0.95 us (1%)
    pallas_call x6, Pallas kernels, call(): pl.pallas_call(kernel, out_shape=outs, in_specs=[pl.BlockSpec(memory_spac...  23.2 us
    all_to_all x1, waiting for transfers between devices, per_device(): lax.all_to_all(sent.reshape(256, 4, 128), BOTH, split_axis=0, concat_axis...  15.8 us
    all_to_all x1, starting transfers between devices, per_device(): lax.all_to_all(sent.reshape(256, 4, 128), BOTH, split_axis=0, concat_axis...  13.6 us
    ppermute x4, starting transfers between devices, neighbours(): return (lax.ppermute(array, axis, up), lax.ppermute(array, axis, down))  12.4 us
    all_to_all x1, waiting for transfers between devices, per_device(): lax.all_to_all(back.reshape(256, 4, 128), BOTH, split_axis=0, concat_axis...  12.2 us
    all_to_all x1, starting transfers between devices, per_device(): lax.all_to_all(back.reshape(256, 4, 128), BOTH, split_axis=0, concat_axis...  11.1 us
  transfers between devices with their start and end apart: 6, of which 2 were waited for; matrix products, arithmetic and copies ran while one was open for 0% of the time, Pallas kernels for 23%

profile of v8, /device:TPU:1, one launch (start us, length us, event | category | flops | bytes accessed | tf_op | source)
XLA Modules:
  0.0 90.1 jit_solution(18308616839982117048)
XLA Ops:
  0.7 0.0 copy-start
  0.7 0.9 copy-done
  1.6 0.1 turn.1
  1.7 5.1 %collective-permute-start.1 = (f32[256,128]{1,0:T(8,128)S(1)}, f32[256,128]{1,0:T(8,128)S(1)}, u32[]{:S(2)}, u32[]{:S(2)}) collective-permute-start(f32[256,128]{1,0:T(8,128)S(1)} %turn.1), channel_id=1, source_target_pairs={{1,0},{2,1},{3,2},{5,4},{6,5},{7,6},{9,8},{10,9},{11,10},{13,12},{... | collective-permute-start | bytes 393224 | tf_op jit(solution)/shard_map/ppermute | solution.py:286
  6.8 1.9 %collective-permute-start = (f32[256,128]{1,0:T(8,128)S(1)}, f32[256,128]{1,0:T(8,128)S(1)}, u32[]{:S(2)}, u32[]{:S(2)}) collective-permute-start(f32[256,128]{1,0:T(8,128)S(1)} %turn.1), channel_id=1, source_target_pairs={{0,1},{1,2},{2,3},{4,5},{5,6},{6,7},{8,9},{9,10},{10,11},{12,13},{... | collective-permute-start | bytes 393224 | tf_op jit(solution)/shard_map/ppermute | solution.py:286
  8.8 0.0 copy-start.1
  8.8 5.0 %to_grid.1 = f32[1024,128]{1,0:T(8,128)} custom-call(s32[1]{0:T(128)S(6)} %copy.19.count_ref, f32[128,256]{1,0:T(8,128)} %bitcast.10, s32[1,256]{1,0:T(1,128)} %bitcast.13, f32[64,64]{1,0:T(8,128)} %proj_ref.1, bf16[128,2048]{1,0:T(8,128)(2,1)} %constant.22.clone.expand_any.expand_ref, bf16[256,256]{1,0:T(8,128)(2,1)} %constant.23.clone.fh_any, ...), custom_call_target="tpu_custom_call" | custom-call | flops 2000000000 | bytes 2097152 | tf_op jit(solution)/shard_map/to_grid/pallas_call | solution.py:271
  13.8 0.0 collective-permute-done.1.after_ref
  13.8 13.6 %all-to-all-start = ((f32[256,4,128]{2,1,0:T(4,128)}), f32[256,4,128]{2,1,0:T(4,128)S(1)}, u32[]{:S(2)}, u32[]{:S(2)}) async-start(f32[256,4,128]{2,1,0:T(4,128)} %bitcast.15), calls=%async_computation | async-start | bytes 1048576 | tf_op jit(solution)/shard_map/all_to_all | solution.py:310
  27.4 0.1 join.1.own_ref
  27.5 1.3 %collective-permute-start.3 = (f32[768,128]{1,0:T(8,128)S(1)}, f32[768,128]{1,0:T(8,128)S(1)}, u32[]{:S(2)}, u32[]{:S(2)}) collective-permute-start(f32[768,128]{1,0:T(8,128)S(1)} %join.1.own_ref), channel_id=1, source_target_pairs={{4,0},{8,4},{12,8},{16,12},{20,16},{24,20},{28,24},{32,28},{36,32}... | collective-permute-start | bytes 1179656 | tf_op jit(solution)/shard_map/ppermute | solution.py:286
  28.8 4.0 %collective-permute-start.2 = (f32[768,128]{1,0:T(8,128)S(1)}, f32[768,128]{1,0:T(8,128)S(1)}, u32[]{:S(2)}, u32[]{:S(2)}) collective-permute-start(f32[768,128]{1,0:T(8,128)S(1)} %join.1.own_ref), channel_id=1, source_target_pairs={{0,4},{4,8},{8,12},{12,16},{16,20},{20,24},{24,28},{28,32},{32,36}... | collective-permute-start | bytes 1179656 | tf_op jit(solution)/shard_map/ppermute | solution.py:286
  32.8 15.8 %all-to-all-done = f32[256,4,128]{2,1,0:T(4,128)S(1)} async-done(((f32[256,4,128]{2,1,0:T(4,128)}), f32[256,4,128]{2,1,0:T(4,128)S(1)}, u32[]{:S(2)}, u32[]{:S(2)}) %all-to-all-start) | async-done | bytes 524320 | tf_op jit(solution)/shard_map/all_to_all | solution.py:310
  48.6 6.3 %convolve.1 = f32[1024,128]{1,0:T(8,128)} custom-call(f32[1024,128]{1,0:T(8,128)S(1)} %bitcast.8, f32[2,512,512]{2,1,0:T(8,128)} %bitcast.16, bf16[2,256,512]{2,1,0:T(8,128)(2,1)} %constant.25.clone.yh_any, bf16[2,256,512]{2,1,0:T(8,128)(2,1)} %constant.26.clone.yl_any, bf16[2,512,256]{2,1,0:T(8,128)(2,1)} %constant.27.clone.xh_any, ...), custom_call_target="tpu_custom_call" | custom-call | flops 5000000000 | bytes 9437184 | tf_op jit(solution)/shard_map/convolve/pallas_call | solution.py:271
  54.9 11.1 %all-to-all-start.1 = ((f32[256,4,128]{2,1,0:T(4,128)}), f32[256,4,128]{2,1,0:T(4,128)S(1)}, u32[]{:S(2)}, u32[]{:S(2)}) async-start(f32[256,4,128]{2,1,0:T(4,128)} %bitcast.5), calls=%async_computation.1 | async-start | bytes 1048576 | tf_op jit(solution)/shard_map/all_to_all | solution.py:321
  66.0 0.0 copy-start.2
  66.0 0.0 copy-start.3
  66.1 0.0 copy-start.4
  66.1 0.0 copy-start.5
  66.1 0.0 copy-start.6
  66.1 0.0 collective-permute-done.3.right_ref
  66.1 8.9 %near.1.near_ref = f32[128,256]{1,0:T(8,128)S(1)} custom-call(s32[6912]{0:T(1024)S(1)} %reshape.34.index_ref, f32[768,128]{1,0:T(8,128)S(1)} %collective-permute-done.2.left_ref, f32[768,128]{1,0:T(8,128)S(1)} %join.1.own_ref, f32[768,128]{1,0:T(8,128)S(1)} %collective-permute-done.3.right_ref, f32[27,2,64,64]{3,2,1,0:T(8,128)} %table_ref.1), custom_call_target="tpu_custom_call" | custom-call | flops 10000000000 | bytes 41943040 | tf_op jit(solution)/shard_map/near/pallas_call | solution.py:271
  75.0 12.2 %all-to-all-done.1 = f32[256,4,128]{2,1,0:T(4,128)S(1)} async-done(((f32[256,4,128]{2,1,0:T(4,128)}), f32[256,4,128]{2,1,0:T(4,128)S(1)}, u32[]{:S(2)}, u32[]{:S(2)}) %all-to-all-start.1) | async-done | bytes 524320 | tf_op jit(solution)/shard_map/all_to_all | solution.py:321
  87.3 2.8 %from_grid.1 = f32[128,256]{1,0:T(8,128)} custom-call(s32[1]{0:T(128)S(6)} %copy.19.count_ref, s32[1,256]{1,0:T(1,128)S(1)} %bitcast.14, f32[1024,128]{1,0:T(8,128)S(1)} %bitcast.9, f32[64,64]{1,0:T(8,128)S(1)} %copy-done.2, bf16[128,2048]{1,0:T(8,128)(2,1)S(1)} %copy-done.4, bf16[128,512]{1,0:T(8,128)(2,1)S(1)} %copy-done.6, ...), custom_call_target="tpu_custom_call" | custom-call | flops 2000000000 | bytes 2097152 | tf_op jit(solution)/shard_map/from_grid/pallas_call | solution.py:271
  (11 shorter events, 0.0 us)
Async XLA Ops:
  0.7 0.9 %copy-start = (f32[2,64,256]{2,1,0:T(8,128)S(1)}, f32[2,64,256]{2,1,0:T(8,128)}, u32[]{:S(2)}) copy-start(f32[2,64,256]{2,1,0:T(8,128)} %param.18) | copy-start | bytes 393220
  1.7 12.1 %collective-permute-start.1 = (f32[256,128]{1,0:T(8,128)S(1)}, f32[256,128]{1,0:T(8,128)S(1)}, u32[]{:S(2)}, u32[]{:S(2)}) collective-permute-start(f32[256,128]{1,0:T(8,128)S(1)} %turn.1), channel_id=1, source_target_pairs={{1,0},{2,1},{3,2},{5,4},{6,5},{7,6},{9,8},{10,9},{11,10},{13,12},{... | collective-permute-start | bytes 393224 | tf_op jit(solution)/shard_map/ppermute | solution.py:286
  6.8 7.0 %collective-permute-start = (f32[256,128]{1,0:T(8,128)S(1)}, f32[256,128]{1,0:T(8,128)S(1)}, u32[]{:S(2)}, u32[]{:S(2)}) collective-permute-start(f32[256,128]{1,0:T(8,128)S(1)} %turn.1), channel_id=1, source_target_pairs={{0,1},{1,2},{2,3},{4,5},{5,6},{6,7},{8,9},{9,10},{10,11},{12,13},{... | collective-permute-start | bytes 393224 | tf_op jit(solution)/shard_map/ppermute | solution.py:286
  8.8 18.7 %copy-start.1 = (f32[2,64,256]{2,1,0:T(8,128)S(1)}, f32[2,64,256]{2,1,0:T(8,128)}, u32[]{:S(2)}) copy-start(f32[2,64,256]{2,1,0:T(8,128)} %param.18) | copy-start | bytes 393220
  13.8 34.8 %all-to-all-start = ((f32[256,4,128]{2,1,0:T(4,128)}), f32[256,4,128]{2,1,0:T(4,128)S(1)}, u32[]{:S(2)}, u32[]{:S(2)}) async-start(f32[256,4,128]{2,1,0:T(4,128)} %bitcast.15), calls=%async_computation | async-start | bytes 1048576 | tf_op jit(solution)/shard_map/all_to_all | solution.py:310
  27.5 38.6 %collective-permute-start.3 = (f32[768,128]{1,0:T(8,128)S(1)}, f32[768,128]{1,0:T(8,128)S(1)}, u32[]{:S(2)}, u32[]{:S(2)}) collective-permute-start(f32[768,128]{1,0:T(8,128)S(1)} %join.1.own_ref), channel_id=1, source_target_pairs={{4,0},{8,4},{12,8},{16,12},{20,16},{24,20},{28,24},{32,28},{36,32}... | collective-permute-start | bytes 1179656 | tf_op jit(solution)/shard_map/ppermute | solution.py:286
  28.8 37.3 %collective-permute-start.2 = (f32[768,128]{1,0:T(8,128)S(1)}, f32[768,128]{1,0:T(8,128)S(1)}, u32[]{:S(2)}, u32[]{:S(2)}) collective-permute-start(f32[768,128]{1,0:T(8,128)S(1)} %join.1.own_ref), channel_id=1, source_target_pairs={{0,4},{4,8},{8,12},{12,16},{16,20},{20,24},{24,28},{28,32},{32,36}... | collective-permute-start | bytes 1179656 | tf_op jit(solution)/shard_map/ppermute | solution.py:286
  48.6 17.4 %copy-start.7 = (s32[27,256]{1,0:T(8,128)S(1)}, s32[27,256]{1,0:T(8,128)}, u32[]{:S(2)}) copy-start(s32[27,256]{1,0:T(8,128)} %param.24) | copy-start | bytes 82948
  54.9 32.3 %all-to-all-start.1 = ((f32[256,4,128]{2,1,0:T(4,128)}), f32[256,4,128]{2,1,0:T(4,128)S(1)}, u32[]{:S(2)}, u32[]{:S(2)}) async-start(f32[256,4,128]{2,1,0:T(4,128)} %bitcast.5), calls=%async_computation.1 | async-start | bytes 1048576 | tf_op jit(solution)/shard_map/all_to_all | solution.py:321
  66.0 21.2 %copy-start.2 = (f32[64,64]{1,0:T(8,128)S(1)}, f32[64,64]{1,0:T(8,128)}, u32[]{:S(2)}) copy-start(f32[64,64]{1,0:T(8,128)} %proj_ref.1) | copy-start | bytes 49156
  66.0 21.2 %copy-start.3 = (s32[256]{0:T(256)S(1)}, s32[256]{0:T(256)}, u32[]{:S(2)}) copy-start(s32[256]{0:T(256)} %param.22) | copy-start | bytes 3076
  66.1 21.2 %copy-start.4 = (bf16[128,2048]{1,0:T(8,128)(2,1)S(1)}, bf16[128,2048]{1,0:T(8,128)(2,1)}, u32[]{:S(2)}) copy-start(bf16[128,2048]{1,0:T(8,128)(2,1)} %constant.22.clone.expand_any.expand_ref) | copy-start | bytes 1572868
  66.1 21.2 %copy-start.5 = (bf16[128,512]{1,0:T(8,128)(2,1)S(1)}, bf16[128,512]{1,0:T(8,128)(2,1)}, u32[]{:S(2)}) copy-start(bf16[128,512]{1,0:T(8,128)(2,1)} %constant.32.clone.fl_ref) | copy-start | bytes 393220
  66.1 21.2 %copy-start.6 = (bf16[128,512]{1,0:T(8,128)(2,1)S(1)}, bf16[128,512]{1,0:T(8,128)(2,1)}, u32[]{:S(2)}) copy-start(bf16[128,512]{1,0:T(8,128)(2,1)} %constant.31.clone.fh_ref) | copy-start | bytes 393220

commit v9 on v5

--- a/solution.py
+++ b/solution.py
@@ -101,39 +101,38 @@
         [(charges_any, charges_ref), (proj_any, proj_ref), (site_any, site_ref),
          (expand_any, expand_ref), (fh_any, fh_ref), (fl_any, fl_ref)], sems)
     token_ref[...] = jnp.zeros((8, 128), F32)
-    count = count_ref[0]
+    rows = lax.broadcasted_iota(jnp.int32, (128, 256), 0)
     slots = lax.broadcasted_iota(jnp.int32, (128, 256), 1)
     for copy in copies[:3]:
         copy.wait()
-    line, plane = site_masks(count, site_ref[...])
-    turned = jnp.where(slots < count, charges_ref[...], 0.0).T
+    occupied = slots < count_ref[0]
+    site = site_ref[...]
+    plane = jnp.where((rows % 16 == site // 32) & occupied, 1.0, 0.0).astype(BF16)
+    plane = jnp.concatenate([plane] * 4, axis=0)
+    masked = jnp.where(occupied, charges_ref[...], 0.0)
     ph, plo = split(proj_ref[...])
     parts = []
     for r in range(2):
-        mh, ml = split(turned[:, 64 * r : 64 * r + 64])
-        parts.append(dot_t(mh, ph) + (dot_t(mh, plo) + dot_t(ml, ph)))
-    both = jnp.concatenate(split(jnp.concatenate(parts, axis=1)), axis=0)
-    plane = jnp.concatenate([plane, plane], axis=1)
-    line = line.astype(BF16)
-    line = jnp.concatenate([line, line], axis=1)
+        mh, ml = split(masked[64 * r : 64 * r + 64])
+        parts.append(dot3(ph, plo, mh, ml))
+    both = jnp.concatenate(split(jnp.concatenate(parts, axis=0)), axis=1)
     copies[3].wait()
-    rows = []
+    grid = jnp.zeros((512, 128), F32)
     for ez in range(4):
-        cols = []
-        for e in range(2):
-            lo = (ez * 4 + 2 * e) * 128
-            spread = dot(both, expand_ref[:, lo : lo + 256])
-            high = (spread[:256] * plane).astype(BF16)
-            low = (spread[256:] * plane).astype(BF16)
-            cols.append(dot(line, jnp.concatenate([high, low], axis=0)))
-        rows.append(jnp.concatenate(cols, axis=1))
-    grid = jnp.concatenate(rows, axis=0)
-    gh, gl = split(jnp.concatenate([grid, swap(grid)], axis=0))
+        line = jnp.where((rows % 32 == site % 32) & (rows // 32 == ez), 1.0, 0.0).astype(BF16)
+        spread = dot(expand_ref[512 * ez : 512 * ez + 512, :], both)
+        for h in range(2):
+            grid = grid + dot_t(spread[:, 256 * h : 256 * h + 256].astype(BF16) * plane, line)
+    turned = []
+    for ex in range(4):
+        turned += [grid[128 * ex + 64 : 128 * ex + 128], -grid[128 * ex : 128 * ex + 64]]
+    gh, gl = split(jnp.concatenate([grid, jnp.concatenate(turned, axis=0)], axis=1))
     copies[4].wait()
     copies[5].wait()
+    fh, fl = fh_ref[...], fl_ref[...]
     for e in range(2):
         c = slice(256 * e, 256 * e + 256)
-        planes = dot3(fh_ref[...], fl_ref[...], gh[:, c], gl[:, c])
+        planes = dot_t(fh, gh[c]) + (dot_t(fh, gl[c]) + dot_t(fl, gh[c]))
         out_ref[pl.ds(2 * e, 256, stride=4), :] = planes[:, :128]
         out_ref[pl.ds(2 * e + 1, 256, stride=4), :] = planes[:, 128:]
 
@@ -300,8 +299,8 @@
 
     cells = charges.reshape(128, 256)
     sent, token = call(
-        to_grid, (shape(1024, 128), shape(8, 128)), (block_count, cells, site, projection, expand, fzh, fzl), "shhhhhh",
-        scratch=[VMEM((128, 256), F32), VMEM((1, 256), jnp.int32), VMEM((64, 64), F32), VMEM((128, 2048), BF16)]
+        to_grid, (shape(1024, 128), shape(8, 128)), (block_count, cells, site, projection, np.ascontiguousarray(expand.T), fzh, fzl), "shhhhhh",
+        scratch=[VMEM((128, 256), F32), VMEM((1, 256), jnp.int32), VMEM((64, 64), F32), VMEM((2048, 128), BF16)]
         + [VMEM((256, 256), BF16)] * 2,
         copies=6, flops=2 * 10**9, bytes_accessed=2 << 20, name="to_grid", room=63,
     )

time: 85.9 us -> 85 us (0.990)
  Pallas kernels: 22.7 us -> 21.8 us
    pallas_call x6, Pallas kernels: 22.7 us -> 21.8 us  [call(): pl.pallas_call(kernel, out_shape=outs, in_specs=[pl.BlockSpec(memory_spac...]
  transfers between devices with their start and end apart: 6 -> 6, of which waited for: 3 -> 3; matrix products, arithmetic and copies ran while one was open for 0% -> 0% of each run, Pallas kernels for 17% -> 18%
where the time goes in v9:
time: 85 us; the launch traced here: 84.6 us
  starting transfers between devices  38.2 us (45%)
  Pallas kernels  21.8 us (26%)
  waiting for transfers between devices  21.6 us (25%)
  local copies, waits for them, and re-layouts  2.19 us (3%)
  between operations  0.85 us (1%)
    pallas_call x6, Pallas kernels, call(): pl.pallas_call(kernel, out_shape=outs, in_specs=[pl.BlockSpec(memory_spac...  21.8 us
    all_to_all x1, starting transfers between devices, per_device(): lax.all_to_all(sent.reshape(256, 4, 128), BOTH, split_axis=0, concat_axis...  16.7 us
    all_to_all x1, waiting for transfers between devices, per_device(): lax.all_to_all(back.reshape(256, 4, 128), BOTH, split_axis=0, concat_axis...  11.2 us
    all_to_all x1, starting transfers between devices, per_device(): lax.all_to_all(back.reshape(256, 4, 128), BOTH, split_axis=0, concat_axis...  11.1 us
    ppermute x4, starting transfers between devices, neighbours(): return (lax.ppermute(array, axis, up), lax.ppermute(array, axis, down))  10.5 us
    ppermute x4, waiting for transfers between devices, neighbours(): return (lax.ppermute(array, axis, up), lax.ppermute(array, axis, down))  5.96 us
    all_to_all x1, waiting for transfers between devices, per_device(): lax.all_to_all(sent.reshape(256, 4, 128), BOTH, split_axis=0, concat_axis...  4.39 us
    unnamed x18, local copies, waits for them, and re-layouts  2.19 us
  transfers between devices with their start and end apart: 6, of which 3 were waited for; matrix products, arithmetic and copies ran while one was open for 0% of the time, Pallas kernels for 18%

profile of v9, /device:TPU:1, one launch (start us, length us, event | category | flops | bytes accessed | tf_op | source)
XLA Modules:
  0.0 84.6 jit_solution(14984647393647088033)
XLA Ops:
  0.7 4.1 %to_grid.1 = (f32[1024,128]{1,0:T(8,128)}, f32[8,128]{1,0:T(8,128)}) custom-call(s32[1]{0:T(128)S(6)} %copy.20.count_ref, f32[128,256]{1,0:T(8,128)} %bitcast.9, s32[1,256]{1,0:T(1,128)} %bitcast.11, f32[64,64]{1,0:T(8,128)} %proj_ref.1, bf16[2048,128]{1,0:T(8,128)(2,1)} %constant.24.clone.expand_any, bf16[256,256]{1,0:T(8,128)(2,1)} %constant.25.clone.fh_any, ...), custom_call_target="tpu_custom_call" | custom-call | flops 2000000000 | bytes 2097152 | tf_op jit(solution)/shard_map/to_grid/pallas_call | solution.py:271
  4.8 16.7 %all-to-all-start = ((f32[256,4,128]{2,1,0:T(4,128)}), f32[256,4,128]{2,1,0:T(4,128)}, u32[]{:S(2)}, u32[]{:S(2)}) async-start(f32[256,4,128]{2,1,0:T(4,128)} %bitcast.13), calls=%async_computation | async-start | bytes 1048576 | tf_op jit(solution)/shard_map/all_to_all | solution.py:307
  21.5 0.0 copy-start.1
  21.5 0.7 copy-done.1
  22.2 0.1 turn.1.b_ref
  22.3 4.1 %collective-permute-start.1 = (f32[256,128]{1,0:T(8,128)S(1)}, f32[256,128]{1,0:T(8,128)S(1)}, u32[]{:S(2)}, u32[]{:S(2)}) collective-permute-start(f32[256,128]{1,0:T(8,128)S(1)} %turn.1.b_ref), channel_id=1, source_target_pairs={{1,0},{2,1},{3,2},{5,4},{6,5},{7,6},{9,8},{10,9},{11,10},{13,12},{... | collective-permute-start | bytes 393224 | tf_op jit(solution)/shard_map/ppermute | solution.py:286
  26.4 1.9 %collective-permute-start = (f32[256,128]{1,0:T(8,128)S(1)}, f32[256,128]{1,0:T(8,128)S(1)}, u32[]{:S(2)}, u32[]{:S(2)}) collective-permute-start(f32[256,128]{1,0:T(8,128)S(1)} %turn.1.b_ref), channel_id=1, source_target_pairs={{0,1},{1,2},{2,3},{4,5},{5,6},{6,7},{8,9},{9,10},{10,11},{12,13},{... | collective-permute-start | bytes 393224 | tf_op jit(solution)/shard_map/ppermute | solution.py:286
  28.3 6.0 %collective-permute-done.1.c_ref = f32[256,128]{1,0:T(8,128)S(1)} collective-permute-done((f32[256,128]{1,0:T(8,128)S(1)}, f32[256,128]{1,0:T(8,128)S(1)}, u32[]{:S(2)}, u32[]{:S(2)}) %collective-permute-start.1) | collective-permute-done | bytes 131104 | tf_op jit(solution)/shard_map/ppermute | solution.py:286
  34.3 0.0 collective-permute-done.a_ref
  34.3 3.1 %collective-permute-start.2 = (f32[768,128]{1,0:T(8,128)S(1)}, f32[768,128]{1,0:T(8,128)S(1)}, u32[]{:S(2)}, u32[]{:S(2)}) collective-permute-start(f32[768,128]{1,0:T(8,128)S(1)} %join.1.own_ref), channel_id=1, source_target_pairs={{0,4},{4,8},{8,12},{12,16},{16,20},{20,24},{24,28},{28,32},{32,36}... | collective-permute-start | bytes 1179656 | tf_op jit(solution)/shard_map/ppermute | solution.py:286
  37.5 4.4 %all-to-all-done = f32[256,4,128]{2,1,0:T(4,128)} async-done(((f32[256,4,128]{2,1,0:T(4,128)}), f32[256,4,128]{2,1,0:T(4,128)}, u32[]{:S(2)}, u32[]{:S(2)}) %all-to-all-start) | async-done | bytes 524320 | tf_op jit(solution)/shard_map/all_to_all | solution.py:307
  41.9 1.3 %collective-permute-start.3 = (f32[768,128]{1,0:T(8,128)S(1)}, f32[768,128]{1,0:T(8,128)}, u32[]{:S(2)}, u32[]{:S(2)}) collective-permute-start(f32[768,128]{1,0:T(8,128)S(1)} %join.1.own_ref), channel_id=1, source_target_pairs={{4,0},{8,4},{12,8},{16,12},{20,16},{24,20},{28,24},{32,28},{36,32}... | collective-permute-start | bytes 1179656 | tf_op jit(solution)/shard_map/ppermute | solution.py:286
  43.1 0.0 copy-start.8
  43.2 6.3 %convolve.1 = f32[1024,128]{1,0:T(8,128)} custom-call(f32[1024,128]{1,0:T(8,128)} %bitcast.3.in_any, f32[2,512,512]{2,1,0:T(8,128)} %bitcast.15, bf16[2,256,512]{2,1,0:T(8,128)(2,1)} %constant.27.clone.yh_any, bf16[2,256,512]{2,1,0:T(8,128)(2,1)} %constant.28.clone.yl_any, bf16[2,512,256]{2,1,0:T(8,128)(2,1)} %constant.29.clone.xh_any, ...), custom_call_target="tpu_custom_call" | custom-call | flops 5000000000 | bytes 9437184 | tf_op jit(solution)/shard_map/convolve/pallas_call | solution.py:271
  49.4 11.1 %all-to-all-start.1 = ((f32[256,4,128]{2,1,0:T(4,128)}), f32[256,4,128]{2,1,0:T(4,128)S(1)}, u32[]{:S(2)}, u32[]{:S(2)}) async-start(f32[256,4,128]{2,1,0:T(4,128)} %bitcast.14), calls=%async_computation.1 | async-start | bytes 1048576 | tf_op jit(solution)/shard_map/all_to_all | solution.py:322
  60.5 0.0 copy-start.3
  60.5 0.0 copy-start.4
  60.6 0.0 collective-permute-done.2.left_ref
  60.6 0.0 collective-permute-done.3.right_ref
  60.6 0.0 copy-start.2
  60.6 1.5 %copy-done.2 = f32[27,2,64,64]{3,2,1,0:T(8,128)S(1)} copy-done((f32[27,2,64,64]{3,2,1,0:T(8,128)S(1)}, f32[27,2,64,64]{3,2,1,0:T(8,128)}, u32[]{:S(2)}) %copy-start.2) | copy-done | bytes 884760
  62.1 8.4 %near.1.near_ref = f32[128,256]{1,0:T(8,128)S(1)} custom-call(s32[6912]{0:T(1024)S(1)} %reshape.34.index_ref, f32[768,128]{1,0:T(8,128)S(1)} %collective-permute-done.2.left_ref, f32[768,128]{1,0:T(8,128)S(1)} %join.1.own_ref, f32[768,128]{1,0:T(8,128)} %collective-permute-done.3.right_ref, f32[27,2,64,64]{3,2,1,0:T(8,128)S(1)} %copy-done.2), custom_call_target="tpu_custom_call" | custom-call | flops 10000000000 | bytes 41943040 | tf_op jit(solution)/shard_map/near/pallas_call | solution.py:271
  70.5 11.2 %all-to-all-done.1 = f32[256,4,128]{2,1,0:T(4,128)S(1)} async-done(((f32[256,4,128]{2,1,0:T(4,128)}), f32[256,4,128]{2,1,0:T(4,128)S(1)}, u32[]{:S(2)}, u32[]{:S(2)}) %all-to-all-start.1) | async-done | bytes 524320 | tf_op jit(solution)/shard_map/all_to_all | solution.py:322
  81.8 2.8 %from_grid.1 = f32[128,256]{1,0:T(8,128)} custom-call(s32[1]{0:T(128)S(6)} %copy.20.count_ref, s32[1,256]{1,0:T(1,128)S(1)} %bitcast.12, f32[1024,128]{1,0:T(8,128)S(1)} %bitcast.8, f32[64,64]{1,0:T(8,128)S(1)} %copy-done.3, bf16[128,2048]{1,0:T(8,128)(2,1)S(1)} %copy-done.5, bf16[128,512]{1,0:T(8,128)(2,1)S(1)} %copy-done.7, ...), custom_call_target="tpu_custom_call" | custom-call | flops 2000000000 | bytes 2097152 | tf_op jit(solution)/shard_map/from_grid/pallas_call | solution.py:271
  (13 shorter events, 0.1 us)
Async XLA Ops:
  0.7 20.8 %copy-start = (f32[2,64,256]{2,1,0:T(8,128)S(1)}, f32[2,64,256]{2,1,0:T(8,128)}, u32[]{:S(2)}) copy-start(f32[2,64,256]{2,1,0:T(8,128)} %param.19) | copy-start | bytes 393220
  4.8 37.1 %all-to-all-start = ((f32[256,4,128]{2,1,0:T(4,128)}), f32[256,4,128]{2,1,0:T(4,128)}, u32[]{:S(2)}, u32[]{:S(2)}) async-start(f32[256,4,128]{2,1,0:T(4,128)} %bitcast.13), calls=%async_computation | async-start | bytes 1048576 | tf_op jit(solution)/shard_map/all_to_all | solution.py:307
  21.5 0.7 copy-start.1
  22.3 12.0 %collective-permute-start.1 = (f32[256,128]{1,0:T(8,128)S(1)}, f32[256,128]{1,0:T(8,128)S(1)}, u32[]{:S(2)}, u32[]{:S(2)}) collective-permute-start(f32[256,128]{1,0:T(8,128)S(1)} %turn.1.b_ref), channel_id=1, source_target_pairs={{1,0},{2,1},{3,2},{5,4},{6,5},{7,6},{9,8},{10,9},{11,10},{13,12},{... | collective-permute-start | bytes 393224 | tf_op jit(solution)/shard_map/ppermute | solution.py:286
  26.4 7.9 %collective-permute-start = (f32[256,128]{1,0:T(8,128)S(1)}, f32[256,128]{1,0:T(8,128)S(1)}, u32[]{:S(2)}, u32[]{:S(2)}) collective-permute-start(f32[256,128]{1,0:T(8,128)S(1)} %turn.1.b_ref), channel_id=1, source_target_pairs={{0,1},{1,2},{2,3},{4,5},{5,6},{6,7},{8,9},{9,10},{10,11},{12,13},{... | collective-permute-start | bytes 393224 | tf_op jit(solution)/shard_map/ppermute | solution.py:286
  34.3 26.2 %collective-permute-start.2 = (f32[768,128]{1,0:T(8,128)S(1)}, f32[768,128]{1,0:T(8,128)S(1)}, u32[]{:S(2)}, u32[]{:S(2)}) collective-permute-start(f32[768,128]{1,0:T(8,128)S(1)} %join.1.own_ref), channel_id=1, source_target_pairs={{0,4},{4,8},{8,12},{12,16},{16,20},{20,24},{24,28},{28,32},{32,36}... | collective-permute-start | bytes 1179656 | tf_op jit(solution)/shard_map/ppermute | solution.py:286
  41.9 18.7 %collective-permute-start.3 = (f32[768,128]{1,0:T(8,128)S(1)}, f32[768,128]{1,0:T(8,128)}, u32[]{:S(2)}, u32[]{:S(2)}) collective-permute-start(f32[768,128]{1,0:T(8,128)S(1)} %join.1.own_ref), channel_id=1, source_target_pairs={{4,0},{8,4},{12,8},{16,12},{20,16},{24,20},{28,24},{32,28},{36,32}... | collective-permute-start | bytes 1179656 | tf_op jit(solution)/shard_map/ppermute | solution.py:286
  43.1 17.4 %copy-start.8 = (s32[27,256]{1,0:T(8,128)S(1)}, s32[27,256]{1,0:T(8,128)}, u32[]{:S(2)}) copy-start(s32[27,256]{1,0:T(8,128)} %param.25) | copy-start | bytes 82948
  49.4 32.3 %all-to-all-start.1 = ((f32[256,4,128]{2,1,0:T(4,128)}), f32[256,4,128]{2,1,0:T(4,128)S(1)}, u32[]{:S(2)}, u32[]{:S(2)}) async-start(f32[256,4,128]{2,1,0:T(4,128)} %bitcast.14), calls=%async_computation.1 | async-start | bytes 1048576 | tf_op jit(solution)/shard_map/all_to_all | solution.py:322
  60.5 21.2 %copy-start.3 = (f32[64,64]{1,0:T(8,128)S(1)}, f32[64,64]{1,0:T(8,128)}, u32[]{:S(2)}) copy-start(f32[64,64]{1,0:T(8,128)} %proj_ref.1) | copy-start | bytes 49156
  60.5 21.2 %copy-start.4 = (s32[256]{0:T(256)S(1)}, s32[256]{0:T(256)}, u32[]{:S(2)}) copy-start(s32[256]{0:T(256)} %param.23) | copy-start | bytes 3076
  60.6 1.5 %copy-start.2 = (f32[27,2,64,64]{3,2,1,0:T(8,128)S(1)}, f32[27,2,64,64]{3,2,1,0:T(8,128)}, u32[]{:S(2)}) copy-start(f32[27,2,64,64]{3,2,1,0:T(8,128)} %table_ref.1) | copy-start | bytes 2654212
  62.1 19.7 %copy-start.5 = (bf16[128,2048]{1,0:T(8,128)(2,1)S(1)}, bf16[128,2048]{1,0:T(8,128)(2,1)}, u32[]{:S(2)}) copy-start(bf16[128,2048]{1,0:T(8,128)(2,1)} %constant.33.clone.expand_ref) | copy-start | bytes 1572868
  62.1 19.7 %copy-start.6 = (bf16[128,512]{1,0:T(8,128)(2,1)S(1)}, bf16[128,512]{1,0:T(8,128)(2,1)}, u32[]{:S(2)}) copy-start(bf16[128,512]{1,0:T(8,128)(2,1)} %constant.35.clone.fl_ref) | copy-start | bytes 393220
  62.1 19.7 %copy-start.7 = (bf16[128,512]{1,0:T(8,128)(2,1)S(1)}, bf16[128,512]{1,0:T(8,128)(2,1)}, u32[]{:S(2)}) copy-start(bf16[128,512]{1,0:T(8,128)(2,1)} %constant.34.clone.fh_ref) | copy-start | bytes 393220

commit v10 on v9

--- a/solution.py
+++ b/solution.py
@@ -36,6 +36,10 @@
 
 def dot3(lh, ll, rh, rl):
     return dot(lh, rh) + (dot(lh, rl) + dot(ll, rh))
+
+
+def dot_l(left, right):
+    return lax.dot_general(left, right, (((0,), (0,)), ((), ())), preferred_element_type=F32)
 
 
 def tables():
@@ -60,14 +64,7 @@
         ang = 2 * np.pi * ((y[:, None] * k[None, :]) % 512) / 512
         c, s = np.cos(ang), np.sin(ang)
         along.append(np.concatenate([np.where(real, c, s), np.where(real, -s, c)], 1))
-    across = []
-    j = np.arange(128)
-    for p in range(2):
-        x = 4 * (j % 64) + 2 * (j // 64) + p
-        ang = 2 * np.pi * ((k[:, None] * x[None, :]) % 512) / 512
-        c, s = np.cos(ang), np.sin(ang)
-        across.append(np.block([[c, s], [-s, c]]))
-    return forward_z, inverse_z, expand, np.stack(along), np.stack(across)
+    return forward_z, inverse_z, expand, np.stack(along)
 
 
 def swap(value):
@@ -142,46 +139,48 @@
     out_ref[...] = jnp.where(slots < count_ref[0], charges_ref[...], 0.0).T
 
 
-def join(a_ref, b_ref, c_ref, out_ref):
-    for i, ref in enumerate((a_ref, b_ref, c_ref)):
-        out_ref[256 * i : 256 * i + 256, :] = ref[...]
-
-
-def convolve(in_any, green_any, yh_any, yl_any, xh_any, xl_any, ih_any, il_any, out_ref,
-             in_ref, green_ref, yh, yl, xh, xl, ih, il, ah, al, sh, sl, qh, ql, bh, bl, sems):
-    (arrived,) = fetch([(in_any, in_ref)], sems)
-    copies = fetch(
-        [(yh_any, yh), (yl_any, yl), (xh_any, xh), (xl_any, xl), (green_any, green_ref), (ih_any, ih), (il_any, il)],
-        sems.at[pl.ds(1, 7)])
+def join(even_ref, own_ref, odd_ref, out_ref):
+    last = lax.axis_index("narrow") % 2
+    out_ref[pl.ds(pl.multiple_of(512 - 512 * last, 512), 256), :] = even_ref[...]
+    out_ref[256:512, :] = own_ref[...]
+    out_ref[pl.ds(pl.multiple_of(512 * last, 512), 256), :] = odd_ref[...]
+
+
+def convolve(in_any, th_any, tl_any, green_any, out_ref,
+             in_ref, th, tl, green_ref, ah, al, sh, sl, qh, ql, bh, bl, sems):
+    arrived, *copies = fetch([(in_any, in_ref), (th_any, th), (tl_any, tl), (green_any, green_ref)], sems)
     arrived.wait()
     first = lax.broadcasted_iota(jnp.int32, (64, 128), 1) % 64 < 32
-    order = (0, 2, 1, 3)
-    for i, ex in enumerate(order):
-        a = slice(64 * i, 64 * i + 64)
+    for ex in range(4):
+        base = ex % 2 * 128 + ex // 2 * 16
         for m in range(2):
             c = slice(128 * m, 128 * m + 128)
             d0 = in_ref[pl.ds(8 * m + ex, 64, stride=16), :]
             d1 = in_ref[pl.ds(8 * m + 4 + ex, 64, stride=16), :]
-            ah[0, a, c], al[0, a, c] = split(jnp.where(first, d0, pltpu.roll(d1, 32, 1)))
-            ah[1, a, c], al[1, a, c] = split(jnp.where(first, pltpu.roll(d0, 96, 1), d1))
+            pieces = split(jnp.where(first, d0, pltpu.roll(d1, 32, 1))), split(jnp.where(first, pltpu.roll(d0, 96, 1), d1))
+            for p, (h, l) in enumerate(pieces):
+                for w in range(4):
+                    a = slice(base + 32 * w, base + 32 * w + 16)
+                    ah[p, a, c], al[p, a, c] = h[16 * w : 16 * w + 16], l[16 * w : 16 * w + 16]
     copies[0].wait()
     copies[1].wait()
     for r in range(2):
         c = slice(256 * r, 256 * r + 256)
-        o = slice(128 * r, 128 * r + 128)
-        even = dot3(ah[0], al[0], yh[0, :, c], yl[0, :, c])
-        odd = dot3(ah[1], al[1], yh[1, :, c], yl[1, :, c])
+        even = dot3(ah[0], al[0], th[0, :, c], tl[0, :, c])
+        odd = dot3(ah[1], al[1], th[1, :, c], tl[1, :, c])
         for half, (h, l) in enumerate((split(even + odd), split(even - odd))):
             k = slice(256 * half, 256 * half + 256)
             for xp in range(2):
-                sh[xp, o, k] = h[128 * xp : 128 * xp + 128]
-                sl[xp, o, k] = l[128 * xp : 128 * xp + 128]
+                for m in range(2):
+                    o, a = slice(128 * m + 64 * r, 128 * m + 64 * r + 64), slice(128 * xp + 64 * m, 128 * xp + 64 * m + 64)
+                    sh[xp, o, k], sl[xp, o, k] = h[a], l[a]
     copies[2].wait()
-    copies[3].wait()
-    copies[4].wait()
     for j in range(2):
         c = slice(256 * j, 256 * j + 256)
-        part = [dot3(xh[xp], xl[xp], sh[xp, :, c], sl[xp, :, c]) for xp in range(2)]
+        part = []
+        for xp in range(2):
+            h, l = sh[xp, :, c], sl[xp, :, c]
+            part.append(dot_l(th[xp], h) + (dot_l(th[xp], l) + dot_l(tl[xp], h)))
         sums, diffs = part[0] + part[1], part[0] - part[1]
         gr, gi = green_ref[0, 0:256, c], green_ref[1, 0:256, c]
         p_re, p_im = gr * sums[:256] - gi * sums[256:], gr * sums[256:] + gi * sums[:256]
@@ -191,23 +190,26 @@
         qh[1, 0:256, c], ql[1, 0:256, c] = split(p_re - q_re)
         qh[0, 256:512, c], ql[0, 256:512, c] = split(p_im + q_im)
         qh[1, 256:512, c], ql[1, 256:512, c] = split(p_im - q_im)
-    copies[5].wait()
-    copies[6].wait()
     for xp in range(2):
-        u0, u1 = [dot3(ih[xp], il[xp], qh[xp, :, c], ql[xp, :, c]) for c in (slice(0, 256), slice(256, 512))]
-        rows = slice(128 * xp, 128 * xp + 128)
+        u0, u1 = [dot3(th[xp], tl[xp], qh[xp, :, c], ql[xp, :, c]) for c in (slice(0, 256), slice(256, 512))]
         for p, (h, l) in enumerate((split(u0 + u1), split(u0 - u1))):
             for r in range(2):
-                bh[p, rows, 256 * r : 256 * r + 256] = h[128 * r : 128 * r + 128]
-                bl[p, rows, 256 * r : 256 * r + 256] = l[128 * r : 128 * r + 128]
-    even, odd = [dot_t(bh[p], yh[p]) + (dot_t(bh[p], yl[p]) + dot_t(bl[p], yh[p])) for p in range(2)]
-    for e, ex in enumerate(order):
-        rows = slice(64 * e, 64 * e + 64)
-        for m in range(2):
-            c = slice(128 * m, 128 * m + 128)
-            ve, vo = even[rows, c], odd[rows, c]
-            out_ref[pl.ds(8 * m + ex, 64, stride=16), :] = jnp.where(first, ve, pltpu.roll(vo, 32, 1))
-            out_ref[pl.ds(8 * m + 4 + ex, 64, stride=16), :] = jnp.where(first, pltpu.roll(ve, 96, 1), vo)
+                for m in range(2):
+                    o, a = slice(128 * m + 64 * r, 128 * m + 64 * r + 64), slice(128 * xp + 64 * m, 128 * xp + 64 * m + 64)
+                    k = slice(256 * r, 256 * r + 256)
+                    bh[p, a, k], bl[p, a, k] = h[o], l[o]
+    even, odd = [dot_t(bh[p], th[p]) + (dot_t(bh[p], tl[p]) + dot_t(bl[p], th[p])) for p in range(2)]
+    first = first[:16]
+    for ex in range(4):
+        base = ex % 2 * 128 + ex // 2 * 16
+        for w in range(4):
+            rows = slice(base + 32 * w, base + 32 * w + 16)
+            for m in range(2):
+                c = slice(128 * m, 128 * m + 128)
+                ve, vo = even[rows, c], odd[rows, c]
+                place = 256 * w + 8 * m + ex
+                out_ref[pl.ds(place, 16, stride=16), :] = jnp.where(first, ve, pltpu.roll(vo, 32, 1))
+                out_ref[pl.ds(place + 4, 16, stride=16), :] = jnp.where(first, pltpu.roll(ve, 96, 1), vo)
 
 
 def from_grid(count_ref, site_ref, in_ref, proj_ref, expand_ref, fh_ref, fl_ref, near_ref, out_ref):
@@ -242,9 +244,11 @@
 CLASSES = 27
 
 
-def near(index_ref, left_ref, own_ref, right_ref, table_ref, out_ref, source_ref, picked):
-    for i, ref in enumerate((left_ref, own_ref, right_ref)):
-        source_ref[768 * i : 768 * i + 768, :] = ref[...]
+def near(index_ref, even_ref, own_ref, odd_ref, table_ref, out_ref, source_ref, picked):
+    last = lax.axis_index("wide") % 2
+    source_ref[pl.ds(pl.multiple_of(1536 - 1536 * last, 512), 768), :] = even_ref[...]
+    source_ref[768:1536, :] = own_ref[...]
+    source_ref[pl.ds(pl.multiple_of(1536 * last, 512), 768), :] = odd_ref[...]
 
     def one(k, carry):
         for b in range(256):
@@ -280,19 +284,16 @@
     )(*args)
 
 
-def neighbours(array, axis, size):
-    up = [(i, i + 1) for i in range(size - 1)]
-    down = [(i + 1, i) for i in range(size - 1)]
-    return lax.ppermute(array, axis, up), lax.ppermute(array, axis, down)
+def swap_pairs(array, axis, size, first):
+    pairs = [(i, i + 1) for i in range(first, size - 1, 2)]
+    return lax.ppermute(array, axis, pairs + [(j, i) for i, j in pairs])
 
 
 def per_device(charges, projection, green_hat, near_table, block_site, block_count, near_source):
-    forward_z, inverse_z, expand, along, across = tables()
+    forward_z, inverse_z, expand, along = tables()
     fzh, fzl = halves(forward_z)
     izh, izl = halves(inverse_z)
     yh, yl = halves(along)
-    xh, xl = halves(across)
-    ih, il = halves(np.ascontiguousarray(across.transpose(0, 2, 1)))
     expand = expand.astype(jnp.bfloat16)
     site = block_site.reshape(1, 256)
     shape = lambda *s: jax.ShapeDtypeStruct(s, F32)
@@ -306,23 +307,24 @@
     )
     planes = lax.all_to_all(sent.reshape(256, 4, 128), BOTH, split_axis=0, concat_axis=0, tiled=True)
     masked = call(turn, shape(256, 128), (block_count, cells, token), "svv", bytes_accessed=1 << 20, name="turn", room=16)
-    before, after = neighbours(masked, "narrow", N)
-    own = call(join, shape(768, 128), (before, masked, after), "vvv", bytes_accessed=2 << 20, name="join", room=16)
-    left, _ = neighbours(own, "wide", W)
+    odd = swap_pairs(masked, "narrow", N, 1)
+    even = swap_pairs(masked, "narrow", N, 0)
+    own = call(join, shape(768, 128), (even, masked, odd), "vvv", bytes_accessed=2 << 20, name="join", room=16)
+    odd = swap_pairs(own, "wide", W, 1)
     later, planes = lax.optimization_barrier((own, planes))
-    _, right = neighbours(later, "wide", W)
+    even = swap_pairs(later, "wide", W, 0)
     back = call(
         convolve, shape(1024, 128),
-        (planes.reshape(1024, 128), green_hat.reshape(2, 512, 512), yh, yl, xh, xl, ih, il), "hhhhhhhh",
-        scratch=[VMEM((1024, 128), F32), VMEM((2, 512, 512), F32)] + [VMEM((2, 256, 512), BF16)] * 2 + [VMEM((2, 512, 256), BF16)] * 2
-        + [VMEM((2, 256, 512), BF16)] * 2 + [VMEM((2, 256, 256), BF16)] * 2 + [VMEM((2, 256, 512), BF16)] * 2
+        (planes.reshape(1024, 128), yh, yl, green_hat.reshape(2, 512, 512)), "hhhh",
+        scratch=[VMEM((1024, 128), F32)] + [VMEM((2, 256, 512), BF16)] * 2 + [VMEM((2, 512, 512), F32)]
+        + [VMEM((2, 256, 256), BF16)] * 2 + [VMEM((2, 256, 512), BF16)] * 2
         + [VMEM((2, 512, 512), BF16)] * 2 + [VMEM((2, 256, 512), BF16)] * 2,
-        copies=8, flops=5 * 10**9, bytes_accessed=9 << 20, name="convolve", room=63,
+        copies=4, flops=5 * 10**9, bytes_accessed=9 << 20, name="convolve", room=63,
     )
     field = lax.all_to_all(back.reshape(256, 4, 128), BOTH, split_axis=0, concat_axis=0, tiled=True)
     index = near_source.reshape(CLASSES * 256)
     beside = call(
-        near, shape(128, 256), (index, left, own, right, near_table), "svvvv",
+        near, shape(128, 256), (index, even, own, odd, near_table), "svvvv",
         scratch=[VMEM((2304, 128), F32), VMEM((CLASSES, 256, 128), F32)],
         flops=10**10, bytes_accessed=40 << 20, name="near", room=16,
     )

time: 85 us -> 85.7 us (level)
  waiting for transfers between devices: 21.6 us -> 26.3 us
  starting transfers between devices: 38.2 us -> 34.6 us
    ppermute x4, starting transfers between devices: 10.5 us -> 4.64 us  [swap_pairs(): return lax.ppermute(array, axis, pairs + [(j, i) for i, j in pairs])]
    all_to_all x1, waiting for transfers between devices: 4.39 us -> 6.82 us  [per_device(): lax.all_to_all(sent.reshape(256, 4, 128), BOTH, split_axis=0, concat_axis...]
    ppermute x4, waiting for transfers between devices: 5.96 us -> 8.25 us  [swap_pairs(): return lax.ppermute(array, axis, pairs + [(j, i) for i, j in pairs])]
    all_to_all x1, starting transfers between devices: 11.1 us -> 13.3 us  [per_device(): lax.all_to_all(back.reshape(256, 4, 128), BOTH, split_axis=0, concat_axis...]
  transfers between devices with their start and end apart: 6 -> 6, of which waited for: 3 -> 3; matrix products, arithmetic and copies ran while one was open for 0% -> 0% of each run, Pallas kernels for 18% -> 17%
where the time goes in v10:
time: 85.7 us; the launch traced here: 85.4 us
  starting transfers between devices  34.6 us (40%)
  waiting for transfers between devices  26.3 us (31%)
  Pallas kernels  21.5 us (25%)
  local copies, waits for them, and re-layouts  2.19 us (3%)
    pallas_call x6, Pallas kernels, call(): pl.pallas_call(kernel, out_shape=outs, in_specs=[pl.BlockSpec(memory_spac...  21.5 us
    all_to_all x1, starting transfers between devices, per_device(): lax.all_to_all(sent.reshape(256, 4, 128), BOTH, split_axis=0, concat_axis...  16.7 us
    all_to_all x1, starting transfers between devices, per_device(): lax.all_to_all(back.reshape(256, 4, 128), BOTH, split_axis=0, concat_axis...  13.3 us
    all_to_all x1, waiting for transfers between devices, per_device(): lax.all_to_all(back.reshape(256, 4, 128), BOTH, split_axis=0, concat_axis...  11.2 us
    ppermute x4, waiting for transfers between devices, swap_pairs(): return lax.ppermute(array, axis, pairs + [(j, i) for i, j in pairs])  8.25 us
    all_to_all x1, waiting for transfers between devices, per_device(): lax.all_to_all(sent.reshape(256, 4, 128), BOTH, split_axis=0, concat_axis...  6.82 us
    ppermute x4, starting transfers between devices, swap_pairs(): return lax.ppermute(array, axis, pairs + [(j, i) for i, j in pairs])  4.64 us
    unnamed x18, local copies, waits for them, and re-layouts  2.19 us
  transfers between devices with their start and end apart: 6, of which 3 were waited for; matrix products, arithmetic and copies ran while one was open for 0% of the time, Pallas kernels for 17%

profile of v10, /device:TPU:1, one launch (start us, length us, event | category | flops | bytes accessed | tf_op | source)
XLA Modules:
  0.0 85.4 jit_solution(10690140194278214516)
XLA Ops:
  0.7 4.1 %to_grid.1 = (f32[1024,128]{1,0:T(8,128)}, f32[8,128]{1,0:T(8,128)}) custom-call(s32[1]{0:T(128)S(6)} %copy.16.count_ref, f32[128,256]{1,0:T(8,128)} %bitcast.9, s32[1,256]{1,0:T(1,128)} %bitcast.11, f32[64,64]{1,0:T(8,128)} %proj_ref.1, bf16[2048,128]{1,0:T(8,128)(2,1)} %constant.16.clone.expand_any, bf16[256,256]{1,0:T(8,128)(2,1)} %constant.17.clone.fh_any, ...), custom_call_target="tpu_custom_call" | custom-call | flops 2000000000 | bytes 2097152 | tf_op jit(solution)/shard_map/to_grid/pallas_call | solution.py:275
  4.8 16.7 %all-to-all-start = ((f32[256,4,128]{2,1,0:T(4,128)}), f32[256,4,128]{2,1,0:T(4,128)}, u32[]{:S(2)}, u32[]{:S(2)}) async-start(f32[256,4,128]{2,1,0:T(4,128)} %bitcast.13), calls=%async_computation | async-start | bytes 1048576 | tf_op jit(solution)/shard_map/all_to_all | solution.py:308
  21.5 0.0 copy-start.1
  21.5 0.7 copy-done.1
  22.2 0.1 turn.1.own_ref
  22.3 3.7 %collective-permute-start.1 = (f32[256,128]{1,0:T(8,128)S(1)}, f32[256,128]{1,0:T(8,128)S(1)}, u32[]{:S(2)}, u32[]{:S(2)}) collective-permute-start(f32[256,128]{1,0:T(8,128)S(1)} %turn.1.own_ref), channel_id=1, source_target_pairs={{1,2},{2,1},{5,6},{6,5},{9,10},{10,9},{13,14},{14,13},{17,18},{18,... | collective-permute-start | bytes 393224 | tf_op jit(solution)/shard_map/ppermute | solution.py:289
  25.9 0.1 collective-permute-start
  26.1 8.2 %collective-permute-done.1.odd_ref = f32[256,128]{1,0:T(8,128)S(1)} collective-permute-done((f32[256,128]{1,0:T(8,128)S(1)}, f32[256,128]{1,0:T(8,128)S(1)}, u32[]{:S(2)}, u32[]{:S(2)}) %collective-permute-start.1) | collective-permute-done | bytes 131104 | tf_op jit(solution)/shard_map/ppermute | solution.py:289
  34.3 0.0 collective-permute-done.even_ref
  34.3 0.7 collective-permute-start.3
  35.0 6.8 %all-to-all-done = f32[256,4,128]{2,1,0:T(4,128)} async-done(((f32[256,4,128]{2,1,0:T(4,128)}), f32[256,4,128]{2,1,0:T(4,128)}, u32[]{:S(2)}, u32[]{:S(2)}) %all-to-all-start) | async-done | bytes 524320 | tf_op jit(solution)/shard_map/all_to_all | solution.py:308
  41.9 0.2 collective-permute-start.2
  42.1 5.9 %convolve.1 = f32[1024,128]{1,0:T(8,128)} custom-call(f32[1024,128]{1,0:T(8,128)} %bitcast.3.in_any, bf16[2,256,512]{2,1,0:T(8,128)(2,1)} %constant.19.clone.th_any, bf16[2,256,512]{2,1,0:T(8,128)(2,1)} %constant.20.clone.tl_any, f32[2,512,512]{2,1,0:T(8,128)} %bitcast.15), custom_call_target="tpu_custom_call" | custom-call | flops 5000000000 | bytes 9437184 | tf_op jit(solution)/shard_map/convolve/pallas_call | solution.py:275
  48.0 13.3 %all-to-all-start.1 = ((f32[256,4,128]{2,1,0:T(4,128)}), f32[256,4,128]{2,1,0:T(4,128)S(1)}, u32[]{:S(2)}, u32[]{:S(2)}) async-start(f32[256,4,128]{2,1,0:T(4,128)} %bitcast.14), calls=%async_computation.1 | async-start | bytes 1048576 | tf_op jit(solution)/shard_map/all_to_all | solution.py:324
  61.3 0.0 copy-start.3
  61.3 0.0 copy-start.4
  61.3 0.0 collective-permute-done.3.odd_ref
  61.3 0.0 collective-permute-done.2.even_ref
  61.3 0.0 copy-start.2
  61.3 1.5 %copy-done.2 = f32[27,2,64,64]{3,2,1,0:T(8,128)S(1)} copy-done((f32[27,2,64,64]{3,2,1,0:T(8,128)S(1)}, f32[27,2,64,64]{3,2,1,0:T(8,128)}, u32[]{:S(2)}) %copy-start.2) | copy-done | bytes 884760
  62.8 8.4 %near.1.near_ref = f32[128,256]{1,0:T(8,128)S(1)} custom-call(s32[6912]{0:T(1024)S(1)} %reshape.34.index_ref, f32[768,128]{1,0:T(8,128)} %collective-permute-done.2.even_ref, f32[768,128]{1,0:T(8,128)S(1)} %join.1.own_ref, f32[768,128]{1,0:T(8,128)S(1)} %collective-permute-done.3.odd_ref, f32[27,2,64,64]{3,2,1,0:T(8,128)S(1)} %copy-done.2), custom_call_target="tpu_custom_call" | custom-call | flops 10000000000 | bytes 41943040 | tf_op jit(solution)/shard_map/near/pallas_call | solution.py:275
  71.3 11.2 %all-to-all-done.1 = f32[256,4,128]{2,1,0:T(4,128)S(1)} async-done(((f32[256,4,128]{2,1,0:T(4,128)}), f32[256,4,128]{2,1,0:T(4,128)S(1)}, u32[]{:S(2)}, u32[]{:S(2)}) %all-to-all-start.1) | async-done | bytes 524320 | tf_op jit(solution)/shard_map/all_to_all | solution.py:324
  82.5 0.0 copy-done.5
  82.5 2.9 %from_grid.1 = f32[128,256]{1,0:T(8,128)} custom-call(s32[1]{0:T(128)S(6)} %copy.16.count_ref, s32[1,256]{1,0:T(1,128)S(1)} %bitcast.12, f32[1024,128]{1,0:T(8,128)S(1)} %bitcast.8, f32[64,64]{1,0:T(8,128)S(1)} %copy-done.3, bf16[128,2048]{1,0:T(8,128)(2,1)S(1)} %copy-done.5, bf16[128,512]{1,0:T(8,128)(2,1)S(1)} %copy-done.7, ...), custom_call_target="tpu_custom_call" | custom-call | flops 2000000000 | bytes 2097152 | tf_op jit(solution)/shard_map/from_grid/pallas_call | solution.py:275
  (13 shorter events, 0.1 us)
Async XLA Ops:
  0.7 20.8 %copy-start = (f32[2,64,256]{2,1,0:T(8,128)S(1)}, f32[2,64,256]{2,1,0:T(8,128)}, u32[]{:S(2)}) copy-start(f32[2,64,256]{2,1,0:T(8,128)} %param.15) | copy-start | bytes 393220
  4.8 37.1 %all-to-all-start = ((f32[256,4,128]{2,1,0:T(4,128)}), f32[256,4,128]{2,1,0:T(4,128)}, u32[]{:S(2)}, u32[]{:S(2)}) async-start(f32[256,4,128]{2,1,0:T(4,128)} %bitcast.13), calls=%async_computation | async-start | bytes 1048576 | tf_op jit(solution)/shard_map/all_to_all | solution.py:308
  21.5 0.7 copy-start.1
  22.3 12.0 %collective-permute-start.1 = (f32[256,128]{1,0:T(8,128)S(1)}, f32[256,128]{1,0:T(8,128)S(1)}, u32[]{:S(2)}, u32[]{:S(2)}) collective-permute-start(f32[256,128]{1,0:T(8,128)S(1)} %turn.1.own_ref), channel_id=1, source_target_pairs={{1,2},{2,1},{5,6},{6,5},{9,10},{10,9},{13,14},{14,13},{17,18},{18,... | collective-permute-start | bytes 393224 | tf_op jit(solution)/shard_map/ppermute | solution.py:289
  25.9 8.4 %collective-permute-start = (f32[256,128]{1,0:T(8,128)S(1)}, f32[256,128]{1,0:T(8,128)S(1)}, u32[]{:S(2)}, u32[]{:S(2)}) collective-permute-start(f32[256,128]{1,0:T(8,128)S(1)} %turn.1.own_ref), channel_id=1, source_target_pairs={{0,1},{2,3},{1,0},{3,2},{4,5},{6,7},{5,4},{7,6},{8,9},{10,11},{9,8... | collective-permute-start | bytes 393224 | tf_op jit(solution)/shard_map/ppermute | solution.py:289
  34.3 27.0 %collective-permute-start.3 = (f32[768,128]{1,0:T(8,128)S(1)}, f32[768,128]{1,0:T(8,128)S(1)}, u32[]{:S(2)}, u32[]{:S(2)}) collective-permute-start(f32[768,128]{1,0:T(8,128)S(1)} %join.1.own_ref), channel_id=1, source_target_pairs={{4,8},{12,16},{20,24},{28,32},{36,40},{44,48},{52,56},{60,64},{68,... | collective-permute-start | bytes 1179656 | tf_op jit(solution)/shard_map/ppermute | solution.py:289
  41.9 19.5 %collective-permute-start.2 = (f32[768,128]{1,0:T(8,128)S(1)}, f32[768,128]{1,0:T(8,128)}, u32[]{:S(2)}, u32[]{:S(2)}) collective-permute-start(f32[768,128]{1,0:T(8,128)S(1)} %join.1.own_ref), channel_id=1, source_target_pairs={{0,4},{8,12},{16,20},{24,28},{32,36},{40,44},{48,52},{56,60},{64,6... | collective-permute-start | bytes 1179656 | tf_op jit(solution)/shard_map/ppermute | solution.py:289
  42.1 19.2 %copy-start.8 = (s32[27,256]{1,0:T(8,128)S(1)}, s32[27,256]{1,0:T(8,128)}, u32[]{:S(2)}) copy-start(s32[27,256]{1,0:T(8,128)} %param.21) | copy-start | bytes 82948
  48.0 34.5 %all-to-all-start.1 = ((f32[256,4,128]{2,1,0:T(4,128)}), f32[256,4,128]{2,1,0:T(4,128)S(1)}, u32[]{:S(2)}, u32[]{:S(2)}) async-start(f32[256,4,128]{2,1,0:T(4,128)} %bitcast.14), calls=%async_computation.1 | async-start | bytes 1048576 | tf_op jit(solution)/shard_map/all_to_all | solution.py:324
  61.3 21.2 %copy-start.3 = (f32[64,64]{1,0:T(8,128)S(1)}, f32[64,64]{1,0:T(8,128)}, u32[]{:S(2)}) copy-start(f32[64,64]{1,0:T(8,128)} %proj_ref.1) | copy-start | bytes 49156
  61.3 21.2 %copy-start.4 = (s32[256]{0:T(256)S(1)}, s32[256]{0:T(256)}, u32[]{:S(2)}) copy-start(s32[256]{0:T(256)} %param.19) | copy-start | bytes 3076
  61.3 1.5 %copy-start.2 = (f32[27,2,64,64]{3,2,1,0:T(8,128)S(1)}, f32[27,2,64,64]{3,2,1,0:T(8,128)}, u32[]{:S(2)}) copy-start(f32[27,2,64,64]{3,2,1,0:T(8,128)} %table_ref.1) | copy-start | bytes 2654212
  62.8 19.7 %copy-start.5 = (bf16[128,2048]{1,0:T(8,128)(2,1)S(1)}, bf16[128,2048]{1,0:T(8,128)(2,1)}, u32[]{:S(2)}) copy-start(bf16[128,2048]{1,0:T(8,128)(2,1)} %constant.21.clone.expand_ref) | copy-start | bytes 1572868
  62.8 19.7 %copy-start.6 = (bf16[128,512]{1,0:T(8,128)(2,1)S(1)}, bf16[128,512]{1,0:T(8,128)(2,1)}, u32[]{:S(2)}) copy-start(bf16[128,512]{1,0:T(8,128)(2,1)} %constant.23.clone.fl_ref) | copy-start | bytes 393220
  62.8 19.7 %copy-start.7 = (bf16[128,512]{1,0:T(8,128)(2,1)S(1)}, bf16[128,512]{1,0:T(8,128)(2,1)}, u32[]{:S(2)}) copy-start(bf16[128,512]{1,0:T(8,128)(2,1)} %constant.22.clone.fh_ref) | copy-start | bytes 393220

commit v11 on v10

--- a/solution.py
+++ b/solution.py
@@ -134,7 +134,8 @@
         out_ref[pl.ds(2 * e + 1, 256, stride=4), :] = planes[:, 128:]
 
 
-def turn(count_ref, charges_ref, after_ref, out_ref):
+def turn(count_ref, charges_ref, *refs):
+    out_ref = refs[-1]
     slots = lax.broadcasted_iota(jnp.int32, (128, 256), 1)
     out_ref[...] = jnp.where(slots < count_ref[0], charges_ref[...], 0.0).T
 
@@ -299,15 +300,17 @@
     shape = lambda *s: jax.ShapeDtypeStruct(s, F32)
 
     cells = charges.reshape(128, 256)
+    early = call(turn, shape(256, 128), (block_count, cells), "sv", bytes_accessed=1 << 20, name="turn_early", room=16)
+    odd = swap_pairs(early, "narrow", N, 1)
     sent, token = call(
         to_grid, (shape(1024, 128), shape(8, 128)), (block_count, cells, site, projection, np.ascontiguousarray(expand.T), fzh, fzl), "shhhhhh",
         scratch=[VMEM((128, 256), F32), VMEM((1, 256), jnp.int32), VMEM((64, 64), F32), VMEM((2048, 128), BF16)]
         + [VMEM((256, 256), BF16)] * 2,
         copies=6, flops=2 * 10**9, bytes_accessed=2 << 20, name="to_grid", room=63,
     )
+    sent, odd = lax.optimization_barrier((sent, odd))
     planes = lax.all_to_all(sent.reshape(256, 4, 128), BOTH, split_axis=0, concat_axis=0, tiled=True)
     masked = call(turn, shape(256, 128), (block_count, cells, token), "svv", bytes_accessed=1 << 20, name="turn", room=16)
-    odd = swap_pairs(masked, "narrow", N, 1)
     even = swap_pairs(masked, "narrow", N, 0)
     own = call(join, shape(768, 128), (even, masked, odd), "vvv", bytes_accessed=2 << 20, name="join", room=16)
     odd = swap_pairs(own, "wide", W, 1)

time: 85.7 us -> 82.3 us (0.960)
  starting transfers between devices: 34.6 us -> 28.8 us
  waiting for transfers between devices: 26.3 us -> 27.6 us
  local copies, waits for them, and re-layouts: 2.19 us -> 3.09 us
    all_to_all x1, waiting for transfers between devices: 6.82 us -> 15.4 us  [per_device(): lax.all_to_all(sent.reshape(256, 4, 128), BOTH, split_axis=0, concat_axis...]
    ppermute x4, waiting for transfers between devices: 8.25 us -> 0.99 us  [swap_pairs(): return lax.ppermute(array, axis, pairs + [(j, i) for i, j in pairs])]
    all_to_all x1, starting transfers between devices: 13.3 us -> 6.05 us  [per_device(): lax.all_to_all(back.reshape(256, 4, 128), BOTH, split_axis=0, concat_axis...]
    ppermute x4, starting transfers between devices: 4.64 us -> 8.4 us  [swap_pairs(): return lax.ppermute(array, axis, pairs + [(j, i) for i, j in pairs])]
    all_to_all x1, starting transfers between devices: 16.7 us -> 14.4 us  [per_device(): lax.all_to_all(sent.reshape(256, 4, 128), BOTH, split_axis=0, concat_axis...]
    unnamed x18 -> x20, local copies, waits for them, and re-layouts: 2.19 us -> 3.09 us
    pallas_call x6 -> x7, Pallas kernels: 21.5 us -> 21.6 us  [call(): pl.pallas_call(kernel, out_shape=outs, in_specs=[pl.BlockSpec(memory_spac...]
  transfers between devices with their start and end apart: 6 -> 6, of which waited for: 3 -> 3; matrix products, arithmetic and copies ran while one was open for 0% -> 0% of each run, Pallas kernels for 17% -> 23%
where the time goes in v11:
time: 82.3 us; the launch traced here: 81.9 us
  starting transfers between devices  28.8 us (35%)
  waiting for transfers between devices  27.6 us (34%)
  Pallas kernels  21.6 us (26%)
  local copies, waits for them, and re-layouts  3.09 us (4%)
  between operations  0.85 us (1%)
    pallas_call x7, Pallas kernels, call(): pl.pallas_call(kernel, out_shape=outs, in_specs=[pl.BlockSpec(memory_spac...  21.6 us
    all_to_all x1, waiting for transfers between devices, per_device(): lax.all_to_all(sent.reshape(256, 4, 128), BOTH, split_axis=0, concat_axis...  15.4 us
    all_to_all x1, starting transfers between devices, per_device(): lax.all_to_all(sent.reshape(256, 4, 128), BOTH, split_axis=0, concat_axis...  14.4 us
    all_to_all x1, waiting for transfers between devices, per_device(): lax.all_to_all(back.reshape(256, 4, 128), BOTH, split_axis=0, concat_axis...  11.2 us
    ppermute x4, starting transfers between devices, swap_pairs(): return lax.ppermute(array, axis, pairs + [(j, i) for i, j in pairs])  8.4 us
    all_to_all x1, starting transfers between devices, per_device(): lax.all_to_all(back.reshape(256, 4, 128), BOTH, split_axis=0, concat_axis...  6.05 us
    unnamed x20, local copies, waits for them, and re-layouts  3.09 us
  transfers between devices with their start and end apart: 6, of which 3 were waited for; matrix products, arithmetic and copies ran while one was open for 0% of the time, Pallas kernels for 23%

profile of v11, /device:TPU:1, one launch (start us, length us, event | category | flops | bytes accessed | tf_op | source)
XLA Modules:
  0.0 81.9 jit_solution(2700889473035670072)
XLA Ops:
  0.7 0.0 copy-start
  0.7 0.9 %copy-done = f32[2,64,256]{2,1,0:T(8,128)S(1)} copy-done((f32[2,64,256]{2,1,0:T(8,128)S(1)}, f32[2,64,256]{2,1,0:T(8,128)}, u32[]{:S(2)}) %copy-start) | copy-done | bytes 131096
  1.6 0.1 turn_early.1
  1.7 4.9 %collective-permute-start.1 = (f32[256,128]{1,0:T(8,128)S(1)}, f32[256,128]{1,0:T(8,128)S(1)}, u32[]{:S(2)}, u32[]{:S(2)}) collective-permute-start(f32[256,128]{1,0:T(8,128)S(1)} %turn_early.1), channel_id=1, source_target_pairs={{1,2},{2,1},{5,6},{6,5},{9,10},{10,9},{13,14},{14,13},{17,18},{18,... | collective-permute-start | bytes 393224 | tf_op jit(solution)/shard_map/ppermute | solution.py:290
  6.6 0.0 copy-start.1
  6.6 4.1 %to_grid.1 = (f32[1024,128]{1,0:T(8,128)}, f32[8,128]{1,0:T(8,128)}) custom-call(s32[1]{0:T(128)S(6)} %copy.16.count_ref, f32[128,256]{1,0:T(8,128)} %bitcast.9, s32[1,256]{1,0:T(1,128)} %bitcast.12, f32[64,64]{1,0:T(8,128)} %proj_ref.1, bf16[2048,128]{1,0:T(8,128)(2,1)} %constant.16.clone.expand_any, bf16[256,256]{1,0:T(8,128)(2,1)} %constant.17.clone.fh_any, ...), custom_call_target="tpu_custom_call" | custom-call | flops 2000000000 | bytes 2097152 | tf_op jit(solution)/shard_map/to_grid/pallas_call | solution.py:276
  10.8 14.4 %all-to-all-start = ((f32[256,4,128]{2,1,0:T(4,128)}), f32[256,4,128]{2,1,0:T(4,128)}, u32[]{:S(2)}, u32[]{:S(2)}) async-start(f32[256,4,128]{2,1,0:T(4,128)} %bitcast.14), calls=%async_computation | async-start | bytes 1048576 | tf_op jit(solution)/shard_map/all_to_all | solution.py:312
  25.2 0.0 copy-start.2
  25.2 0.7 copy-done.2
  25.9 0.1 turn.1.own_ref
  26.0 2.3 %collective-permute-start = (f32[256,128]{1,0:T(8,128)S(1)}, f32[256,128]{1,0:T(8,128)S(1)}, u32[]{:S(2)}, u32[]{:S(2)}) collective-permute-start(f32[256,128]{1,0:T(8,128)S(1)} %turn.1.own_ref), channel_id=1, source_target_pairs={{0,1},{2,3},{1,0},{3,2},{4,5},{6,7},{5,4},{7,6},{8,9},{10,11},{9,8... | collective-permute-start | bytes 393224 | tf_op jit(solution)/shard_map/ppermute | solution.py:290
  28.3 1.0 %collective-permute-done.even_ref = f32[256,128]{1,0:T(8,128)S(1)} collective-permute-done((f32[256,128]{1,0:T(8,128)S(1)}, f32[256,128]{1,0:T(8,128)S(1)}, u32[]{:S(2)}, u32[]{:S(2)}) %collective-permute-start) | collective-permute-done | bytes 131104 | tf_op jit(solution)/shard_map/ppermute | solution.py:290
  29.3 0.7 collective-permute-start.3
  30.0 15.4 %all-to-all-done = f32[256,4,128]{2,1,0:T(4,128)} async-done(((f32[256,4,128]{2,1,0:T(4,128)}), f32[256,4,128]{2,1,0:T(4,128)}, u32[]{:S(2)}, u32[]{:S(2)}) %all-to-all-start) | async-done | bytes 524320 | tf_op jit(solution)/shard_map/all_to_all | solution.py:312
  45.4 0.5 collective-permute-start.2
  45.9 5.9 %convolve.1 = f32[1024,128]{1,0:T(8,128)} custom-call(f32[1024,128]{1,0:T(8,128)} %bitcast.3.in_any, bf16[2,256,512]{2,1,0:T(8,128)(2,1)} %constant.19.clone.th_any, bf16[2,256,512]{2,1,0:T(8,128)(2,1)} %constant.20.clone.tl_any, f32[2,512,512]{2,1,0:T(8,128)} %bitcast.16), custom_call_target="tpu_custom_call" | custom-call | flops 5000000000 | bytes 9437184 | tf_op jit(solution)/shard_map/convolve/pallas_call | solution.py:276
  51.8 6.0 %all-to-all-start.1 = ((f32[256,4,128]{2,1,0:T(4,128)}), f32[256,4,128]{2,1,0:T(4,128)S(1)}, u32[]{:S(2)}, u32[]{:S(2)}) async-start(f32[256,4,128]{2,1,0:T(4,128)} %bitcast.15), calls=%async_computation.1 | async-start | bytes 1048576 | tf_op jit(solution)/shard_map/all_to_all | solution.py:327
  57.9 0.0 copy-start.4
  57.9 0.0 copy-start.5
  57.9 0.0 copy-start.3
  57.9 1.5 %copy-done.3 = f32[27,2,64,64]{3,2,1,0:T(8,128)S(1)} copy-done((f32[27,2,64,64]{3,2,1,0:T(8,128)S(1)}, f32[27,2,64,64]{3,2,1,0:T(8,128)}, u32[]{:S(2)}) %copy-start.3) | copy-done | bytes 884760
  59.4 8.4 %near.1.near_ref = f32[128,256]{1,0:T(8,128)S(1)} custom-call(s32[6912]{0:T(1024)S(1)} %reshape.34.index_ref, f32[768,128]{1,0:T(8,128)} %collective-permute-done.2.even_ref, f32[768,128]{1,0:T(8,128)S(1)} %join.1.own_ref, f32[768,128]{1,0:T(8,128)S(1)} %collective-permute-done.3.odd_ref, f32[27,2,64,64]{3,2,1,0:T(8,128)S(1)} %copy-done.3), custom_call_target="tpu_custom_call" | custom-call | flops 10000000000 | bytes 41943040 | tf_op jit(solution)/shard_map/near/pallas_call | solution.py:276
  67.8 11.2 %all-to-all-done.1 = f32[256,4,128]{2,1,0:T(4,128)S(1)} async-done(((f32[256,4,128]{2,1,0:T(4,128)}), f32[256,4,128]{2,1,0:T(4,128)S(1)}, u32[]{:S(2)}, u32[]{:S(2)}) %all-to-all-start.1) | async-done | bytes 524320 | tf_op jit(solution)/shard_map/all_to_all | solution.py:327
  79.1 2.9 %from_grid.1 = f32[128,256]{1,0:T(8,128)} custom-call(s32[1]{0:T(128)S(6)} %copy.16.count_ref, s32[1,256]{1,0:T(1,128)S(1)} %bitcast.13, f32[1024,128]{1,0:T(8,128)S(1)} %bitcast.8, f32[64,64]{1,0:T(8,128)S(1)} %copy-done.4, bf16[128,2048]{1,0:T(8,128)(2,1)S(1)} %copy-done.6, bf16[128,512]{1,0:T(8,128)(2,1)S(1)} %copy-done.8, ...), custom_call_target="tpu_custom_call" | custom-call | flops 2000000000 | bytes 2097152 | tf_op jit(solution)/shard_map/from_grid/pallas_call | solution.py:276
  (16 shorter events, 0.1 us)
Async XLA Ops:
  0.7 0.9 %copy-start = (f32[2,64,256]{2,1,0:T(8,128)S(1)}, f32[2,64,256]{2,1,0:T(8,128)}, u32[]{:S(2)}) copy-start(f32[2,64,256]{2,1,0:T(8,128)} %param.15) | copy-start | bytes 393220
  1.7 9.1 %collective-permute-start.1 = (f32[256,128]{1,0:T(8,128)S(1)}, f32[256,128]{1,0:T(8,128)S(1)}, u32[]{:S(2)}, u32[]{:S(2)}) collective-permute-start(f32[256,128]{1,0:T(8,128)S(1)} %turn_early.1), channel_id=1, source_target_pairs={{1,2},{2,1},{5,6},{6,5},{9,10},{10,9},{13,14},{14,13},{17,18},{18,... | collective-permute-start | bytes 393224 | tf_op jit(solution)/shard_map/ppermute | solution.py:290
  6.6 18.5 %copy-start.1 = (f32[2,64,256]{2,1,0:T(8,128)S(1)}, f32[2,64,256]{2,1,0:T(8,128)}, u32[]{:S(2)}) copy-start(f32[2,64,256]{2,1,0:T(8,128)} %param.15) | copy-start | bytes 393220
  10.8 34.6 %all-to-all-start = ((f32[256,4,128]{2,1,0:T(4,128)}), f32[256,4,128]{2,1,0:T(4,128)}, u32[]{:S(2)}, u32[]{:S(2)}) async-start(f32[256,4,128]{2,1,0:T(4,128)} %bitcast.14), calls=%async_computation | async-start | bytes 1048576 | tf_op jit(solution)/shard_map/all_to_all | solution.py:312
  25.2 0.7 copy-start.2
  26.0 3.3 %collective-permute-start = (f32[256,128]{1,0:T(8,128)S(1)}, f32[256,128]{1,0:T(8,128)S(1)}, u32[]{:S(2)}, u32[]{:S(2)}) collective-permute-start(f32[256,128]{1,0:T(8,128)S(1)} %turn.1.own_ref), channel_id=1, source_target_pairs={{0,1},{2,3},{1,0},{3,2},{4,5},{6,7},{5,4},{7,6},{8,9},{10,11},{9,8... | collective-permute-start | bytes 393224 | tf_op jit(solution)/shard_map/ppermute | solution.py:290
  29.3 28.6 %collective-permute-start.3 = (f32[768,128]{1,0:T(8,128)S(1)}, f32[768,128]{1,0:T(8,128)S(1)}, u32[]{:S(2)}, u32[]{:S(2)}) collective-permute-start(f32[768,128]{1,0:T(8,128)S(1)} %join.1.own_ref), channel_id=1, source_target_pairs={{4,8},{12,16},{20,24},{28,32},{36,40},{44,48},{52,56},{60,64},{68,... | collective-permute-start | bytes 1179656 | tf_op jit(solution)/shard_map/ppermute | solution.py:290
  45.4 12.5 %collective-permute-start.2 = (f32[768,128]{1,0:T(8,128)S(1)}, f32[768,128]{1,0:T(8,128)}, u32[]{:S(2)}, u32[]{:S(2)}) collective-permute-start(f32[768,128]{1,0:T(8,128)S(1)} %join.1.own_ref), channel_id=1, source_target_pairs={{0,4},{8,12},{16,20},{24,28},{32,36},{40,44},{48,52},{56,60},{64,6... | collective-permute-start | bytes 1179656 | tf_op jit(solution)/shard_map/ppermute | solution.py:290
  45.9 12.0 %copy-start.9 = (s32[27,256]{1,0:T(8,128)S(1)}, s32[27,256]{1,0:T(8,128)}, u32[]{:S(2)}) copy-start(s32[27,256]{1,0:T(8,128)} %param.21) | copy-start | bytes 82948
  51.8 27.3 %all-to-all-start.1 = ((f32[256,4,128]{2,1,0:T(4,128)}), f32[256,4,128]{2,1,0:T(4,128)S(1)}, u32[]{:S(2)}, u32[]{:S(2)}) async-start(f32[256,4,128]{2,1,0:T(4,128)} %bitcast.15), calls=%async_computation.1 | async-start | bytes 1048576 | tf_op jit(solution)/shard_map/all_to_all | solution.py:327
  57.9 21.2 %copy-start.4 = (f32[64,64]{1,0:T(8,128)S(1)}, f32[64,64]{1,0:T(8,128)}, u32[]{:S(2)}) copy-start(f32[64,64]{1,0:T(8,128)} %proj_ref.1) | copy-start | bytes 49156
  57.9 21.2 %copy-start.5 = (s32[256]{0:T(256)S(1)}, s32[256]{0:T(256)}, u32[]{:S(2)}) copy-start(s32[256]{0:T(256)} %param.19) | copy-start | bytes 3076
  57.9 1.5 %copy-start.3 = (f32[27,2,64,64]{3,2,1,0:T(8,128)S(1)}, f32[27,2,64,64]{3,2,1,0:T(8,128)}, u32[]{:S(2)}) copy-start(f32[27,2,64,64]{3,2,1,0:T(8,128)} %table_ref.1) | copy-start | bytes 2654212
  59.4 19.7 %copy-start.6 = (bf16[128,2048]{1,0:T(8,128)(2,1)S(1)}, bf16[128,2048]{1,0:T(8,128)(2,1)}, u32[]{:S(2)}) copy-start(bf16[128,2048]{1,0:T(8,128)(2,1)} %constant.21.clone.expand_ref) | copy-start | bytes 1572868
  59.4 19.7 %copy-start.7 = (bf16[128,512]{1,0:T(8,128)(2,1)S(1)}, bf16[128,512]{1,0:T(8,128)(2,1)}, u32[]{:S(2)}) copy-start(bf16[128,512]{1,0:T(8,128)(2,1)} %constant.23.clone.fl_ref) | copy-start | bytes 393220
  59.4 19.7 %copy-start.8 = (bf16[128,512]{1,0:T(8,128)(2,1)S(1)}, bf16[128,512]{1,0:T(8,128)(2,1)}, u32[]{:S(2)}) copy-start(bf16[128,512]{1,0:T(8,128)(2,1)} %constant.22.clone.fh_ref) | copy-start | bytes 393220

commit v12 on v11

--- a/solution.py
+++ b/solution.py
@@ -314,8 +314,7 @@
     even = swap_pairs(masked, "narrow", N, 0)
     own = call(join, shape(768, 128), (even, masked, odd), "vvv", bytes_accessed=2 << 20, name="join", room=16)
     odd = swap_pairs(own, "wide", W, 1)
-    later, planes = lax.optimization_barrier((own, planes))
-    even = swap_pairs(later, "wide", W, 0)
+    even = swap_pairs(own, "wide", W, 0)
     back = call(
         convolve, shape(1024, 128),
         (planes.reshape(1024, 128), yh, yl, green_hat.reshape(2, 512, 512)), "hhhh",

time: 82.3 us -> 81.5 us (level)
  waiting for transfers between devices: 27.6 us -> 25.7 us
  starting transfers between devices: 28.8 us -> 29.9 us
    all_to_all x1, waiting for transfers between devices: 15.4 us -> 13.4 us  [per_device(): lax.all_to_all(sent.reshape(256, 4, 128), BOTH, split_axis=0, concat_axis...]
    ppermute x4, starting transfers between devices: 8.4 us -> 9.95 us  [swap_pairs(): return lax.ppermute(array, axis, pairs + [(j, i) for i, j in pairs])]
where the time goes in v12:
time: 81.5 us; the launch traced here: 81.1 us
  starting transfers between devices  29.9 us (37%)
  waiting for transfers between devices  25.7 us (32%)
  Pallas kernels  21.6 us (27%)
  local copies, waits for them, and re-layouts  3.09 us (4%)
  between operations  0.85 us (1%)
    pallas_call x7, Pallas kernels, call(): pl.pallas_call(kernel, out_shape=outs, in_specs=[pl.BlockSpec(memory_spac...  21.6 us
    all_to_all x1, starting transfers between devices, per_device(): lax.all_to_all(sent.reshape(256, 4, 128), BOTH, split_axis=0, concat_axis...  14.4 us
    all_to_all x1, waiting for transfers between devices, per_device(): lax.all_to_all(sent.reshape(256, 4, 128), BOTH, split_axis=0, concat_axis...  13.4 us
    all_to_all x1, waiting for transfers between devices, per_device(): lax.all_to_all(back.reshape(256, 4, 128), BOTH, split_axis=0, concat_axis...  11.3 us
    ppermute x4, starting transfers between devices, swap_pairs(): return lax.ppermute(array, axis, pairs + [(j, i) for i, j in pairs])  9.95 us
    all_to_all x1, starting transfers between devices, per_device(): lax.all_to_all(back.reshape(256, 4, 128), BOTH, split_axis=0, concat_axis...  5.57 us
    unnamed x20, local copies, waits for them, and re-layouts  3.09 us
  transfers between devices with their start and end apart: 6, of which 3 were waited for; matrix products, arithmetic and copies ran while one was open for 0% of the time, Pallas kernels for 23%

profile of v12, /device:TPU:1, one launch (start us, length us, event | category | flops | bytes accessed | tf_op | source)
XLA Modules:
  0.0 81.1 jit_solution(7606321698170250840)
XLA Ops:
  0.7 0.0 copy-start
  0.7 0.9 %copy-done = f32[2,64,256]{2,1,0:T(8,128)S(1)} copy-done((f32[2,64,256]{2,1,0:T(8,128)S(1)}, f32[2,64,256]{2,1,0:T(8,128)}, u32[]{:S(2)}) %copy-start) | copy-done | bytes 131096
  1.6 0.1 turn_early.1
  1.7 4.9 %collective-permute-start = (f32[256,128]{1,0:T(8,128)S(1)}, f32[256,128]{1,0:T(8,128)S(1)}, u32[]{:S(2)}, u32[]{:S(2)}) collective-permute-start(f32[256,128]{1,0:T(8,128)S(1)} %turn_early.1), channel_id=1, source_target_pairs={{1,2},{2,1},{5,6},{6,5},{9,10},{10,9},{13,14},{14,13},{17,18},{18,... | collective-permute-start | bytes 393224 | tf_op jit(solution)/shard_map/ppermute | solution.py:290
  6.6 0.0 copy-start.1
  6.6 4.1 %to_grid.1 = (f32[1024,128]{1,0:T(8,128)}, f32[8,128]{1,0:T(8,128)}) custom-call(s32[1]{0:T(128)S(6)} %copy.16.count_ref, f32[128,256]{1,0:T(8,128)} %bitcast.9, s32[1,256]{1,0:T(1,128)} %bitcast.12, f32[64,64]{1,0:T(8,128)} %proj_ref.1, bf16[2048,128]{1,0:T(8,128)(2,1)} %constant.16.clone.expand_any, bf16[256,256]{1,0:T(8,128)(2,1)} %constant.17.clone.fh_any, ...), custom_call_target="tpu_custom_call" | custom-call | flops 2000000000 | bytes 2097152 | tf_op jit(solution)/shard_map/to_grid/pallas_call | solution.py:276
  10.8 14.4 %all-to-all-start = ((f32[256,4,128]{2,1,0:T(4,128)}), f32[256,4,128]{2,1,0:T(4,128)}, u32[]{:S(2)}, u32[]{:S(2)}) async-start(f32[256,4,128]{2,1,0:T(4,128)} %bitcast.14), calls=%async_computation | async-start | bytes 1048576 | tf_op jit(solution)/shard_map/all_to_all | solution.py:312
  25.2 0.0 copy-start.2
  25.2 0.7 copy-done.2
  25.9 0.1 turn.1.own_ref
  26.0 2.3 %collective-permute-start.1 = (f32[256,128]{1,0:T(8,128)S(1)}, f32[256,128]{1,0:T(8,128)S(1)}, u32[]{:S(2)}, u32[]{:S(2)}) collective-permute-start(f32[256,128]{1,0:T(8,128)S(1)} %turn.1.own_ref), channel_id=1, source_target_pairs={{0,1},{2,3},{1,0},{3,2},{4,5},{6,7},{5,4},{7,6},{8,9},{10,11},{9,8... | collective-permute-start | bytes 393224 | tf_op jit(solution)/shard_map/ppermute | solution.py:290
  28.3 1.0 %collective-permute-done.1.even_ref = f32[256,128]{1,0:T(8,128)S(1)} collective-permute-done((f32[256,128]{1,0:T(8,128)S(1)}, f32[256,128]{1,0:T(8,128)S(1)}, u32[]{:S(2)}, u32[]{:S(2)}) %collective-permute-start.1) | collective-permute-done | bytes 131104 | tf_op jit(solution)/shard_map/ppermute | solution.py:290
  29.3 0.7 collective-permute-start.3
  30.0 2.0 %collective-permute-start.2 = (f32[768,128]{1,0:T(8,128)S(1)}, f32[768,128]{1,0:T(8,128)}, u32[]{:S(2)}, u32[]{:S(2)}) collective-permute-start(f32[768,128]{1,0:T(8,128)S(1)} %join.1.own_ref), channel_id=1, source_target_pairs={{0,4},{8,12},{16,20},{24,28},{32,36},{40,44},{48,52},{56,60},{64,6... | collective-permute-start | bytes 1179656 | tf_op jit(solution)/shard_map/ppermute | solution.py:290
  32.0 13.4 %all-to-all-done = f32[256,4,128]{2,1,0:T(4,128)} async-done(((f32[256,4,128]{2,1,0:T(4,128)}), f32[256,4,128]{2,1,0:T(4,128)}, u32[]{:S(2)}, u32[]{:S(2)}) %all-to-all-start) | async-done | bytes 524320 | tf_op jit(solution)/shard_map/all_to_all | solution.py:312
  45.4 5.9 %convolve.1 = f32[1024,128]{1,0:T(8,128)} custom-call(f32[1024,128]{1,0:T(8,128)} %bitcast.3.in_any, bf16[2,256,512]{2,1,0:T(8,128)(2,1)} %constant.19.clone.th_any, bf16[2,256,512]{2,1,0:T(8,128)(2,1)} %constant.20.clone.tl_any, f32[2,512,512]{2,1,0:T(8,128)} %bitcast.16), custom_call_target="tpu_custom_call" | custom-call | flops 5000000000 | bytes 9437184 | tf_op jit(solution)/shard_map/convolve/pallas_call | solution.py:276
  51.3 5.6 %all-to-all-start.1 = ((f32[256,4,128]{2,1,0:T(4,128)}), f32[256,4,128]{2,1,0:T(4,128)S(1)}, u32[]{:S(2)}, u32[]{:S(2)}) async-start(f32[256,4,128]{2,1,0:T(4,128)} %bitcast.15), calls=%async_computation.1 | async-start | bytes 1048576 | tf_op jit(solution)/shard_map/all_to_all | solution.py:326
  56.9 0.0 copy-start.4
  56.9 0.0 copy-start.5
  57.0 0.0 copy-start.3
  57.0 1.5 %copy-done.3 = f32[27,2,64,64]{3,2,1,0:T(8,128)S(1)} copy-done((f32[27,2,64,64]{3,2,1,0:T(8,128)S(1)}, f32[27,2,64,64]{3,2,1,0:T(8,128)}, u32[]{:S(2)}) %copy-start.3) | copy-done | bytes 884760
  58.5 8.4 %near.1.near_ref = f32[128,256]{1,0:T(8,128)S(1)} custom-call(s32[6912]{0:T(1024)S(1)} %reshape.34.index_ref, f32[768,128]{1,0:T(8,128)} %collective-permute-done.2.even_ref, f32[768,128]{1,0:T(8,128)S(1)} %join.1.own_ref, f32[768,128]{1,0:T(8,128)S(1)} %collective-permute-done.3.odd_ref, f32[27,2,64,64]{3,2,1,0:T(8,128)S(1)} %copy-done.3), custom_call_target="tpu_custom_call" | custom-call | flops 10000000000 | bytes 41943040 | tf_op jit(solution)/shard_map/near/pallas_call | solution.py:276
  66.9 11.3 %all-to-all-done.1 = f32[256,4,128]{2,1,0:T(4,128)S(1)} async-done(((f32[256,4,128]{2,1,0:T(4,128)}), f32[256,4,128]{2,1,0:T(4,128)S(1)}, u32[]{:S(2)}, u32[]{:S(2)}) %all-to-all-start.1) | async-done | bytes 524320 | tf_op jit(solution)/shard_map/all_to_all | solution.py:326
  78.2 2.8 %from_grid.1 = f32[128,256]{1,0:T(8,128)} custom-call(s32[1]{0:T(128)S(6)} %copy.16.count_ref, s32[1,256]{1,0:T(1,128)S(1)} %bitcast.13, f32[1024,128]{1,0:T(8,128)S(1)} %bitcast.8, f32[64,64]{1,0:T(8,128)S(1)} %copy-done.4, bf16[128,2048]{1,0:T(8,128)(2,1)S(1)} %copy-done.6, bf16[128,512]{1,0:T(8,128)(2,1)S(1)} %copy-done.8, ...), custom_call_target="tpu_custom_call" | custom-call | flops 2000000000 | bytes 2097152 | tf_op jit(solution)/shard_map/from_grid/pallas_call | solution.py:276
  (16 shorter events, 0.1 us)
Async XLA Ops:
  0.7 0.9 %copy-start = (f32[2,64,256]{2,1,0:T(8,128)S(1)}, f32[2,64,256]{2,1,0:T(8,128)}, u32[]{:S(2)}) copy-start(f32[2,64,256]{2,1,0:T(8,128)} %param.15) | copy-start | bytes 393220
  1.7 9.1 %collective-permute-start = (f32[256,128]{1,0:T(8,128)S(1)}, f32[256,128]{1,0:T(8,128)S(1)}, u32[]{:S(2)}, u32[]{:S(2)}) collective-permute-start(f32[256,128]{1,0:T(8,128)S(1)} %turn_early.1), channel_id=1, source_target_pairs={{1,2},{2,1},{5,6},{6,5},{9,10},{10,9},{13,14},{14,13},{17,18},{18,... | collective-permute-start | bytes 393224 | tf_op jit(solution)/shard_map/ppermute | solution.py:290
  6.6 18.5 %copy-start.1 = (f32[2,64,256]{2,1,0:T(8,128)S(1)}, f32[2,64,256]{2,1,0:T(8,128)}, u32[]{:S(2)}) copy-start(f32[2,64,256]{2,1,0:T(8,128)} %param.15) | copy-start | bytes 393220
  10.8 34.6 %all-to-all-start = ((f32[256,4,128]{2,1,0:T(4,128)}), f32[256,4,128]{2,1,0:T(4,128)}, u32[]{:S(2)}, u32[]{:S(2)}) async-start(f32[256,4,128]{2,1,0:T(4,128)} %bitcast.14), calls=%async_computation | async-start | bytes 1048576 | tf_op jit(solution)/shard_map/all_to_all | solution.py:312
  25.2 0.7 copy-start.2
  26.0 3.3 %collective-permute-start.1 = (f32[256,128]{1,0:T(8,128)S(1)}, f32[256,128]{1,0:T(8,128)S(1)}, u32[]{:S(2)}, u32[]{:S(2)}) collective-permute-start(f32[256,128]{1,0:T(8,128)S(1)} %turn.1.own_ref), channel_id=1, source_target_pairs={{0,1},{2,3},{1,0},{3,2},{4,5},{6,7},{5,4},{7,6},{8,9},{10,11},{9,8... | collective-permute-start | bytes 393224 | tf_op jit(solution)/shard_map/ppermute | solution.py:290
  29.3 27.7 %collective-permute-start.3 = (f32[768,128]{1,0:T(8,128)S(1)}, f32[768,128]{1,0:T(8,128)S(1)}, u32[]{:S(2)}, u32[]{:S(2)}) collective-permute-start(f32[768,128]{1,0:T(8,128)S(1)} %join.1.own_ref), channel_id=1, source_target_pairs={{4,8},{12,16},{20,24},{28,32},{36,40},{44,48},{52,56},{60,64},{68,... | collective-permute-start | bytes 1179656 | tf_op jit(solution)/shard_map/ppermute | solution.py:290
  30.0 27.0 %collective-permute-start.2 = (f32[768,128]{1,0:T(8,128)S(1)}, f32[768,128]{1,0:T(8,128)}, u32[]{:S(2)}, u32[]{:S(2)}) collective-permute-start(f32[768,128]{1,0:T(8,128)S(1)} %join.1.own_ref), channel_id=1, source_target_pairs={{0,4},{8,12},{16,20},{24,28},{32,36},{40,44},{48,52},{56,60},{64,6... | collective-permute-start | bytes 1179656 | tf_op jit(solution)/shard_map/ppermute | solution.py:290
  45.4 11.5 %copy-start.9 = (s32[27,256]{1,0:T(8,128)S(1)}, s32[27,256]{1,0:T(8,128)}, u32[]{:S(2)}) copy-start(s32[27,256]{1,0:T(8,128)} %param.21) | copy-start | bytes 82948
  51.3 26.9 %all-to-all-start.1 = ((f32[256,4,128]{2,1,0:T(4,128)}), f32[256,4,128]{2,1,0:T(4,128)S(1)}, u32[]{:S(2)}, u32[]{:S(2)}) async-start(f32[256,4,128]{2,1,0:T(4,128)} %bitcast.15), calls=%async_computation.1 | async-start | bytes 1048576 | tf_op jit(solution)/shard_map/all_to_all | solution.py:326
  56.9 21.3 %copy-start.4 = (f32[64,64]{1,0:T(8,128)S(1)}, f32[64,64]{1,0:T(8,128)}, u32[]{:S(2)}) copy-start(f32[64,64]{1,0:T(8,128)} %proj_ref.1) | copy-start | bytes 49156
  56.9 21.3 %copy-start.5 = (s32[256]{0:T(256)S(1)}, s32[256]{0:T(256)}, u32[]{:S(2)}) copy-start(s32[256]{0:T(256)} %param.19) | copy-start | bytes 3076
  57.0 1.5 %copy-start.3 = (f32[27,2,64,64]{3,2,1,0:T(8,128)S(1)}, f32[27,2,64,64]{3,2,1,0:T(8,128)}, u32[]{:S(2)}) copy-start(f32[27,2,64,64]{3,2,1,0:T(8,128)} %table_ref.1) | copy-start | bytes 2654212
  58.4 19.8 %copy-start.6 = (bf16[128,2048]{1,0:T(8,128)(2,1)S(1)}, bf16[128,2048]{1,0:T(8,128)(2,1)}, u32[]{:S(2)}) copy-start(bf16[128,2048]{1,0:T(8,128)(2,1)} %constant.21.clone.expand_ref) | copy-start | bytes 1572868
  58.4 19.8 %copy-start.7 = (bf16[128,512]{1,0:T(8,128)(2,1)S(1)}, bf16[128,512]{1,0:T(8,128)(2,1)}, u32[]{:S(2)}) copy-start(bf16[128,512]{1,0:T(8,128)(2,1)} %constant.23.clone.fl_ref) | copy-start | bytes 393220
  58.5 19.8 %copy-start.8 = (bf16[128,512]{1,0:T(8,128)(2,1)S(1)}, bf16[128,512]{1,0:T(8,128)(2,1)}, u32[]{:S(2)}) copy-start(bf16[128,512]{1,0:T(8,128)(2,1)} %constant.22.clone.fh_ref) | copy-start | bytes 393220

commit v13 on v12

--- a/solution.py
+++ b/solution.py
@@ -147,10 +147,9 @@
     out_ref[pl.ds(pl.multiple_of(512 * last, 512), 256), :] = odd_ref[...]
 
 
-def convolve(in_any, th_any, tl_any, green_any, out_ref,
-             in_ref, th, tl, green_ref, ah, al, sh, sl, qh, ql, bh, bl, sems):
-    arrived, *copies = fetch([(in_any, in_ref), (th_any, th), (tl_any, tl), (green_any, green_ref)], sems)
-    arrived.wait()
+def convolve(in_ref, th_any, tl_any, green_any, out_ref,
+             th, tl, green_ref, ah, al, sh, sl, qh, ql, bh, bl, sems):
+    copies = fetch([(th_any, th), (tl_any, tl), (green_any, green_ref)], sems)
     first = lax.broadcasted_iota(jnp.int32, (64, 128), 1) % 64 < 32
     for ex in range(4):
         base = ex % 2 * 128 + ex // 2 * 16
@@ -279,7 +278,7 @@
         in_specs=[pl.BlockSpec(memory_space=spaces[k]) for k in kinds],
         out_specs=out_spec if single else tuple(out_spec for _ in outs),
         scratch_shapes=scratch,
-        compiler_params=pltpu.CompilerParams(vmem_limit_bytes=room << 20),
+        compiler_params=pltpu.CompilerParams(vmem_limit_bytes=int(room * 2**20)),
         cost_estimate=pl.CostEstimate(flops=flops, bytes_accessed=bytes_accessed, transcendentals=0),
         name=name,
     )(*args)
@@ -317,23 +316,23 @@
     even = swap_pairs(own, "wide", W, 0)
     back = call(
         convolve, shape(1024, 128),
-        (planes.reshape(1024, 128), yh, yl, green_hat.reshape(2, 512, 512)), "hhhh",
-        scratch=[VMEM((1024, 128), F32)] + [VMEM((2, 256, 512), BF16)] * 2 + [VMEM((2, 512, 512), F32)]
+        (planes.reshape(1024, 128), yh, yl, green_hat.reshape(2, 512, 512)), "vhhh",
+        scratch=[VMEM((2, 256, 512), BF16)] * 2 + [VMEM((2, 512, 512), F32)]
         + [VMEM((2, 256, 256), BF16)] * 2 + [VMEM((2, 256, 512), BF16)] * 2
         + [VMEM((2, 512, 512), BF16)] * 2 + [VMEM((2, 256, 512), BF16)] * 2,
-        copies=4, flops=5 * 10**9, bytes_accessed=9 << 20, name="convolve", room=63,
+        copies=3, flops=5 * 10**9, bytes_accessed=9 << 20, name="convolve", room=52.5,
     )
     field = lax.all_to_all(back.reshape(256, 4, 128), BOTH, split_axis=0, concat_axis=0, tiled=True)
     index = near_source.reshape(CLASSES * 256)
     beside = call(
         near, shape(128, 256), (index, even, own, odd, near_table), "svvvv",
         scratch=[VMEM((2304, 128), F32), VMEM((CLASSES, 256, 128), F32)],
-        flops=10**10, bytes_accessed=40 << 20, name="near", room=16,
+        flops=10**10, bytes_accessed=40 << 20, name="near", room=52.5,
     )
     result = call(
         from_grid, shape(128, 256),
         (block_count, site, field.reshape(1024, 128), projection, expand, izh, izl, beside), "svvvvvvv",
-        flops=2 * 10**9, bytes_accessed=2 << 20, name="from_grid", room=12,
+        flops=2 * 10**9, bytes_accessed=2 << 20, name="from_grid", room=52.5,
     )
     return result.reshape(2, 64, 256)
 

time: 81.5 us -> 86.8 us (1.065)
  starting transfers between devices: 29.9 us -> 34.6 us
  waiting for transfers between devices: 25.7 us -> 27.4 us
  local copies, waits for them, and re-layouts: 3.09 us -> 1.63 us
    all_to_all x1, starting transfers between devices: 5.57 us -> 11.3 us  [per_device(): lax.all_to_all(back.reshape(256, 4, 128), BOTH, split_axis=0, concat_axis...]
    unnamed x20 -> x18, local copies, waits for them, and re-layouts: 3.09 us -> 1.62 us
    all_to_all x1, starting transfers between devices: 14.4 us -> 13.4 us  [per_device(): lax.all_to_all(sent.reshape(256, 4, 128), BOTH, split_axis=0, concat_axis...]
    all_to_all x1, waiting for transfers between devices: 11.3 us -> 12.2 us  [per_device(): lax.all_to_all(back.reshape(256, 4, 128), BOTH, split_axis=0, concat_axis...]
  transfers between devices with their start and end apart: 6 -> 6, of which waited for: 3 -> 3; matrix products, arithmetic and copies ran while one was open for 0% -> 0% of each run, Pallas kernels for 23% -> 22%
where the time goes in v13:
time: 86.8 us; the launch traced here: 86.5 us
  starting transfers between devices  34.6 us (40%)
  waiting for transfers between devices  27.4 us (32%)
  Pallas kernels  22 us (25%)
  local copies, waits for them, and re-layouts  1.63 us (2%)
    pallas_call x7, Pallas kernels, call(): pl.pallas_call(kernel, out_shape=outs, in_specs=[pl.BlockSpec(memory_spac...  22 us
    all_to_all x1, waiting for transfers between devices, per_device(): lax.all_to_all(sent.reshape(256, 4, 128), BOTH, split_axis=0, concat_axis...  14.2 us
    all_to_all x1, starting transfers between devices, per_device(): lax.all_to_all(sent.reshape(256, 4, 128), BOTH, split_axis=0, concat_axis...  13.4 us
    all_to_all x1, waiting for transfers between devices, per_device(): lax.all_to_all(back.reshape(256, 4, 128), BOTH, split_axis=0, concat_axis...  12.2 us
    all_to_all x1, starting transfers between devices, per_device(): lax.all_to_all(back.reshape(256, 4, 128), BOTH, split_axis=0, concat_axis...  11.3 us
    ppermute x4, starting transfers between devices, swap_pairs(): return lax.ppermute(array, axis, pairs + [(j, i) for i, j in pairs])  9.95 us
  transfers between devices with their start and end apart: 6, of which 3 were waited for; matrix products, arithmetic and copies ran while one was open for 0% of the time, Pallas kernels for 22%

profile of v13, /device:TPU:1, one launch (start us, length us, event | category | flops | bytes accessed | tf_op | source)
XLA Modules:
  0.0 86.5 jit_solution(10345080912507323391)
XLA Ops:
  0.7 0.0 copy-start
  0.7 0.9 %copy-done = f32[2,64,256]{2,1,0:T(8,128)S(1)} copy-done((f32[2,64,256]{2,1,0:T(8,128)S(1)}, f32[2,64,256]{2,1,0:T(8,128)}, u32[]{:S(2)}) %copy-start) | copy-done | bytes 131096
  1.6 0.1 turn_early.1
  1.7 4.9 %collective-permute-start = (f32[256,128]{1,0:T(8,128)S(1)}, f32[256,128]{1,0:T(8,128)S(1)}, u32[]{:S(2)}, u32[]{:S(2)}) collective-permute-start(f32[256,128]{1,0:T(8,128)S(1)} %turn_early.1), channel_id=1, source_target_pairs={{1,2},{2,1},{5,6},{6,5},{9,10},{10,9},{13,14},{14,13},{17,18},{18,... | collective-permute-start | bytes 393224 | tf_op jit(solution)/shard_map/ppermute | solution.py:289
  6.6 0.0 copy-start.1
  6.6 4.1 %to_grid.1 = (f32[1024,128]{1,0:T(8,128)}, f32[8,128]{1,0:T(8,128)}) custom-call(s32[1]{0:T(128)S(6)} %copy.16.count_ref, f32[128,256]{1,0:T(8,128)} %bitcast.10, s32[1,256]{1,0:T(1,128)} %bitcast.13, f32[64,64]{1,0:T(8,128)} %proj_ref.1, bf16[2048,128]{1,0:T(8,128)(2,1)} %constant.16.clone.expand_any, bf16[256,256]{1,0:T(8,128)(2,1)} %constant.17.clone.fh_any, ...), custom_call_target="tpu_custom_call" | custom-call | flops 2000000000 | bytes 2097152 | tf_op jit(solution)/shard_map/to_grid/pallas_call | solution.py:275
  10.8 13.4 %all-to-all-start = ((f32[256,4,128]{2,1,0:T(4,128)}), f32[256,4,128]{2,1,0:T(4,128)S(1)}, u32[]{:S(2)}, u32[]{:S(2)}) async-start(f32[256,4,128]{2,1,0:T(4,128)} %bitcast.15), calls=%async_computation | async-start | bytes 1048576 | tf_op jit(solution)/shard_map/all_to_all | solution.py:311
  24.2 0.0 copy-start.2
  24.2 0.7 copy-done.2
  24.8 0.1 turn.1.own_ref
  25.0 2.2 %collective-permute-start.1 = (f32[256,128]{1,0:T(8,128)S(1)}, f32[256,128]{1,0:T(8,128)S(1)}, u32[]{:S(2)}, u32[]{:S(2)}) collective-permute-start(f32[256,128]{1,0:T(8,128)S(1)} %turn.1.own_ref), channel_id=1, source_target_pairs={{0,1},{2,3},{1,0},{3,2},{4,5},{6,7},{5,4},{7,6},{8,9},{10,11},{9,8... | collective-permute-start | bytes 393224 | tf_op jit(solution)/shard_map/ppermute | solution.py:289
  27.2 1.0 %collective-permute-done.1.even_ref = f32[256,128]{1,0:T(8,128)S(1)} collective-permute-done((f32[256,128]{1,0:T(8,128)S(1)}, f32[256,128]{1,0:T(8,128)S(1)}, u32[]{:S(2)}, u32[]{:S(2)}) %collective-permute-start.1) | collective-permute-done | bytes 131104 | tf_op jit(solution)/shard_map/ppermute | solution.py:289
  28.2 0.7 collective-permute-start.3
  28.9 2.1 %collective-permute-start.2 = (f32[768,128]{1,0:T(8,128)S(1)}, f32[768,128]{1,0:T(8,128)S(1)}, u32[]{:S(2)}, u32[]{:S(2)}) collective-permute-start(f32[768,128]{1,0:T(8,128)S(1)} %join.1.own_ref), channel_id=1, source_target_pairs={{0,4},{8,12},{16,20},{24,28},{32,36},{40,44},{48,52},{56,60},{64,6... | collective-permute-start | bytes 1179656 | tf_op jit(solution)/shard_map/ppermute | solution.py:289
  31.0 14.2 %all-to-all-done = f32[256,4,128]{2,1,0:T(4,128)S(1)} async-done(((f32[256,4,128]{2,1,0:T(4,128)}), f32[256,4,128]{2,1,0:T(4,128)S(1)}, u32[]{:S(2)}, u32[]{:S(2)}) %all-to-all-start) | async-done | bytes 524320 | tf_op jit(solution)/shard_map/all_to_all | solution.py:311
  45.2 5.9 %convolve.1 = f32[1024,128]{1,0:T(8,128)} custom-call(f32[1024,128]{1,0:T(8,128)S(1)} %bitcast.8, bf16[2,256,512]{2,1,0:T(8,128)(2,1)} %constant.19.clone.th_any, bf16[2,256,512]{2,1,0:T(8,128)(2,1)} %constant.20.clone.tl_any, f32[2,512,512]{2,1,0:T(8,128)} %bitcast.16), custom_call_target="tpu_custom_call" | custom-call | flops 5000000000 | bytes 9437184 | tf_op jit(solution)/shard_map/convolve/pallas_call | solution.py:275
  51.1 11.3 %all-to-all-start.1 = ((f32[256,4,128]{2,1,0:T(4,128)}), f32[256,4,128]{2,1,0:T(4,128)S(1)}, u32[]{:S(2)}, u32[]{:S(2)}) async-start(f32[256,4,128]{2,1,0:T(4,128)} %bitcast.5), calls=%async_computation.1 | async-start | bytes 1048576 | tf_op jit(solution)/shard_map/all_to_all | solution.py:325
  62.5 0.0 copy-start.4
  62.5 0.0 copy-start.5
  62.5 0.0 copy-start.6
  62.5 0.0 copy-start.7
  62.5 8.9 %near.1.near_ref = f32[128,256]{1,0:T(8,128)S(1)} custom-call(s32[6912]{0:T(1024)S(1)} %reshape.34.index_ref, f32[768,128]{1,0:T(8,128)S(1)} %collective-permute-done.2.even_ref, f32[768,128]{1,0:T(8,128)S(1)} %join.1.own_ref, f32[768,128]{1,0:T(8,128)S(1)} %collective-permute-done.3.odd_ref, f32[27,2,64,64]{3,2,1,0:T(8,128)} %table_ref.1), custom_call_target="tpu_custom_call" | custom-call | flops 10000000000 | bytes 41943040 | tf_op jit(solution)/shard_map/near/pallas_call | solution.py:275
  71.5 12.2 %all-to-all-done.1 = f32[256,4,128]{2,1,0:T(4,128)S(1)} async-done(((f32[256,4,128]{2,1,0:T(4,128)}), f32[256,4,128]{2,1,0:T(4,128)S(1)}, u32[]{:S(2)}, u32[]{:S(2)}) %all-to-all-start.1) | async-done | bytes 524320 | tf_op jit(solution)/shard_map/all_to_all | solution.py:325
  83.7 2.8 %from_grid.1 = f32[128,256]{1,0:T(8,128)} custom-call(s32[1]{0:T(128)S(6)} %copy.16.count_ref, s32[1,256]{1,0:T(1,128)S(1)} %bitcast.14, f32[1024,128]{1,0:T(8,128)S(1)} %bitcast.9, f32[64,64]{1,0:T(8,128)S(1)} %copy-done.3, bf16[128,2048]{1,0:T(8,128)(2,1)S(1)} %copy-done.5, bf16[128,512]{1,0:T(8,128)(2,1)S(1)} %copy-done.7, ...), custom_call_target="tpu_custom_call" | custom-call | flops 2000000000 | bytes 2097152 | tf_op jit(solution)/shard_map/from_grid/pallas_call | solution.py:275
  (14 shorter events, 0.1 us)
Async XLA Ops:
  0.7 0.9 %copy-start = (f32[2,64,256]{2,1,0:T(8,128)S(1)}, f32[2,64,256]{2,1,0:T(8,128)}, u32[]{:S(2)}) copy-start(f32[2,64,256]{2,1,0:T(8,128)} %param.15) | copy-start | bytes 393220
  1.7 9.1 %collective-permute-start = (f32[256,128]{1,0:T(8,128)S(1)}, f32[256,128]{1,0:T(8,128)S(1)}, u32[]{:S(2)}, u32[]{:S(2)}) collective-permute-start(f32[256,128]{1,0:T(8,128)S(1)} %turn_early.1), channel_id=1, source_target_pairs={{1,2},{2,1},{5,6},{6,5},{9,10},{10,9},{13,14},{14,13},{17,18},{18,... | collective-permute-start | bytes 393224 | tf_op jit(solution)/shard_map/ppermute | solution.py:289
  6.6 17.5 %copy-start.1 = (f32[2,64,256]{2,1,0:T(8,128)S(1)}, f32[2,64,256]{2,1,0:T(8,128)}, u32[]{:S(2)}) copy-start(f32[2,64,256]{2,1,0:T(8,128)} %param.15) | copy-start | bytes 393220
  10.8 34.4 %all-to-all-start = ((f32[256,4,128]{2,1,0:T(4,128)}), f32[256,4,128]{2,1,0:T(4,128)S(1)}, u32[]{:S(2)}, u32[]{:S(2)}) async-start(f32[256,4,128]{2,1,0:T(4,128)} %bitcast.15), calls=%async_computation | async-start | bytes 1048576 | tf_op jit(solution)/shard_map/all_to_all | solution.py:311
  24.2 0.7 copy-start.2
  25.0 3.2 %collective-permute-start.1 = (f32[256,128]{1,0:T(8,128)S(1)}, f32[256,128]{1,0:T(8,128)S(1)}, u32[]{:S(2)}, u32[]{:S(2)}) collective-permute-start(f32[256,128]{1,0:T(8,128)S(1)} %turn.1.own_ref), channel_id=1, source_target_pairs={{0,1},{2,3},{1,0},{3,2},{4,5},{6,7},{5,4},{7,6},{8,9},{10,11},{9,8... | collective-permute-start | bytes 393224 | tf_op jit(solution)/shard_map/ppermute | solution.py:289
  28.2 34.3 %collective-permute-start.3 = (f32[768,128]{1,0:T(8,128)S(1)}, f32[768,128]{1,0:T(8,128)S(1)}, u32[]{:S(2)}, u32[]{:S(2)}) collective-permute-start(f32[768,128]{1,0:T(8,128)S(1)} %join.1.own_ref), channel_id=1, source_target_pairs={{4,8},{12,16},{20,24},{28,32},{36,40},{44,48},{52,56},{60,64},{68,... | collective-permute-start | bytes 1179656 | tf_op jit(solution)/shard_map/ppermute | solution.py:289
  28.9 33.6 %collective-permute-start.2 = (f32[768,128]{1,0:T(8,128)S(1)}, f32[768,128]{1,0:T(8,128)S(1)}, u32[]{:S(2)}, u32[]{:S(2)}) collective-permute-start(f32[768,128]{1,0:T(8,128)S(1)} %join.1.own_ref), channel_id=1, source_target_pairs={{0,4},{8,12},{16,20},{24,28},{32,36},{40,44},{48,52},{56,60},{64,6... | collective-permute-start | bytes 1179656 | tf_op jit(solution)/shard_map/ppermute | solution.py:289
  45.2 17.2 %copy-start.8 = (s32[27,256]{1,0:T(8,128)S(1)}, s32[27,256]{1,0:T(8,128)}, u32[]{:S(2)}) copy-start(s32[27,256]{1,0:T(8,128)} %param.21) | copy-start | bytes 82948
  51.1 32.5 %all-to-all-start.1 = ((f32[256,4,128]{2,1,0:T(4,128)}), f32[256,4,128]{2,1,0:T(4,128)S(1)}, u32[]{:S(2)}, u32[]{:S(2)}) async-start(f32[256,4,128]{2,1,0:T(4,128)} %bitcast.5), calls=%async_computation.1 | async-start | bytes 1048576 | tf_op jit(solution)/shard_map/all_to_all | solution.py:325
  62.4 21.2 %copy-start.3 = (f32[64,64]{1,0:T(8,128)S(1)}, f32[64,64]{1,0:T(8,128)}, u32[]{:S(2)}) copy-start(f32[64,64]{1,0:T(8,128)} %proj_ref.1) | copy-start | bytes 49156
  62.5 21.2 %copy-start.4 = (s32[256]{0:T(256)S(1)}, s32[256]{0:T(256)}, u32[]{:S(2)}) copy-start(s32[256]{0:T(256)} %param.19) | copy-start | bytes 3076
  62.5 21.2 %copy-start.5 = (bf16[128,2048]{1,0:T(8,128)(2,1)S(1)}, bf16[128,2048]{1,0:T(8,128)(2,1)}, u32[]{:S(2)}) copy-start(bf16[128,2048]{1,0:T(8,128)(2,1)} %constant.21.clone.expand_ref) | copy-start | bytes 1572868
  62.5 21.2 %copy-start.6 = (bf16[128,512]{1,0:T(8,128)(2,1)S(1)}, bf16[128,512]{1,0:T(8,128)(2,1)}, u32[]{:S(2)}) copy-start(bf16[128,512]{1,0:T(8,128)(2,1)} %constant.23.clone.fl_ref) | copy-start | bytes 393220
  62.5 21.2 %copy-start.7 = (bf16[128,512]{1,0:T(8,128)(2,1)S(1)}, bf16[128,512]{1,0:T(8,128)(2,1)}, u32[]{:S(2)}) copy-start(bf16[128,512]{1,0:T(8,128)(2,1)} %constant.22.clone.fh_ref) | copy-start | bytes 393220
